TPU v7x, 32 devices: a whole 2x2x4 slice. The times are simulated.
32 devices in a mesh: expert: 8 (over z, core), tensor: 4 (over y, x).
Axes of the slice: x: 2, y: 2, z: 4, core: 2. Of those that a mesh axis runs over, the one named last changes fastest.
Arguments:
- hidden_in: bfloat16 [1024, 4096], P('expert', 'tensor'), may hold values from -92 to 92
- norm_gain: float32 [4096], P('tensor'), may hold values from 0.5 to 1.5
- expert_ids: int32 [1024, 8], P('expert'), may hold values from 0 to 15, all different within a row; in each aligned block of 128 rows (0 to 127, 128 to 255, ...) at most 96 rows name the same one
- route_weights: float32 [1024, 8], P('expert'), may hold values from 0.05 to 0.5
- w_gate: bfloat16 [16, 1536, 4096], P('expert', 'tensor'), may hold values from -0.09375 to 0.09375
- w_up: bfloat16 [16, 1536, 4096], P('expert', 'tensor'), may hold values from -0.09375 to 0.09375
- w_down: bfloat16 [16, 1536, 4096], P('expert', 'tensor'), may hold values from -0.15625 to 0.15625
Outputs:
- moe_out: bfloat16 [1024, 4096], P('expert', 'tensor')
Inputs may be any that keep to these rules, and one draw needn't show every extreme that they name: `expert_ids`: in each aligned block of 128 rows (the rows of one index of the expert axis) no expert is named by more than 96 rows, a bound that some block reaches.
All inputs are finite; a program needn't handle non-finite values.
Results may differ from a plain program's by a relative error of at most 0.019.
Values may be sent and summed in bfloat16 or wider, within the bound.
No kernel may reach another device: no remote copies, remote signals or barrier semaphores. Data moves between devices by JAX's collectives and lax.ppermute only.
A program may use at most 128 MiB of HBM per device.

v0:
```python
import jax
import jax.numpy as jnp
from jax import lax
from jax.sharding import PartitionSpec as P

D = 4096


epsilon = 1e-06


def local_partials(inner, w_down):
    partial_list = []
    for expert_slot in range(inner.shape[0]):
        partial_one = jnp.dot(
            inner[expert_slot], w_down[expert_slot], preferred_element_type=jnp.float32
        )
        partial_list.append(partial_one.astype(jnp.bfloat16))
    return jnp.stack(partial_list, axis=0)


def body(hidden_in, norm_gain, expert_ids, route_weights, w_gate, w_up, w_down):
    tokens_here = hidden_in.shape[0]
    width_local = hidden_in.shape[1]
    choices_count = expert_ids.shape[1]
    exp_local = w_gate.shape[0]
    groups = lax.axis_size("expert")
    experts_all = exp_local * groups
    capacity = min(tokens_here, 3 * tokens_here * choices_count // (2 * experts_all))
    widened = hidden_in.astype(jnp.float32)
    squares = lax.psum(jnp.sum(widened * widened, axis=1), "tensor")
    normed = (widened * lax.rsqrt(squares / D + epsilon)[:, None] * norm_gain[None, :]).astype(
        jnp.bfloat16
    )
    picked_mask = (
        expert_ids[:, :, None] == jnp.arange(experts_all, dtype=jnp.int32)[None, None, :]
    ).astype(jnp.int32)
    chosen = jnp.sum(picked_mask, axis=1)
    before = jnp.cumsum(chosen, axis=0) - chosen
    position = jnp.sum(picked_mask * before[:, None, :], axis=2)
    flat_index = expert_ids * capacity + position
    slot_ids = jnp.arange(experts_all * capacity, dtype=jnp.int32)
    placing = jnp.sum(
        (flat_index[None, :, :] == slot_ids[:, None, None]).astype(jnp.float32), axis=2
    ).astype(jnp.bfloat16)
    outgoing = jnp.dot(placing, normed, preferred_element_type=jnp.float32).astype(jnp.bfloat16)
    outgoing = outgoing.reshape(experts_all, capacity, width_local)
    arrived = lax.all_to_all(outgoing, "expert", split_axis=0, concat_axis=1, tiled=True)
    piece = lax.all_gather(arrived, "tensor", axis=2, tiled=True)
    gate_add = jnp.einsum("erd,efd->erf", piece, w_gate, preferred_element_type=jnp.float32)
    up_add = jnp.einsum("erd,efd->erf", piece, w_up, preferred_element_type=jnp.float32)
    inner = (jax.nn.silu(gate_add) * up_add).astype(jnp.bfloat16)
    partials = local_partials(inner, w_down)
    returned = lax.all_to_all(partials, "expert", split_axis=1, concat_axis=0, tiled=True)
    lookup = returned.reshape(experts_all * capacity, returned.shape[2])
    gathered = lookup[flat_index].astype(jnp.float32)
    weighted = jnp.sum(gathered * route_weights[:, :, None], axis=1)
    mixed = lax.psum_scatter(
        weighted.astype(jnp.bfloat16), "tensor", scatter_dimension=1, tiled=True
    )
    return mixed


def solution(mesh):
    placed = (
        P("expert", "tensor"),
        P("tensor"),
        P("expert", None),
        P("expert", None),
        P("expert", "tensor", None),
        P("expert", "tensor", None),
        P("expert", "tensor", None),
    )
    return jax.shard_map(
        body, mesh=mesh, in_specs=placed, out_specs=P("expert", "tensor"), check_vma=False
    )
```

profile of v0, /device:TPU:0, one launch (start us, length us, event | category | flops | bytes accessed | tf_op | source)
XLA Modules:
  0.0 656.4 jit_solution(12611872128439492468)
XLA Ops:
  6.5 0.0 all-gather.2.cloned.1.call-start
  6.5 0.7 convert_reduce_fusion.1
  7.2 0.1 copy.26
  7.3 0.2 reduce_window_sum.11
  7.5 0.1 copy.28
  7.6 0.7 select_reduce_fusion
  8.3 0.7 compare_select_fusion
  9.0 8.0 %convert_reduce_fusion = bf16[1536,128]{1,0:T(8,128)(2,1)S(1)} fusion(s32[128,8]{0,1:T(8,128)S(1)} %get-tuple-element.6), kind=kLoop, calls=%fused_computation.6 | loop fusion | flops 4521984 | bytes 397312 | tf_op jit(solution)/shard_map/reduce_sum | solution.py:43
  17.0 1.1 fusion.7
  18.1 11.4 %psum.7 = f32[128]{0:T(128)S(1)} all-reduce(f32[128]{0:T(128)S(1)} %fusion.7), channel_id=1, replica_groups=mesh['expert'=8,'tensor'=4] {'tensor'}, use_global_device_ids=true, to_apply=%region_5.6 | all-reduce | flops 128 | bytes 1024 | tf_op jit(solution)/shard_map/psum | solution.py:31
  29.5 2.0 convolution_convert_fusion.2
  31.5 76.2 %all_to_all.33 = bf16[16,96,1024]{2,1,0:T(8,128)(2,1)S(1)} all-to-all(bf16[16,96,1024]{2,1,0:T(8,128)(2,1)S(1)} %bitcast.35), channel_id=1, replica_groups=mesh['expert'=8,'tensor'=4] {'expert'}, dimensions={0} | all-to-all | bytes 6291456 | tf_op jit(solution)/shard_map/all_to_all | solution.py:48
  107.7 2.1 copy.29
  109.8 0.0 all-gather.2.cloned.1.call-update
  109.8 119.7 %all-gather.2.cloned.1.call-done = bf16[2,768,4096]{2,1,0:T(8,128)(2,1)} async-done(((bf16[2,768,1024]{2,1,0:T(8,128)(2,1)}), bf16[2,768,4096]{2,1,0:T(8,128)(2,1)}) %all-gather.2.cloned.1.call-update) | async-done | bytes 12582928 | tf_op jit(solution)/shard_map/all_gather | solution.py:49
  229.5 11.8 %fusion.14 = f32[2,768,384]{2,1,0:T(8,128)S(1)} fusion(bf16[2,768,4096]{2,1,0:T(8,128)(2,1)} %all-gather.2.cloned.1.call-done, bf16[2,384,4096]{2,1,0:T(8,128)(2,1)} %param.11), kind=kOutput, calls=%fused_computation.33 | convolution fusion | flops 4831838208 | bytes 21233664 | tf_op jit(solution)/shard_map/erd,efd->erf/dot_general | solution.py:50
  241.4 8.9 %multiply_convert_fusion = bf16[2,768,384]{2,1,0:T(8,128)(2,1)S(1)} fusion(f32[2,768,384]{2,1,0:T(8,128)S(1)} %fusion.14, bf16[2,768,4096]{2,1,0:T(8,128)(2,1)S(1)} %copy-done.1, bf16[2,384,4096]{2,1,0:T(8,128)(2,1)} %param.12), kind=kOutput, calls=%fused_computation.15 | convolution fusion | flops 4835377152 | bytes 22413312 | tf_op jit(solution)/shard_map/erd,efd->erf/dot_general | solution.py:51
  250.2 5.6 fusion.1
  255.9 5.6 fusion.2
  261.5 1.2 pad_maximum_fusion
  262.7 33.0 %copy.30 = bf16[2,768,4096]{2,0,1:T(2,128)(2,1)} copy(bf16[2,768,4096]{2,1,0:T(8,128)(2,1)S(1)} %pad_maximum_fusion) | data formatting | bytes 25165824 | tf_op jit(solution)/shard_map/stack | solution.py:19
  295.8 5.5 all-to-all-start.1
  301.2 0.3 reduce-scatter.2.cloned.1.call-start
  301.5 0.1 copy.32
  301.6 0.1 reshape.25
  301.7 0.1 copy.33
  301.8 273.2 %all-to-all-done.1 = bf16[2,768,4096]{2,0,1:T(2,128)(2,1)} async-done(((bf16[2,768,4096]{2,0,1:T(2,128)(2,1)}), bf16[2,768,4096]{2,0,1:T(2,128)(2,1)}, u32[]{:S(2)}, u32[]{:S(2)}) %all-to-all-start.1) | async-done | bytes 12582944 | tf_op jit(solution)/shard_map/all_to_all | solution.py:54
  575.0 14.5 %copy.31 = bf16[2,8,96,4096]{3,2,0,1:T(8,128)(2,1)} copy(bf16[2,8,96,4096]{3,0,2,1:T(2,128)(2,1)} %bitcast.10) | data formatting | bytes 25165824 | tf_op jit(solution)/shard_map/all_to_all | solution.py:54
  589.5 21.3 %gather_fusion = bf16[1024,4096]{1,0:T(8,128)(2,1)} fusion(bf16[1536,4096]{1,0:T(8,128)(2,1)} %bitcast.33, s32[1024]{0:T(1024)S(1)} %broadcast_clamp_fusion), kind=kCustom, calls=%fused_computation | custom fusion | bytes 16781312 | tf_op jit(solution)/shard_map/gather | solution.py:56
  610.7 13.0 %fusion = bf16[128,4096]{1,0:T(8,128)(2,1)} fusion(bf16[1024,4096]{1,0:T(8,128)(2,1)} %gather_fusion, f32[128,8]{1,0:T(8,128)S(1)} %copy.33), kind=kLoop, calls=%fused_computation.2 | loop fusion | flops 12058624 | bytes 9441280 | tf_op jit(solution)/shard_map/reduce_sum | solution.py:57
  623.7 0.0 reduce-scatter.2.cloned.1.call-update
  623.7 25.8 %reduce-scatter.2.cloned.1.call-done = bf16[128,1024]{1,0:T(8,128)(2,1)} async-done(((bf16[128,4096]{1,0:T(8,128)(2,1)}), bf16[128,1024]{1,0:T(8,128)(2,1)}) %reduce-scatter.2.cloned.1.call-update) | async-done | bytes 262160 | tf_op jit(solution)/shard_map/reduce_scatter | solution.py:58
  (7 shorter events, 0.0 us)
Async XLA Ops:
  6.5 223.0 %all-gather.2.cloned.1.call-start = ((), (), s32[]{:S(2)}) async-start(), calls=%async_computation.3 | async-start | bytes 15728640 | tf_op jit(solution)/shard_map/all_gather | solution.py:49
  229.5 11.8 %copy-start.1 = (bf16[2,768,4096]{2,1,0:T(8,128)(2,1)S(1)}, bf16[2,768,4096]{2,1,0:T(8,128)(2,1)}, u32[]{:S(2)}) copy-start(bf16[2,768,4096]{2,1,0:T(8,128)(2,1)} %all-gather.2.cloned.1.call-done) | copy-start | bytes 37748740
  295.8 5.9 copy-start
  295.8 279.3 %all-to-all-start.1 = ((bf16[2,768,4096]{2,0,1:T(2,128)(2,1)}), bf16[2,768,4096]{2,0,1:T(2,128)(2,1)}, u32[]{:S(2)}, u32[]{:S(2)}) async-start(bf16[2,768,4096]{2,0,1:T(2,128)(2,1)} %copy.30), calls=%async_computation.1 | async-start | bytes 25165824 | tf_op jit(solution)/shard_map/all_to_all | solution.py:54
  301.2 348.3 %reduce-scatter.2.cloned.1.call-start = ((), (), s32[]{:S(2)}) async-start(), calls=%async_computation.4 | async-start | bytes 1310720 | tf_op jit(solution)/shard_map/reduce_scatter | solution.py:58
Sparse Core Ops, SparseCore 0:
  110.0 119.5 all-gather.1
  623.9 25.6 reduce-scatter.1
where the time goes:
time: 657 us; the launch traced here: 656 us
  waiting for transfers between devices  419 us (64%)
  blocking collectives  87.6 us (13%)
  local copies, waits for them, and re-layouts  71.3 us (11%)
  matrix products  33.9 us (5%)
  other arithmetic  25.7 us (4%)
  between operations  13.5 us (2%)
    all_to_all x1, waiting for transfers between devices, body(): lax.all_to_all(partials, 'expert', split_axis=1, concat_axis=0, tiled=True)  273 us
    all_gather x1, waiting for transfers between devices, body(): piece = lax.all_gather(arrived, 'tensor', axis=2, tiled=True)  120 us
    all_to_all x1, blocking collectives, body(): lax.all_to_all(outgoing, 'expert', split_axis=0, concat_axis=1, tiled=True)  76.2 us
    another operation x1, local copies, waits for them, and re-layouts, local_partials(): return jnp.stack(partial_list, axis=0)  33 us
    reduce_scatter x1, waiting for transfers between devices, body(): lax.psum_scatter(weighted.astype(jnp.bfloat16), 'tensor', scatter_dimensi...  25.8 us
    gather x1, local copies, waits for them, and re-layouts, body(): gathered = lookup[flat_index].astype(jnp.float32)  21.3 us
    all_to_all x1, local copies, waits for them, and re-layouts, body(): lax.all_to_all(partials, 'expert', split_axis=1, concat_axis=0, tiled=True)  14.5 us
  transfers between devices with their start and end apart: 3, of which 3 were waited for; matrix products, arithmetic and copies ran while one was open for 0% of the time, Pallas kernels for 0%

commit v1 on v0

v1 whole, which is shorter than its diff:
```python
import functools

import jax
import jax.numpy as jnp
from jax import lax
from jax.experimental import pallas as pl
from jax.experimental.pallas import tpu as pltpu
from jax.sharding import PartitionSpec as P

AXES = ("expert", "tensor")
CORES = 2
EXTRA = 8
epsilon = 1e-06
NT = (((1,), (1,)), ((), ()))


def split3(v):
    hi = v.astype(jnp.bfloat16)
    rest = v - hi.astype(jnp.float32)
    mid = rest.astype(jnp.bfloat16)
    lo = (rest - mid.astype(jnp.float32)).astype(jnp.bfloat16)
    return hi, mid, lo


def masks_of(n_tensor):
    bits = n_tensor.bit_length() - 1
    first = [1 << b for b in range(bits)]
    half = bits // 2
    return first, first[half:] + first[:half]


def spread(masks, j):
    out = 0
    for s, m in enumerate(masks):
        if (j >> s) & 1:
            out ^= m
    return out


def expert_kernel(pieces, offsets, block, order_ref, *refs):
    n_in = 2 * 2
    (a0, a1, b0, b1, scal, wg, wu, wd) = refs[: n_in + 4]
    (mine_keep, mine_send, sib_keep, sib_send) = refs[n_in + 4 : n_in + 8]
    xs, hs = refs[n_in + 8 :]
    half = pieces // 2
    rows = offsets * block
    width = xs.shape[2]
    for side, (lo, hi) in enumerate(((a0, a1), (b0, b1))):
        for j in range(pieces):
            src = lo if j < half else hi
            q = order_ref[side, j]
            for o in range(offsets):
                at = side * rows + o * block
                xs[q, at : at + block, :] = src[j % half, o, 0:block, :]
    n_exp, hidden = wg.shape[0], wg.shape[1]
    scale = scal[:, 0:1]
    for e in range(n_exp):
        gate = jnp.zeros((2 * rows, hidden), jnp.float32)
        up = jnp.zeros((2 * rows, hidden), jnp.float32)
        for q in range(pieces):
            cols = slice(q * width, (q + 1) * width)
            gate += lax.dot_general(xs[q], wg[e, :, cols], NT, preferred_element_type=jnp.float32)
            up += lax.dot_general(xs[q], wu[e, :, cols], NT, preferred_element_type=jnp.float32)
        gate = gate * scale
        inner = gate / (1.0 + jnp.exp(-gate)) * (up * scale) * scal[:, 1 + e : 2 + e]
        hs[:, e * hidden : (e + 1) * hidden] = inner.astype(jnp.bfloat16)
    for side, (keep, send) in enumerate(((mine_keep, mine_send), (sib_keep, sib_send))):
        inner = hs[side * rows : (side + 1) * rows, :]
        for j in range(pieces):
            q = order_ref[side, j]
            cols = pl.ds(pl.multiple_of(q * width, width), width)
            out = jnp.dot(inner, wd[:, cols], preferred_element_type=jnp.float32)
            dst = keep if j < half else send
            for o in range(offsets):
                dst[j % half, o] = out[o * block : (o + 1) * block].astype(jnp.bfloat16)


def run_experts(order, a0, a1, b0, b1, scal, wg, wu, wd, block):
    half, offsets, _, width = a0.shape
    pieces = 2 * half
    rows = offsets * block
    hidden = wg.shape[0] * wg.shape[1]
    part = jax.ShapeDtypeStruct((half, offsets, block, width), jnp.bfloat16)
    vmem = pl.BlockSpec(memory_space=pltpu.VMEM)
    macs = 2 * rows * 3 * hidden * pieces * width
    return pl.pallas_call(
        functools.partial(expert_kernel, pieces, offsets, block),
        out_shape=[part] * 4,
        in_specs=[pl.BlockSpec(memory_space=pltpu.SMEM)] + [vmem] * 8,
        out_specs=[vmem] * 4,
        scratch_shapes=[
            pltpu.VMEM((pieces, 2 * rows, width), jnp.bfloat16),
            pltpu.VMEM((2 * rows, hidden), jnp.bfloat16),
        ],
        compiler_params=pltpu.CompilerParams(vmem_limit_bytes=56 * 1024 * 1024),
        cost_estimate=pl.CostEstimate(
            flops=2 * macs, bytes_accessed=3 * hidden * pieces * width * 2, transcendentals=2 * rows * hidden
        ),
    )(order, a0, a1, b0, b1, scal, wg, wu, wd)


def body(hidden_in, norm_gain, expert_ids, route_weights, w_gate, w_up, w_down):
    block, width = hidden_in.shape
    exp_local = w_gate.shape[0]
    groups, n_tensor = lax.axis_size("expert"), lax.axis_size("tensor")
    n_z = groups // CORES
    experts_all = exp_local * groups
    group_here, slice_here = lax.axis_index("expert"), lax.axis_index("tensor")
    core = group_here % CORES
    masks = masks_of(n_tensor)
    stages = len(masks[0])

    def send(value, target):
        pairs = []
        for z in range(n_z):
            for c in range(CORES):
                for t in range(n_tensor):
                    z2, c2, t2 = target(z, c, t)
                    pairs.append(((z * CORES + c) * n_tensor + t, (z2 * CORES + c2) * n_tensor + t2))
        return lax.ppermute(value, AXES, pairs)

    def stage_swap(value, s):
        return send(value, lambda z, c, t: (z, c, t ^ masks[c][s]))

    def core_swap(value):
        return send(value, lambda z, c, t: (z, 1 - c, t))

    widened = hidden_in.astype(jnp.float32)
    scaled = (widened * norm_gain[None, :]).astype(jnp.bfloat16)
    squares = jnp.sum(widened * widened, axis=1)
    dense = jnp.sum(
        jnp.where(
            expert_ids.T[None, :, :] == jnp.arange(experts_all, dtype=jnp.int32)[:, None, None],
            route_weights.T[None, :, :],
            0.0,
        ),
        axis=1,
    )
    table = jnp.concatenate([squares[None, :], dense], axis=0)
    extra = jnp.stack(split3(table), axis=1).reshape(-1)
    n_extra = -(-extra.shape[0] // (EXTRA * width)) * EXTRA
    extra = jnp.pad(extra, (0, n_extra * width - extra.shape[0])).reshape(n_extra, width)
    payload = jnp.concatenate([scaled, extra], axis=0)

    chunk = [[spread(masks[c], j) for j in range(n_tensor)] for c in range(CORES)]
    order = slice_here ^ jnp.array([chunk, chunk[::-1]], jnp.int32)[core]

    near = [0]
    for k in range(1, n_z // 2 + 1):
        near += [k] if 2 * k == n_z else [k, n_z - k]
    plans = [[k] for k in near]

    arrived = [payload if k == 0 else send(payload, lambda z, c, t, k=k: ((z - k) % n_z, c, t)) for k in near]
    arrived = dict(zip(near, arrived))
    wd = w_down.reshape(-1, w_down.shape[2])
    total = None
    back = {}
    for plan in plans:
        blk = jnp.stack([arrived[k] for k in plan], axis=0)[None]
        for s in range(stages - 1):
            blk = jnp.concatenate([blk, stage_swap(blk, s)], axis=0)
        far = stage_swap(blk, stages - 1)
        blk_sib = core_swap(blk)
        far_sib = core_swap(far)

        def tables(lo, hi):
            both = jnp.concatenate([lo[:, :, block:], hi[:, :, block:]], axis=0).astype(jnp.float32)
            flat = both.reshape(n_tensor, len(plan), -1)[:, :, : 3 * (1 + experts_all) * block]
            flat = flat.reshape(n_tensor, len(plan), 1 + experts_all, 3, block)
            flat = flat[:, :, :, 0] + flat[:, :, :, 1] + flat[:, :, :, 2]
            total_squares = jnp.sum(flat[:, :, 0], axis=0)
            scale = lax.rsqrt(total_squares / (n_tensor * width) + epsilon)
            weights = lax.dynamic_slice_in_dim(flat[0], 1 + group_here * exp_local, exp_local, axis=1)
            return jnp.concatenate([scale[:, None], weights], axis=1).transpose(0, 2, 1).reshape(-1, 1 + exp_local)

        scal = jnp.concatenate([tables(blk, far), tables(blk_sib, far_sib)], axis=0)
        mine_keep, mine_send, sib_keep, sib_send = run_experts(
            order, blk, far, blk_sib, far_sib, scal, w_gate, w_up, wd, block
        )
        f32 = jnp.float32
        from_sib = core_swap(sib_send)
        out = (mine_send.astype(f32) + from_sib.astype(f32)).astype(jnp.bfloat16)
        keep = mine_keep.astype(f32) + core_swap(sib_keep).astype(f32)
        for s in range(stages - 1, -1, -1):
            got = stage_swap(out, s)
            keep = keep + got.astype(f32)
            if s:
                half = keep.shape[0] // 2
                out = keep[half:].astype(jnp.bfloat16)
                keep = keep[:half]
        done = keep[0]
        for i, k in enumerate(plan):
            if k == 0:
                back[k] = done[i]
            else:
                back[k] = send(
                    done[i].astype(jnp.bfloat16), lambda z, c, t, k=k: ((z + k) % n_z, c, t)
                ).astype(f32)
    total = back[near[0]]
    for k in near[1:]:
        total = total + back[k]
    return total.astype(jnp.bfloat16)


def solution(mesh):
    placed = (
        P("expert", "tensor"),
        P("tensor"),
        P("expert", None),
        P("expert", None),
        P("expert", "tensor", None),
        P("expert", "tensor", None),
        P("expert", "tensor", None),
    )
    return jax.shard_map(
        body, mesh=mesh, in_specs=placed, out_specs=P("expert", "tensor"), check_vma=False
    )
```

time: 657 us -> 193 us (0.29)
  waiting for transfers between devices: 419 us -> 63.1 us
  blocking collectives: 87.6 us -> 0 us
  Pallas kernels: 0 us -> 57.3 us
  local copies, waits for them, and re-layouts: 71.3 us -> 15.3 us
  starting transfers between devices: 5.74 us -> 40 us
  matrix products: 33.9 us -> 0 us
  between operations: 13.5 us -> 1.01 us
  other arithmetic: 25.7 us -> 15.1 us
    all_to_all x1 -> x0, waiting for transfers between devices: 273 us -> none  [body(): lax.all_to_all(partials, 'expert', split_axis=1, concat_axis=0, tiled=True)]
    all_gather x1 -> x0, waiting for transfers between devices: 120 us -> none  [body(): piece = lax.all_gather(arrived, 'tensor', axis=2, tiled=True)]
    all_to_all x1 -> x0, blocking collectives: 76.2 us -> none  [body(): lax.all_to_all(outgoing, 'expert', split_axis=0, concat_axis=1, tiled=True)]
    ppermute x0 -> x38, waiting for transfers between devices: none -> 63.1 us  [send(): return lax.ppermute(value, AXES, pairs)]
    pallas_call x0 -> x4, Pallas kernels: none -> 57.3 us  [run_experts(): pl.pallas_call(functools.partial(expert_kernel, pieces, offsets, block),...]
    ppermute x0 -> x38, starting transfers between devices: none -> 40 us  [send(): return lax.ppermute(value, AXES, pairs)]
    dot_general x5 -> x0, matrix products: 33.9 us -> none  [the longest x1 11.8 us: body(): jnp.einsum('erd,efd->erf', piece, w_gate, preferred_element_type=jnp.floa...]
    another operation x1, local copies, waits for them, and re-layouts: 33 us -> 0.01 us  [body(): extra = jnp.stack(split3(table), axis=1).reshape(-1)]
  transfers between devices with their start and end apart: 3 -> 38, of which waited for: 3 -> 12; matrix products, arithmetic and copies ran while one was open for 0% -> 14% of each run, Pallas kernels for 0% -> 30%
where the time goes in v1:
time: 193 us; the launch traced here: 192 us
  waiting for transfers between devices  63.1 us (33%)
  Pallas kernels  57.3 us (30%)
  starting transfers between devices  40 us (21%)
  local copies, waits for them, and re-layouts  15.3 us (8%)
  other arithmetic  15.1 us (8%)
    ppermute x38, waiting for transfers between devices, send(): return lax.ppermute(value, AXES, pairs)  63.1 us
    pallas_call x4, Pallas kernels, run_experts(): pl.pallas_call(functools.partial(expert_kernel, pieces, offsets, block),...  57.3 us
    ppermute x38, starting transfers between devices, send(): return lax.ppermute(value, AXES, pairs)  40 us
    slice x8, local copies, waits for them, and re-layouts, tables(): hi[:, :, block:]  5.33 us
  transfers between devices with their start and end apart: 38, of which 12 were waited for; matrix products, arithmetic and copies ran while one was open for 14% of the time, Pallas kernels for 30%

profile of v1, /device:TPU:0, one launch (start us, length us, event | category | flops | bytes accessed | tf_op | source)
XLA Modules:
  0.0 191.9 jit_solution(7875431885419151894)
XLA Ops:
  2.0 5.1 %collective-permute-start.8 = (bf16[136,1024]{1,0:T(8,128)(2,1)S(1)}, bf16[136,1024]{1,0:T(8,128)(2,1)S(1)}, u32[]{:S(2)}, u32[]{:S(2)}) collective-permute-start(bf16[136,1024]{1,0:T(8,128)(2,1)S(1)} %get-tuple-element.37), channel_id=1, source_target_pairs={{0,24},{1,25},{2,26},{3,27},{4,28},{5,29},{6,30},{7,31},{8,0},{9,1... | collective-permute-start | bytes 835592 | tf_op jit(solution)/shard_map/ppermute | solution.py:120
  7.1 1.5 collective-permute-start
  9.6 4.6 %collective-permute-done.8 = bf16[136,1024]{1,0:T(8,128)(2,1)S(1)} collective-permute-done((bf16[136,1024]{1,0:T(8,128)(2,1)S(1)}, bf16[136,1024]{1,0:T(8,128)(2,1)S(1)}, u32[]{:S(2)}, u32[]{:S(2)}) %collective-permute-start.8) | collective-permute-done | bytes 278560 | tf_op jit(solution)/shard_map/ppermute | solution.py:120
  14.2 1.5 collective-permute-start.9
  17.0 1.6 collective-permute-start.1
  18.6 2.6 %collective-permute-done.18 = bf16[136,1024]{1,0:T(8,128)(2,1)S(1)} collective-permute-done((bf16[136,1024]{1,0:T(8,128)(2,1)S(1)}, bf16[136,1024]{1,0:T(8,128)(2,1)S(1)}, u32[]{:S(2)}, u32[]{:S(2)}) %collective-permute-start.18) | collective-permute-done | bytes 278560 | tf_op jit(solution)/shard_map/ppermute | solution.py:120
  21.2 1.5 collective-permute-start.19
  22.7 8.2 %collective-permute-done.28 = bf16[136,1024]{1,0:T(8,128)(2,1)S(1)} collective-permute-done((bf16[136,1024]{1,0:T(8,128)(2,1)S(1)}, bf16[136,1024]{1,0:T(8,128)(2,1)S(1)}, u32[]{:S(2)}, u32[]{:S(2)}) %collective-permute-start.28) | collective-permute-done | bytes 278560 | tf_op jit(solution)/shard_map/ppermute | solution.py:120
  30.9 1.5 collective-permute-start.29
  32.5 1.6 collective-permute-start.10
  34.9 5.5 %collective-permute-done.29 = bf16[1,1,136,1024]{3,2,1,0:T(8,128)(2,1)S(1)} collective-permute-done((bf16[1,1,136,1024]{3,2,1,0:T(8,128)(2,1)S(1)}, bf16[1,1,136,1024]{3,2,1,0:T(8,128)(2,1)S(1)}, u32[]{:S(2)}, u32[]{:S(2)}) %collective-permute-start.29) | collective-permute-done | bytes 278560 | tf_op jit(solution)/shard_map/ppermute | solution.py:120
  40.4 1.6 collective-permute-start.20
  54.5 1.4 collective-permute-done.30.refs_1_
  63.3 14.2 %shard_map.82 = (bf16[2,1,128,1024]{3,2,1,0:T(8,128)(2,1)}, bf16[2,1,128,1024]{3,2,1,0:T(8,128)(2,1)}, bf16[2,1,128,1024]{3,2,1,0:T(8,128)(2,1)}, bf16[2,1,128,1024]{3,2,1,0:T(8,128)(2,1)}) custom-call(s32[2,4]{1,0:T(2,128)} %fusion.20.order_ref, bf16[2,1,136,1024]{3,2,1,0:T(8,128)(2,1)} %copy-done.3, ...), custom_call_target="tpu_custom_call" | custom-call | flops 4831838208 | bytes 18874368 | tf_op jit(solution)/shard_map/pallas_call | solution.py:86
  81.8 14.4 %shard_map.83 = (bf16[2,1,128,1024]{3,2,1,0:T(8,128)(2,1)}, bf16[2,1,128,1024]{3,2,1,0:T(8,128)(2,1)}, bf16[2,1,128,1024]{3,2,1,0:T(8,128)(2,1)}, bf16[2,1,128,1024]{3,2,1,0:T(8,128)(2,1)}) custom-call(s32[2,4]{1,0:T(2,128)} %fusion.20.order_ref, bf16[2,1,136,1024]{3,2,1,0:T(8,128)(2,1)} %copy-done.2, ...), custom_call_target="tpu_custom_call" | custom-call | flops 4831838208 | bytes 18874368 | tf_op jit(solution)/shard_map/pallas_call | solution.py:86
  97.6 14.2 %shard_map.84 = (bf16[2,1,128,1024]{3,2,1,0:T(8,128)(2,1)}, bf16[2,1,128,1024]{3,2,1,0:T(8,128)(2,1)}, bf16[2,1,128,1024]{3,2,1,0:T(8,128)(2,1)}, bf16[2,1,128,1024]{3,2,1,0:T(8,128)(2,1)}) custom-call(s32[2,4]{1,0:T(2,128)} %fusion.20.order_ref, bf16[2,1,136,1024]{3,2,1,0:T(8,128)(2,1)} %copy-done.1, ...), custom_call_target="tpu_custom_call" | custom-call | flops 4831838208 | bytes 18874368 | tf_op jit(solution)/shard_map/pallas_call | solution.py:86
  113.2 14.6 %shard_map.85 = (bf16[2,1,128,1024]{3,2,1,0:T(8,128)(2,1)}, bf16[2,1,128,1024]{3,2,1,0:T(8,128)(2,1)}, bf16[2,1,128,1024]{3,2,1,0:T(8,128)(2,1)}, bf16[2,1,128,1024]{3,2,1,0:T(8,128)(2,1)}) custom-call(s32[2,4]{1,0:T(2,128)} %fusion.20.order_ref, bf16[2,1,136,1024]{3,2,1,0:T(8,128)(2,1)} %copy-done, bf16[2,1,136,1024]{3,2,1,0:T(8,128)(2,1)} %copy-done.4, ...), custom_call_target="tpu_custom_call" | custom-call | flops 4831838208 | bytes 18874368 | tf_op jit(solution)/shard_map/pallas_call | solution.py:86
  128.9 1.7 collective-permute-start.6
  130.8 1.6 collective-permute-start.15
  133.7 4.4 %collective-permute-done.6 = bf16[2,1,128,1024]{3,2,1,0:T(8,128)(2,1)S(1)} collective-permute-done((bf16[2,1,128,1024]{3,2,1,0:T(8,128)(2,1)S(1)}, bf16[2,1,128,1024]{3,2,1,0:T(8,128)(2,1)S(1)}, u32[]{:S(2)}, u32[]{:S(2)}) %collective-permute-start.6) | collective-permute-done | bytes 524320 | tf_op jit(solution)/shard_map/ppermute | solution.py:120
  138.1 1.6 collective-permute-start.25
  140.5 3.2 %collective-permute-done.15 = bf16[2,1,128,1024]{3,2,1,0:T(8,128)(2,1)S(1)} collective-permute-done((bf16[2,1,128,1024]{3,2,1,0:T(8,128)(2,1)S(1)}, bf16[2,1,128,1024]{3,2,1,0:T(8,128)(2,1)S(1)}, u32[]{:S(2)}, u32[]{:S(2)}) %collective-permute-start.15) | collective-permute-done | bytes 524320 | tf_op jit(solution)/shard_map/ppermute | solution.py:120
  143.7 1.5 collective-permute-start.7
  146.1 6.9 %collective-permute-done.25 = bf16[2,1,128,1024]{3,2,1,0:T(8,128)(2,1)S(1)} collective-permute-done((bf16[2,1,128,1024]{3,2,1,0:T(8,128)(2,1)S(1)}, bf16[2,1,128,1024]{3,2,1,0:T(8,128)(2,1)S(1)}, u32[]{:S(2)}, u32[]{:S(2)}) %collective-permute-start.25) | collective-permute-done | bytes 524320 | tf_op jit(solution)/shard_map/ppermute | solution.py:120
  153.4 1.6 collective-permute-start.26
  154.9 8.4 %collective-permute-done.35 = bf16[2,1,128,1024]{3,2,1,0:T(8,128)(2,1)S(1)} collective-permute-done((bf16[2,1,128,1024]{3,2,1,0:T(8,128)(2,1)S(1)}, bf16[2,1,128,1024]{3,2,1,0:T(8,128)(2,1)S(1)}, u32[]{:S(2)}, u32[]{:S(2)}) %collective-permute-start.35) | collective-permute-done | bytes 524320 | tf_op jit(solution)/shard_map/ppermute | solution.py:120
  163.7 1.6 collective-permute-start.36
  165.3 6.1 %collective-permute-start.17 = (bf16[128,1024]{1,0:T(8,128)(2,1)S(1)}, bf16[128,1024]{1,0:T(8,128)(2,1)S(1)}, u32[]{:S(2)}, u32[]{:S(2)}) collective-permute-start(bf16[128,1024]{1,0:T(8,128)(2,1)S(1)} %fusion.10), channel_id=1, source_target_pairs={{0,8},{1,9},{2,10},{3,11},{4,12},{5,13},{6,14},{7,15},{8,16},{9,17... | collective-permute-start | bytes 786440 | tf_op jit(solution)/shard_map/ppermute | solution.py:120
  171.7 1.5 collective-permute-start.37
  173.2 5.0 %collective-permute-done.17 = bf16[128,1024]{1,0:T(8,128)(2,1)S(1)} collective-permute-done((bf16[128,1024]{1,0:T(8,128)(2,1)S(1)}, bf16[128,1024]{1,0:T(8,128)(2,1)S(1)}, u32[]{:S(2)}, u32[]{:S(2)}) %collective-permute-start.17) | collective-permute-done | bytes 262176 | tf_op jit(solution)/shard_map/ppermute | solution.py:120
  178.2 5.6 %collective-permute-done.27 = bf16[128,1024]{1,0:T(8,128)(2,1)S(1)} collective-permute-done((bf16[128,1024]{1,0:T(8,128)(2,1)S(1)}, bf16[128,1024]{1,0:T(8,128)(2,1)S(1)}, u32[]{:S(2)}, u32[]{:S(2)}) %collective-permute-start.27) | collective-permute-done | bytes 262176 | tf_op jit(solution)/shard_map/ppermute | solution.py:120
  183.8 7.2 %collective-permute-done.37 = bf16[128,1024]{1,0:T(8,128)(2,1)S(1)} collective-permute-done((bf16[128,1024]{1,0:T(8,128)(2,1)S(1)}, bf16[128,1024]{1,0:T(8,128)(2,1)S(1)}, u32[]{:S(2)}, u32[]{:S(2)}) %collective-permute-start.37) | collective-permute-done | bytes 262176 | tf_op jit(solution)/shard_map/ppermute | solution.py:120
  (229 shorter events, 37.5 us)
Async XLA Ops:
  2.0 12.2 %collective-permute-start.8 = (bf16[136,1024]{1,0:T(8,128)(2,1)S(1)}, bf16[136,1024]{1,0:T(8,128)(2,1)S(1)}, u32[]{:S(2)}, u32[]{:S(2)}) collective-permute-start(bf16[136,1024]{1,0:T(8,128)(2,1)S(1)} %get-tuple-element.37), channel_id=1, source_target_pairs={{0,24},{1,25},{2,26},{3,27},{4,28},{5,29},{6,30},{7,31},{8,0},{9,1... | collective-permute-start | bytes 835592 | tf_op jit(solution)/shard_map/ppermute | solution.py:120
  8.6 12.5 %collective-permute-start.18 = (bf16[136,1024]{1,0:T(8,128)(2,1)S(1)}, bf16[136,1024]{1,0:T(8,128)(2,1)S(1)}, u32[]{:S(2)}, u32[]{:S(2)}) collective-permute-start(bf16[136,1024]{1,0:T(8,128)(2,1)S(1)} %get-tuple-element.37), channel_id=1, source_target_pairs={{0,8},{1,9},{2,10},{3,11},{4,12},{5,13},{6,14},{7,15},{8,16},{9,17... | collective-permute-start | bytes 835592 | tf_op jit(solution)/shard_map/ppermute | solution.py:120
  8.6 22.2 %collective-permute-start.28 = (bf16[136,1024]{1,0:T(8,128)(2,1)S(1)}, bf16[136,1024]{1,0:T(8,128)(2,1)S(1)}, u32[]{:S(2)}, u32[]{:S(2)}) collective-permute-start(bf16[136,1024]{1,0:T(8,128)(2,1)S(1)} %get-tuple-element.37), channel_id=1, source_target_pairs={{0,16},{1,17},{2,18},{3,19},{4,20},{5,21},{6,22},{7,23},{8,24},{9,... | collective-permute-start | bytes 835592 | tf_op jit(solution)/shard_map/ppermute | solution.py:120
  14.2 18.2 %collective-permute-start.9 = (bf16[1,1,136,1024]{3,2,1,0:T(8,128)(2,1)S(1)}, bf16[1,1,136,1024]{3,2,1,0:T(8,128)(2,1)S(1)}, u32[]{:S(2)}, u32[]{:S(2)}) collective-permute-start(bf16[1,1,136,1024]{3,2,1,0:T(8,128)(2,1)S(1)} %bitcast.192), channel_id=1, source_target_pairs={{0,1},{1,0},{2,3},{3,2},{4,6},{5,7},{6,4},{7,5},{8,9},{9,8},{10,11... | collective-permute-start | bytes 835592 | tf_op jit(solution)/shard_map/ppermute | solution.py:120
  17.0 27.1 %collective-permute-start.1 = (bf16[2,1,136,1024]{3,2,1,0:T(8,128)(2,1)S(1)}, bf16[2,1,136,1024]{3,2,1,0:T(8,128)(2,1)}, u32[]{:S(2)}, u32[]{:S(2)}) collective-permute-start(bf16[2,1,136,1024]{3,2,1,0:T(8,128)(2,1)S(1)} %pad_maximum_fusion.refs_0_), channel_id=1, source_target_pairs={{0,2},{1,3},{2,0},{3,1},{4,5},{5,4},{6,7},{7,6},{8,10},{9,11},{10,... | collective-permute-start | bytes 1671176 | tf_op jit(solution)/shard_map/ppermute | solution.py:120
  18.6 24.1 %collective-permute-start.2 = (bf16[2,1,136,1024]{3,2,1,0:T(8,128)(2,1)S(1)}, bf16[2,1,136,1024]{3,2,1,0:T(8,128)(2,1)}, u32[]{:S(2)}, u32[]{:S(2)}) collective-permute-start(bf16[2,1,136,1024]{3,2,1,0:T(8,128)(2,1)S(1)} %pad_maximum_fusion.refs_0_), channel_id=1, source_target_pairs={{0,4},{1,5},{2,6},{3,7},{4,0},{5,1},{6,2},{7,3},{8,12},{9,13},{10,... | collective-permute-start | bytes 1671176 | tf_op jit(solution)/shard_map/ppermute | solution.py:120
  21.2 12.9 %collective-permute-start.19 = (bf16[1,1,136,1024]{3,2,1,0:T(8,128)(2,1)S(1)}, bf16[1,1,136,1024]{3,2,1,0:T(8,128)(2,1)S(1)}, u32[]{:S(2)}, u32[]{:S(2)}) collective-permute-start(bf16[1,1,136,1024]{3,2,1,0:T(8,128)(2,1)S(1)} %bitcast.189), channel_id=1, source_target_pairs={{0,1},{1,0},{2,3},{3,2},{4,6},{5,7},{6,4},{7,5},{8,9},{9,8},{10,11... | collective-permute-start | bytes 835592 | tf_op jit(solution)/shard_map/ppermute | solution.py:120
  32.5 13.1 %collective-permute-start.10 = (bf16[2,1,136,1024]{3,2,1,0:T(8,128)(2,1)S(1)}, bf16[2,1,136,1024]{3,2,1,0:T(8,128)(2,1)}, u32[]{:S(2)}, u32[]{:S(2)}) collective-permute-start(bf16[2,1,136,1024]{3,2,1,0:T(8,128)(2,1)S(1)} %pad_maximum_fusion.1.refs_0_), channel_id=1, source_target_pairs={{0,2},{1,3},{2,0},{3,1},{4,5},{5,4},{6,7},{7,6},{8,10},{9,11},{10,... | collective-permute-start | bytes 1671176 | tf_op jit(solution)/shard_map/ppermute | solution.py:120
  34.1 13.7 %collective-permute-start.11 = (bf16[2,1,136,1024]{3,2,1,0:T(8,128)(2,1)S(1)}, bf16[2,1,136,1024]{3,2,1,0:T(8,128)(2,1)}, u32[]{:S(2)}, u32[]{:S(2)}) collective-permute-start(bf16[2,1,136,1024]{3,2,1,0:T(8,128)(2,1)S(1)} %pad_maximum_fusion.1.refs_0_), channel_id=1, source_target_pairs={{0,4},{1,5},{2,6},{3,7},{4,0},{5,1},{6,2},{7,3},{8,12},{9,13},{10,... | collective-permute-start | bytes 1671176 | tf_op jit(solution)/shard_map/ppermute | solution.py:120
  40.4 11.1 %collective-permute-start.20 = (bf16[2,1,136,1024]{3,2,1,0:T(8,128)(2,1)S(1)}, bf16[2,1,136,1024]{3,2,1,0:T(8,128)(2,1)}, u32[]{:S(2)}, u32[]{:S(2)}) collective-permute-start(bf16[2,1,136,1024]{3,2,1,0:T(8,128)(2,1)S(1)} %pad_maximum_fusion.2.refs_0_), channel_id=1, source_target_pairs={{0,2},{1,3},{2,0},{3,1},{4,5},{5,4},{6,7},{7,6},{8,10},{9,11},{10,... | collective-permute-start | bytes 1671176 | tf_op jit(solution)/shard_map/ppermute | solution.py:120
  44.2 11.7 %collective-permute-start.30 = (bf16[2,1,136,1024]{3,2,1,0:T(8,128)(2,1)S(1)}, bf16[2,1,136,1024]{3,2,1,0:T(8,128)(2,1)S(1)}, u32[]{:S(2)}, u32[]{:S(2)}) collective-permute-start(bf16[2,1,136,1024]{3,2,1,0:T(8,128)(2,1)S(1)} %pad_maximum_fusion.3.refs_0_), channel_id=1, source_target_pairs={{0,2},{1,3},{2,0},{3,1},{4,5},{5,4},{6,7},{7,6},{8,10},{9,11},{10,... | collective-permute-start | bytes 1671176 | tf_op jit(solution)/shard_map/ppermute | solution.py:120
  45.5 13.1 %collective-permute-start.31 = (bf16[2,1,136,1024]{3,2,1,0:T(8,128)(2,1)S(1)}, bf16[2,1,136,1024]{3,2,1,0:T(8,128)(2,1)S(1)}, u32[]{:S(2)}, u32[]{:S(2)}) collective-permute-start(bf16[2,1,136,1024]{3,2,1,0:T(8,128)(2,1)S(1)} %pad_maximum_fusion.3.refs_0_), channel_id=1, source_target_pairs={{0,4},{1,5},{2,6},{3,7},{4,0},{5,1},{6,2},{7,3},{8,12},{9,13},{10,... | collective-permute-start | bytes 1671176 | tf_op jit(solution)/shard_map/ppermute | solution.py:120
  47.8 12.3 %collective-permute-start.3 = (bf16[2,1,136,1024]{3,2,1,0:T(8,128)(2,1)}, bf16[2,1,136,1024]{3,2,1,0:T(8,128)(2,1)}, u32[]{:S(2)}, u32[]{:S(2)}) collective-permute-start(bf16[2,1,136,1024]{3,2,1,0:T(8,128)(2,1)} %collective-permute-done.1.refs_1_), channel_id=1, source_target_pairs={{0,4},{1,5},{2,6},{3,7},{4,0},{5,1},{6,2},{7,3},{8,12},{9,13},{10,... | collective-permute-start | bytes 1671176 | tf_op jit(solution)/shard_map/ppermute | solution.py:120
  58.7 19.4 %collective-permute-start.12 = (bf16[2,1,136,1024]{3,2,1,0:T(8,128)(2,1)}, bf16[2,1,136,1024]{3,2,1,0:T(8,128)(2,1)}, u32[]{:S(2)}, u32[]{:S(2)}) collective-permute-start(bf16[2,1,136,1024]{3,2,1,0:T(8,128)(2,1)} %collective-permute-done.10.refs_1_), channel_id=1, source_target_pairs={{0,4},{1,5},{2,6},{3,7},{4,0},{5,1},{6,2},{7,3},{8,12},{9,13},{10,... | collective-permute-start | bytes 1671176 | tf_op jit(solution)/shard_map/ppermute | solution.py:120
  58.8 20.2 %collective-permute-start.22 = (bf16[2,1,136,1024]{3,2,1,0:T(8,128)(2,1)}, bf16[2,1,136,1024]{3,2,1,0:T(8,128)(2,1)}, u32[]{:S(2)}, u32[]{:S(2)}) collective-permute-start(bf16[2,1,136,1024]{3,2,1,0:T(8,128)(2,1)} %collective-permute-done.20.refs_1_), channel_id=1, source_target_pairs={{0,4},{1,5},{2,6},{3,7},{4,0},{5,1},{6,2},{7,3},{8,12},{9,13},{10,... | collective-permute-start | bytes 1671176 | tf_op jit(solution)/shard_map/ppermute | solution.py:120
  59.3 20.7 %collective-permute-start.32 = (bf16[2,1,136,1024]{3,2,1,0:T(8,128)(2,1)S(1)}, bf16[2,1,136,1024]{3,2,1,0:T(8,128)(2,1)}, u32[]{:S(2)}, u32[]{:S(2)}) collective-permute-start(bf16[2,1,136,1024]{3,2,1,0:T(8,128)(2,1)S(1)} %collective-permute-done.30.refs_1_), channel_id=1, source_target_pairs={{0,4},{1,5},{2,6},{3,7},{4,0},{5,1},{6,2},{7,3},{8,12},{9,13},{10,... | collective-permute-start | bytes 1671176 | tf_op jit(solution)/shard_map/ppermute | solution.py:120
  77.5 50.2 %collective-permute-start.5 = (bf16[2,1,128,1024]{3,2,1,0:T(8,128)(2,1)}, bf16[2,1,128,1024]{3,2,1,0:T(8,128)(2,1)S(1)}, u32[]{:S(2)}, u32[]{:S(2)}) collective-permute-start(bf16[2,1,128,1024]{3,2,1,0:T(8,128)(2,1)} %get-tuple-element.24), channel_id=1, source_target_pairs={{0,4},{1,5},{2,6},{3,7},{4,0},{5,1},{6,2},{7,3},{8,12},{9,13},{10,... | collective-permute-start | bytes 1572872 | tf_op jit(solution)/shard_map/ppermute | solution.py:120
  78.0 55.6 %collective-permute-start.4 = (bf16[2,1,128,1024]{3,2,1,0:T(8,128)(2,1)}, bf16[2,1,128,1024]{3,2,1,0:T(8,128)(2,1)S(1)}, u32[]{:S(2)}, u32[]{:S(2)}) collective-permute-start(bf16[2,1,128,1024]{3,2,1,0:T(8,128)(2,1)} %get-tuple-element.22), channel_id=1, source_target_pairs={{0,4},{1,5},{2,6},{3,7},{4,0},{5,1},{6,2},{7,3},{8,12},{9,13},{10,... | collective-permute-start | bytes 1572872 | tf_op jit(solution)/shard_map/ppermute | solution.py:120
  96.2 31.9 %collective-permute-start.14 = (bf16[2,1,128,1024]{3,2,1,0:T(8,128)(2,1)}, bf16[2,1,128,1024]{3,2,1,0:T(8,128)(2,1)S(1)}, u32[]{:S(2)}, u32[]{:S(2)}) collective-permute-start(bf16[2,1,128,1024]{3,2,1,0:T(8,128)(2,1)} %get-tuple-element.28), channel_id=1, source_target_pairs={{0,4},{1,5},{2,6},{3,7},{4,0},{5,1},{6,2},{7,3},{8,12},{9,13},{10,... | collective-permute-start | bytes 1572872 | tf_op jit(solution)/shard_map/ppermute | solution.py:120
  96.6 43.4 %collective-permute-start.13 = (bf16[2,1,128,1024]{3,2,1,0:T(8,128)(2,1)}, bf16[2,1,128,1024]{3,2,1,0:T(8,128)(2,1)S(1)}, u32[]{:S(2)}, u32[]{:S(2)}) collective-permute-start(bf16[2,1,128,1024]{3,2,1,0:T(8,128)(2,1)} %get-tuple-element.26), channel_id=1, source_target_pairs={{0,4},{1,5},{2,6},{3,7},{4,0},{5,1},{6,2},{7,3},{8,12},{9,13},{10,... | collective-permute-start | bytes 1572872 | tf_op jit(solution)/shard_map/ppermute | solution.py:120
  111.8 17.0 %collective-permute-start.24 = (bf16[2,1,128,1024]{3,2,1,0:T(8,128)(2,1)}, bf16[2,1,128,1024]{3,2,1,0:T(8,128)(2,1)S(1)}, u32[]{:S(2)}, u32[]{:S(2)}) collective-permute-start(bf16[2,1,128,1024]{3,2,1,0:T(8,128)(2,1)} %get-tuple-element.32), channel_id=1, source_target_pairs={{0,4},{1,5},{2,6},{3,7},{4,0},{5,1},{6,2},{7,3},{8,12},{9,13},{10,... | collective-permute-start | bytes 1572872 | tf_op jit(solution)/shard_map/ppermute | solution.py:120
  127.8 17.7 %collective-permute-start.23 = (bf16[2,1,128,1024]{3,2,1,0:T(8,128)(2,1)S(1)}, bf16[2,1,128,1024]{3,2,1,0:T(8,128)(2,1)S(1)}, u32[]{:S(2)}, u32[]{:S(2)}) collective-permute-start(bf16[2,1,128,1024]{3,2,1,0:T(8,128)(2,1)S(1)} %copy-done.14), channel_id=1, source_target_pairs={{0,4},{1,5},{2,6},{3,7},{4,0},{5,1},{6,2},{7,3},{8,12},{9,13},{10,... | collective-permute-start | bytes 1572872 | tf_op jit(solution)/shard_map/ppermute | solution.py:120
  130.8 13.0 %collective-permute-start.15 = (bf16[2,1,128,1024]{3,2,1,0:T(8,128)(2,1)S(1)}, bf16[2,1,128,1024]{3,2,1,0:T(8,128)(2,1)S(1)}, u32[]{:S(2)}, u32[]{:S(2)}) collective-permute-start(bf16[2,1,128,1024]{3,2,1,0:T(8,128)(2,1)S(1)} %add_convert_fusion.2), channel_id=1, source_target_pairs={{0,2},{1,3},{2,0},{3,1},{4,5},{5,4},{6,7},{7,6},{8,10},{9,11},{10,... | collective-permute-start | bytes 1572872 | tf_op jit(solution)/shard_map/ppermute | solution.py:120
  133.6 21.3 %collective-permute-start.33 = (bf16[2,1,128,1024]{3,2,1,0:T(8,128)(2,1)S(1)}, bf16[2,1,128,1024]{3,2,1,0:T(8,128)(2,1)S(1)}, u32[]{:S(2)}, u32[]{:S(2)}) collective-permute-start(bf16[2,1,128,1024]{3,2,1,0:T(8,128)(2,1)S(1)} %copy-done.15), channel_id=1, source_target_pairs={{0,4},{1,5},{2,6},{3,7},{4,0},{5,1},{6,2},{7,3},{8,12},{9,13},{10,... | collective-permute-start | bytes 1572872 | tf_op jit(solution)/shard_map/ppermute | solution.py:120
  138.1 15.0 %collective-permute-start.25 = (bf16[2,1,128,1024]{3,2,1,0:T(8,128)(2,1)S(1)}, bf16[2,1,128,1024]{3,2,1,0:T(8,128)(2,1)S(1)}, u32[]{:S(2)}, u32[]{:S(2)}) collective-permute-start(bf16[2,1,128,1024]{3,2,1,0:T(8,128)(2,1)S(1)} %add_convert_fusion.1), channel_id=1, source_target_pairs={{0,2},{1,3},{2,0},{3,1},{4,5},{5,4},{6,7},{7,6},{8,10},{9,11},{10,... | collective-permute-start | bytes 1572872 | tf_op jit(solution)/shard_map/ppermute | solution.py:120
  140.1 23.3 %collective-permute-start.35 = (bf16[2,1,128,1024]{3,2,1,0:T(8,128)(2,1)S(1)}, bf16[2,1,128,1024]{3,2,1,0:T(8,128)(2,1)S(1)}, u32[]{:S(2)}, u32[]{:S(2)}) collective-permute-start(bf16[2,1,128,1024]{3,2,1,0:T(8,128)(2,1)S(1)} %add_convert_fusion), channel_id=1, source_target_pairs={{0,2},{1,3},{2,0},{3,1},{4,5},{5,4},{6,7},{7,6},{8,10},{9,11},{10,... | collective-permute-start | bytes 1572872 | tf_op jit(solution)/shard_map/ppermute | solution.py:120
  143.7 29.5 %collective-permute-start.7 = (bf16[1,1,128,1024]{3,2,1,0:T(8,128)(2,1)S(1)}, bf16[1,1,128,1024]{3,2,1,0:T(8,128)(2,1)S(1)}, u32[]{:S(2)}, u32[]{:S(2)}) collective-permute-start(bf16[1,1,128,1024]{3,2,1,0:T(8,128)(2,1)S(1)} %slice.481), channel_id=1, source_target_pairs={{0,1},{1,0},{2,3},{3,2},{4,6},{5,7},{6,4},{7,5},{8,9},{9,8},{10,11... | collective-permute-start | bytes 786440 | tf_op jit(solution)/shard_map/ppermute | solution.py:120
  145.5 19.7 %collective-permute-start.16 = (bf16[1,1,128,1024]{3,2,1,0:T(8,128)(2,1)S(1)}, bf16[1,1,128,1024]{3,2,1,0:T(8,128)(2,1)S(1)}, u32[]{:S(2)}, u32[]{:S(2)}) collective-permute-start(bf16[1,1,128,1024]{3,2,1,0:T(8,128)(2,1)S(1)} %slice.480), channel_id=1, source_target_pairs={{0,1},{1,0},{2,3},{3,2},{4,6},{5,7},{6,4},{7,5},{8,9},{9,8},{10,11... | collective-permute-start | bytes 786440 | tf_op jit(solution)/shard_map/ppermute | solution.py:120
  153.4 18.1 %collective-permute-start.26 = (bf16[1,1,128,1024]{3,2,1,0:T(8,128)(2,1)S(1)}, bf16[1,1,128,1024]{3,2,1,0:T(8,128)(2,1)S(1)}, u32[]{:S(2)}, u32[]{:S(2)}) collective-permute-start(bf16[1,1,128,1024]{3,2,1,0:T(8,128)(2,1)S(1)} %slice.479), channel_id=1, source_target_pairs={{0,1},{1,0},{2,3},{3,2},{4,6},{5,7},{6,4},{7,5},{8,9},{9,8},{10,11... | collective-permute-start | bytes 786440 | tf_op jit(solution)/shard_map/ppermute | solution.py:120
  165.3 12.9 %collective-permute-start.17 = (bf16[128,1024]{1,0:T(8,128)(2,1)S(1)}, bf16[128,1024]{1,0:T(8,128)(2,1)S(1)}, u32[]{:S(2)}, u32[]{:S(2)}) collective-permute-start(bf16[128,1024]{1,0:T(8,128)(2,1)S(1)} %fusion.10), channel_id=1, source_target_pairs={{0,8},{1,9},{2,10},{3,11},{4,12},{5,13},{6,14},{7,15},{8,16},{9,17... | collective-permute-start | bytes 786440 | tf_op jit(solution)/shard_map/ppermute | solution.py:120
  171.5 12.3 %collective-permute-start.27 = (bf16[128,1024]{1,0:T(8,128)(2,1)S(1)}, bf16[128,1024]{1,0:T(8,128)(2,1)S(1)}, u32[]{:S(2)}, u32[]{:S(2)}) collective-permute-start(bf16[128,1024]{1,0:T(8,128)(2,1)S(1)} %fusion.11), channel_id=1, source_target_pairs={{0,24},{1,25},{2,26},{3,27},{4,28},{5,29},{6,30},{7,31},{8,0},{9,1... | collective-permute-start | bytes 786440 | tf_op jit(solution)/shard_map/ppermute | solution.py:120
  171.7 19.4 %collective-permute-start.37 = (bf16[128,1024]{1,0:T(8,128)(2,1)S(1)}, bf16[128,1024]{1,0:T(8,128)(2,1)S(1)}, u32[]{:S(2)}, u32[]{:S(2)}) collective-permute-start(bf16[128,1024]{1,0:T(8,128)(2,1)S(1)} %fusion.12), channel_id=1, source_target_pairs={{0,16},{1,17},{2,18},{3,19},{4,20},{5,21},{6,22},{7,23},{8,24},{9,... | collective-permute-start | bytes 786440 | tf_op jit(solution)/shard_map/ppermute | solution.py:120
  (24 other events, 440.8 us)

commit v2 on v0

v2 whole, which is shorter than its diff:
```python
import functools

import jax
import jax.numpy as jnp
from jax import lax
from jax.experimental import pallas as pl
from jax.experimental.pallas import tpu as pltpu
from jax.sharding import PartitionSpec as P

AXES = ("expert", "tensor")
CORES = 2
LANES = 128
SPLIT = 3
epsilon = 1e-06
NT = (((1,), (1,)), ((), ()))
TN = (((0,), (0,)), ((), ()))
f32 = jnp.float32
bf16 = jnp.bfloat16
VMEM = pl.BlockSpec(memory_space=pltpu.VMEM)
SMEM = pl.BlockSpec(memory_space=pltpu.SMEM)


def masks_of(n_tensor):
    first = [1 << b for b in range(n_tensor.bit_length() - 1)]
    return first, first[::-1]


def spread(masks, j):
    out = 0
    for s, m in enumerate(masks):
        if (j >> s) & 1:
            out ^= m
    return out


def mirror(pieces, j):
    first, second = masks_of(pieces)
    return spread([1 << second.index(m) for m in first], j)


def payload_kernel(experts_all, hidden, gain, ids, weights, out):
    block, width = hidden.shape
    h = hidden[...].astype(f32)
    out[0:block, :] = (h * gain[...]).astype(bf16)
    squares = jnp.sum(h * h, axis=1, keepdims=True)
    rows = [jnp.broadcast_to(squares, (block, LANES)).T[0:1, :]]
    for e in range(experts_all):
        rows.append(jnp.sum(jnp.where(ids[...] == e, weights[...], 0.0), axis=0, keepdims=True))
    slots = []
    for v in rows:
        for _ in range(SPLIT):
            part = v.astype(bf16).astype(f32)
            slots.append(part)
            v = v - part
    per_row = width // LANES
    zero = jnp.zeros((1, LANES), f32)
    n_extra = out.shape[0] - block
    slots += [zero] * (n_extra * per_row - len(slots))
    lines = [jnp.concatenate(slots[r * per_row : (r + 1) * per_row], axis=1) for r in range(n_extra)]
    out[block:, :] = jnp.concatenate(lines, axis=0).astype(bf16)


def expert_kernel(pieces, offsets, block, fetch, *refs):
    place, first, a0, a1, b0, b1, wg, wu, wd = refs[:9]
    mine_keep, mine_send, sib_keep, sib_send = refs[9:13]
    xs, hs = refs[13 + 3 * fetch : 15 + 3 * fetch]
    half = pieces // 2
    rows = offsets * block
    width = a0.shape[3]
    n_extra = a0.shape[2] - block
    n_exp, hidden = wg.shape[0], wg.shape[1]
    others = [mirror(pieces, j) for j in range(pieces)]

    def piece(side, j):
        j = others[j] if side else j
        return ((a0, a1), (b0, b1))[side][j // half], j % half

    def columns(j):
        return pl.ds(pl.multiple_of(place[j] * width, width), width)

    copies = []
    if fetch:
        (wg_from, wu_from, wd_from), (wg, wu, wd), sems = (wg, wu, wd), refs[13:16], refs[-1]
        moves = [(x.at[e], y.at[e]) for e in range(n_exp) for x, y in ((wg_from, wg), (wu_from, wu))]
        moves += [(wd_from.at[:, columns(j)], wd.at[:, columns(j)]) for j in range(pieces)]
        copies = [pltpu.make_async_copy(x, y, sems.at[n]) for n, (x, y) in enumerate(moves)]
        for copy in copies:
            copy.start()

    def wait(n):
        if copies:
            copies[n].wait()

    for side in range(2):
        for j in range(pieces):
            src, i = piece(side, j)
            for o in range(offsets):
                at = side * rows + o * block
                xs[at : at + block, j * width : (j + 1) * width] = src[i, o, 0:block, :]

    value = (
        lax.broadcasted_iota(jnp.int32, (n_extra, width), 0) * (width // LANES)
        + lax.broadcasted_iota(jnp.int32, (n_extra, width), 1) // LANES
    ) // SPLIT

    def pick(table, v):
        row = jnp.sum(jnp.where(value == v, table, 0.0), axis=0, keepdims=True)
        return sum(row[:, g * LANES : (g + 1) * LANES] for g in range(width // LANES))

    scales, picked = [], [[] for _ in range(n_exp)]
    for side in range(2):
        for o in range(offsets):
            tables = []
            for j in range(pieces):
                src, i = piece(side, j)
                tables.append(src[i, o, block:, :].astype(f32))
            scales.append(pick(sum(tables), 0))
            for e in range(n_exp):
                picked[e].append(pick(tables[0], first[0] + (1 + e)))
    scale = lax.rsqrt(jnp.concatenate(scales, axis=1) / (pieces * width) + epsilon)

    for e in range(n_exp):
        wait(2 * e)
        wait(2 * e + 1)
        gate = jnp.zeros((hidden, 2 * rows), f32)
        up = jnp.zeros((hidden, 2 * rows), f32)
        for j in range(pieces):
            x = xs[:, j * width : (j + 1) * width]
            gate += lax.dot_general(wg[e, :, columns(j)], x, NT, preferred_element_type=f32)
            up += lax.dot_general(wu[e, :, columns(j)], x, NT, preferred_element_type=f32)
        gate = gate * scale
        inner = gate / (1.0 + jnp.exp(-gate)) * (up * scale) * jnp.concatenate(picked[e], axis=1)
        hs[e * hidden : (e + 1) * hidden, :] = inner.astype(bf16)

    for j in range(pieces):
        wait(2 * n_exp + j)
        out = lax.dot_general(hs[...], wd[:, columns(j)], TN, preferred_element_type=f32).astype(bf16)
        for side, (keep, away) in enumerate(((mine_keep, mine_send), (sib_keep, sib_send))):
            to = others[j] if side else j
            for o in range(offsets):
                at = side * rows + o * block
                (keep if to < half else away)[to % half, o] = out[at : at + block]


def run_experts(place, first, a0, a1, b0, b1, weights, block, fetch):
    half, offsets, _, width = a0.shape
    pieces = 2 * half
    rows = offsets * block
    n_exp, hidden = weights[0].shape[0], weights[2].shape[0]
    held = [pltpu.VMEM(w.shape, w.dtype) for w in weights] if fetch else []
    sems = [pltpu.SemaphoreType.DMA((2 * n_exp + pieces,))] if fetch else []
    out = pl.pallas_call(
        functools.partial(expert_kernel, pieces, offsets, block, fetch),
        out_shape=[jax.ShapeDtypeStruct((half, offsets, block, width), bf16)] * 4 + held,
        in_specs=[SMEM] * 2 + [VMEM] * 4 + [pl.BlockSpec(memory_space=pl.ANY) if fetch else VMEM] * 3,
        out_specs=[VMEM] * (4 + len(held)),
        scratch_shapes=[
            pltpu.VMEM((2 * rows, pieces * width), bf16),
            pltpu.VMEM((hidden, 2 * rows), bf16),
        ]
        + sems,
        compiler_params=pltpu.CompilerParams(vmem_limit_bytes=30 * 1024 * 1024),
        cost_estimate=pl.CostEstimate(
            flops=4 * rows * 3 * hidden * pieces * width,
            bytes_accessed=8 * rows * pieces * width,
            transcendentals=2 * rows * hidden,
        ),
    )(place, first, a0, a1, b0, b1, *weights)
    if fetch:
        weights = [pltpu.with_memory_space_constraint(w, pltpu.VMEM) for w in out[4:]]
    return out[:4], weights


def body(hidden_in, norm_gain, expert_ids, route_weights, w_gate, w_up, w_down):
    block, width = hidden_in.shape
    exp_local = w_gate.shape[0]
    groups, n_tensor = lax.axis_size("expert"), lax.axis_size("tensor")
    n_z = groups // CORES
    experts_all = exp_local * groups
    group_here, slice_here = lax.axis_index("expert"), lax.axis_index("tensor")
    core = group_here % CORES
    masks = masks_of(n_tensor)
    stages = len(masks[0])

    def send(value, target):
        pairs = []
        for z in range(n_z):
            for c in range(CORES):
                for t in range(n_tensor):
                    z2, c2, t2 = target(z, c, t)
                    pairs.append(((z * CORES + c) * n_tensor + t, (z2 * CORES + c2) * n_tensor + t2))
        return lax.ppermute(value, AXES, pairs)

    def stage_swap(value, s):
        return send(value, lambda z, c, t: (z, c, t ^ masks[c][s]))

    def core_swap(value):
        return send(value, lambda z, c, t: (z, 1 - c, t))

    def shift(value, k):
        return send(value, lambda z, c, t: ((z + k) % n_z, c, t)) if k % n_z else value

    slots = SPLIT * (1 + experts_all)
    n_extra = -(-slots // (8 * width // LANES)) * 8
    payload = pl.pallas_call(
        functools.partial(payload_kernel, experts_all),
        out_shape=jax.ShapeDtypeStruct((block + n_extra, width), bf16),
        in_specs=[VMEM] * 4,
        out_specs=VMEM,
    )(hidden_in, norm_gain[None, :], expert_ids.T, route_weights.T)

    chunk = [[spread(masks[c], j) for j in range(n_tensor)] for c in range(CORES)]
    place = slice_here ^ jnp.array(chunk, jnp.int32)[core]
    first = (group_here * exp_local).astype(jnp.int32)[None]

    weights = [w_gate, w_up, w_down.reshape(-1, w_down.shape[2])]

    near = sorted(range(n_z), key=lambda k: min(k, n_z - k))
    blk, far, blk_sib, out, keep, back = {0: payload[None, None]}, {}, {}, {}, {}, {}
    tied = range(1, n_z + 2 * stages)

    def put(store, i, value):
        store[i] = value

    def summed(i, s, got):
        kept = keep[i] + got.astype(f32)
        half = kept.shape[0] // 2
        if s:
            out[i] = kept[half:].astype(bf16)
        keep[i] = kept[:half] if s else kept

    for r in range(n_z + 2 * stages + 1):
        moves = []
        i = r - stages
        if 0 <= i < n_z:
            far_sib = core_swap(far[i])
        for s in range(stages):
            if 0 <= r - s < n_z:
                i = r - s
                got = stage_swap(blk[i], s)
                if s < stages - 1:
                    moves.append((got, lambda got, i=i: put(blk, i, jnp.concatenate([blk[i], got], axis=0))))
                else:
                    moves.append((got, lambda got, i=i: put(far, i, got)))
                    moves.append((core_swap(blk[i]), lambda got, i=i: put(blk_sib, i, got)))
        for s in range(stages):
            i = r - 2 * stages + s
            if 1 <= i <= n_z:
                i %= n_z
                moves.append((stage_swap(out[i], s), lambda got, i=i, s=s: summed(i, s, got)))
        if r + 1 < n_z:
            moves.append((shift(payload, -near[r + 1]), lambda got, i=r + 1: put(blk, i, got[None, None])))
        i = r - 2 * stages - 1
        if 1 <= i < n_z:
            moves.append((shift(keep[i][0, 0].astype(bf16), near[i]), lambda got, i=i: put(back, i, got.astype(f32))))
        made = []
        i = r - stages
        if 0 <= i < n_z:
            made, weights = run_experts(place, first, blk[i], far[i], blk_sib[i], far_sib, weights, block, i == 0)
        gots = [got for got, _ in moves]
        if r in tied:
            gots, made = lax.optimization_barrier((gots, made))
        for got, (_, take) in zip(gots, moves):
            take(got)
        if made:
            mine_keep, mine_send, sib_keep, sib_send = made
            out[i] = (mine_send.astype(f32) + core_swap(sib_send).astype(f32)).astype(bf16)
            keep[i] = mine_keep.astype(f32) + core_swap(sib_keep).astype(f32)
    return sum([back[i] for i in range(1, n_z)], keep[0][0, 0]).astype(bf16)


def solution(mesh):
    placed = (
        P("expert", "tensor"),
        P("tensor"),
        P("expert", None),
        P("expert", None),
        P("expert", "tensor", None),
        P("expert", "tensor", None),
        P("expert", "tensor", None),
    )
    return jax.shard_map(
        body, mesh=mesh, in_specs=placed, out_specs=P("expert", "tensor"), check_vma=False
    )
```

time: 657 us -> 123 us (0.19)
  waiting for transfers between devices: 419 us -> 50.4 us
  blocking collectives: 87.6 us -> 0 us
  local copies, waits for them, and re-layouts: 71.3 us -> 0.13 us
  matrix products: 33.9 us -> 0 us
  starting transfers between devices: 5.74 us -> 38.1 us
  Pallas kernels: 0 us -> 29.1 us
  other arithmetic: 25.7 us -> 4.72 us
  between operations: 13.5 us -> 0.29 us
    all_to_all x1 -> x0, waiting for transfers between devices: 273 us -> none  [body(): lax.all_to_all(partials, 'expert', split_axis=1, concat_axis=0, tiled=True)]
    all_gather x1 -> x0, waiting for transfers between devices: 120 us -> none  [body(): piece = lax.all_gather(arrived, 'tensor', axis=2, tiled=True)]
    all_to_all x1 -> x0, blocking collectives: 76.2 us -> none  [body(): lax.all_to_all(outgoing, 'expert', split_axis=0, concat_axis=1, tiled=True)]
    ppermute x0 -> x38, waiting for transfers between devices: none -> 50.4 us  [send(): return lax.ppermute(value, AXES, pairs)]
    ppermute x0 -> x38, starting transfers between devices: none -> 38.1 us  [send(): return lax.ppermute(value, AXES, pairs)]
    dot_general x5 -> x0, matrix products: 33.9 us -> none  [the longest x1 11.8 us: body(): jnp.einsum('erd,efd->erf', piece, w_gate, preferred_element_type=jnp.floa...]
    another operation x1 -> x0, local copies, waits for them, and re-layouts: 33 us -> none  [local_partials(): return jnp.stack(partial_list, axis=0)]
    pallas_call x0 -> x5, Pallas kernels: none -> 29.1 us  [the longest x4 27.2 us: run_experts(): pl.pallas_call(functools.partial(expert_kernel, pieces, offsets, block, f...]
  transfers between devices with their start and end apart: 3 -> 38, of which waited for: 3 -> 16; matrix products, arithmetic and copies ran while one was open for 0% -> 3% of each run, Pallas kernels for 0% -> 22%
where the time goes in v2:
time: 123 us
  waiting for transfers between devices  50.4 us (41%)
  starting transfers between devices  38.1 us (31%)
  Pallas kernels  29.1 us (24%)
  other arithmetic  4.72 us (4%)
    ppermute x38, waiting for transfers between devices, send(): return lax.ppermute(value, AXES, pairs)  50.4 us
    ppermute x38, starting transfers between devices, send(): return lax.ppermute(value, AXES, pairs)  38.1 us
    pallas_call x4, Pallas kernels, run_experts(): pl.pallas_call(functools.partial(expert_kernel, pieces, offsets, block, f...  27.2 us
  transfers between devices with their start and end apart: 38, of which 16 were waited for; matrix products, arithmetic and copies ran while one was open for 3% of the time, Pallas kernels for 22%

profile of v2, /device:TPU:0, one launch (start us, length us, event | category | flops | bytes accessed | tf_op | source)
XLA Modules:
  0.0 122.7 jit_solution(5291982997285376308)
XLA Ops:
  0.0 1.9 %shard_map.82 = bf16[136,1024]{1,0:T(8,128)(2,1)} custom-call(bf16[128,1024]{1,0:T(8,128)(2,1)} %hidden.1, f32[1,1024]{1,0:T(1,128)} %bitcast.36, s32[8,128]{1,0:T(8,128)} %bitcast.37, f32[8,128]{1,0:T(8,128)} %bitcast.38), custom_call_target="tpu_custom_call" | custom-call | tf_op jit(solution)/shard_map/pallas_call | solution.py:205
  1.9 2.9 %collective-permute-start.2 = (bf16[1,1,136,1024]{3,2,1,0:T(8,128)(2,1)}, bf16[1,1,136,1024]{3,2,1,0:T(8,128)(2,1)S(1)}, u32[]{:S(2)}, u32[]{:S(2)}) collective-permute-start(bf16[1,1,136,1024]{3,2,1,0:T(8,128)(2,1)} %bitcast.28), channel_id=1, source_target_pairs={{0,1},{1,0},{2,3},{3,2},{4,6},{5,7},{6,4},{7,5},{8,9},{9,8},{10,11... | collective-permute-start | bytes 835592 | tf_op jit(solution)/shard_map/ppermute | solution.py:192
  4.8 3.6 %collective-permute-start = (bf16[136,1024]{1,0:T(8,128)(2,1)}, bf16[136,1024]{1,0:T(8,128)(2,1)S(1)}, u32[]{:S(2)}, u32[]{:S(2)}) collective-permute-start(bf16[136,1024]{1,0:T(8,128)(2,1)} %shard_map.82), channel_id=1, source_target_pairs={{0,24},{1,25},{2,26},{3,27},{4,28},{5,29},{6,30},{7,31},{8,0},{9,1... | collective-permute-start | bytes 835592 | tf_op jit(solution)/shard_map/ppermute | solution.py:192
  8.4 1.1 collective-permute-done.2
  10.6 2.1 %collective-permute-start.3 = (bf16[2,1,136,1024]{3,2,1,0:T(8,128)(2,1)S(1)}, bf16[2,1,136,1024]{3,2,1,0:T(8,128)(2,1)S(1)}, u32[]{:S(2)}, u32[]{:S(2)}) collective-permute-start(bf16[2,1,136,1024]{3,2,1,0:T(8,128)(2,1)S(1)} %pad_maximum_fusion.refs_2_), channel_id=1, source_target_pairs={{0,2},{1,3},{2,0},{3,1},{4,5},{5,4},{6,7},{7,6},{8,10},{9,11},{10,... | collective-permute-start | bytes 1671176 | tf_op jit(solution)/shard_map/ppermute | solution.py:192
  12.8 1.6 %collective-permute-start.5 = (bf16[136,1024]{1,0:T(8,128)(2,1)}, bf16[136,1024]{1,0:T(8,128)(2,1)S(1)}, u32[]{:S(2)}, u32[]{:S(2)}) collective-permute-start(bf16[136,1024]{1,0:T(8,128)(2,1)} %shard_map.82), channel_id=1, source_target_pairs={{0,8},{1,9},{2,10},{3,11},{4,12},{5,13},{6,14},{7,15},{8,16},{9,17... | collective-permute-start | bytes 835592 | tf_op jit(solution)/shard_map/ppermute | solution.py:192
  14.4 1.8 %collective-permute-start.1 = (bf16[1,1,136,1024]{3,2,1,0:T(8,128)(2,1)S(1)}, bf16[1,1,136,1024]{3,2,1,0:T(8,128)(2,1)S(1)}, u32[]{:S(2)}, u32[]{:S(2)}) collective-permute-start(bf16[1,1,136,1024]{3,2,1,0:T(8,128)(2,1)S(1)} %bitcast.34), channel_id=1, source_target_pairs={{0,1},{1,0},{2,3},{3,2},{4,6},{5,7},{6,4},{7,5},{8,9},{9,8},{10,11... | collective-permute-start | bytes 835592 | tf_op jit(solution)/shard_map/ppermute | solution.py:192
  16.2 7.3 %collective-permute-done.5 = bf16[136,1024]{1,0:T(8,128)(2,1)S(1)} collective-permute-done((bf16[136,1024]{1,0:T(8,128)(2,1)}, bf16[136,1024]{1,0:T(8,128)(2,1)S(1)}, u32[]{:S(2)}, u32[]{:S(2)}) %collective-permute-start.5) | collective-permute-done | bytes 278560 | tf_op jit(solution)/shard_map/ppermute | solution.py:192
  23.6 2.7 %collective-permute-start.9 = (bf16[136,1024]{1,0:T(8,128)(2,1)}, bf16[136,1024]{1,0:T(8,128)(2,1)S(1)}, u32[]{:S(2)}, u32[]{:S(2)}) collective-permute-start(bf16[136,1024]{1,0:T(8,128)(2,1)} %shard_map.82), channel_id=1, source_target_pairs={{0,16},{1,17},{2,18},{3,19},{4,20},{5,21},{6,22},{7,23},{8,24},{9,... | collective-permute-start | bytes 835592 | tf_op jit(solution)/shard_map/ppermute | solution.py:192
  26.7 1.5 %collective-permute-start.7 = (bf16[2,1,136,1024]{3,2,1,0:T(8,128)(2,1)S(1)}, bf16[2,1,136,1024]{3,2,1,0:T(8,128)(2,1)S(1)}, u32[]{:S(2)}, u32[]{:S(2)}) collective-permute-start(bf16[2,1,136,1024]{3,2,1,0:T(8,128)(2,1)S(1)} %pad_maximum_fusion.1.refs_2_), channel_id=1, source_target_pairs={{0,2},{1,3},{2,0},{3,1},{4,5},{5,4},{6,7},{7,6},{8,10},{9,11},{10,... | collective-permute-start | bytes 1671176 | tf_op jit(solution)/shard_map/ppermute | solution.py:192
  28.9 1.5 %collective-permute-start.6 = (bf16[1,1,136,1024]{3,2,1,0:T(8,128)(2,1)S(1)}, bf16[1,1,136,1024]{3,2,1,0:T(8,128)(2,1)S(1)}, u32[]{:S(2)}, u32[]{:S(2)}) collective-permute-start(bf16[1,1,136,1024]{3,2,1,0:T(8,128)(2,1)S(1)} %bitcast.32), channel_id=1, source_target_pairs={{0,1},{1,0},{2,3},{3,2},{4,6},{5,7},{6,4},{7,5},{8,9},{9,8},{10,11... | collective-permute-start | bytes 835592 | tf_op jit(solution)/shard_map/ppermute | solution.py:192
  30.4 9.6 %shard_map.83 = (bf16[2,1,128,1024]{3,2,1,0:T(8,128)(2,1)S(1)}, bf16[2,1,128,1024]{3,2,1,0:T(8,128)(2,1)S(1)}, bf16[2,1,128,1024]{3,2,1,0:T(8,128)(2,1)S(1)}, bf...) custom-call(s32[4]{0:T(128)S(1)} %xor_bitcast_fusion.refs_0_, ...), custom_call_target="tpu_custom_call" | custom-call | flops 4831838208 | bytes 4194304 | tf_op jit(solution)/shard_map/pallas_call | solution.py:152
  40.8 1.3 %collective-permute-start.13 = (bf16[2,1,136,1024]{3,2,1,0:T(8,128)(2,1)S(1)}, bf16[2,1,136,1024]{3,2,1,0:T(8,128)(2,1)S(1)}, u32[]{:S(2)}, u32[]{:S(2)}) collective-permute-start(bf16[2,1,136,1024]{3,2,1,0:T(8,128)(2,1)S(1)} %pad_maximum_fusion.2.refs_2_), channel_id=1, source_target_pairs={{0,2},{1,3},{2,0},{3,1},{4,5},{5,4},{6,7},{7,6},{8,10},{9,11},{10,... | collective-permute-start | bytes 1671176 | tf_op jit(solution)/shard_map/ppermute | solution.py:192
  42.1 1.5 %collective-permute-start.12 = (bf16[1,1,136,1024]{3,2,1,0:T(8,128)(2,1)S(1)}, bf16[1,1,136,1024]{3,2,1,0:T(8,128)(2,1)S(1)}, u32[]{:S(2)}, u32[]{:S(2)}) collective-permute-start(bf16[1,1,136,1024]{3,2,1,0:T(8,128)(2,1)S(1)} %bitcast.30), channel_id=1, source_target_pairs={{0,1},{1,0},{2,3},{3,2},{4,6},{5,7},{6,4},{7,5},{8,9},{9,8},{10,11... | collective-permute-start | bytes 835592 | tf_op jit(solution)/shard_map/ppermute | solution.py:192
  43.6 5.8 %shard_map.84 = (bf16[2,1,128,1024]{3,2,1,0:T(8,128)(2,1)S(1)}, bf16[2,1,128,1024]{3,2,1,0:T(8,128)(2,1)S(1)}, bf16[2,1,128,1024]{3,2,1,0:T(8,128)(2,1)S(1)}, bf16[2,1,128,1024]{3,2,1,0:T(8,128)(2,1)S(1)}) custom-call(s32[4]{0:T(128)S(1)} %xor_bitcast_fusion.refs_0_, s32[1]{0:T(128)} %bitcast.7.refs_1_, ...), custom_call_target="tpu_custom_call" | custom-call | flops 4831838208 | bytes 4194304 | tf_op jit(solution)/shard_map/pallas_call | solution.py:152
  49.4 2.3 %collective-permute-done.12 = bf16[1,1,136,1024]{3,2,1,0:T(8,128)(2,1)S(1)} collective-permute-done((bf16[1,1,136,1024]{3,2,1,0:T(8,128)(2,1)S(1)}, bf16[1,1,136,1024]{3,2,1,0:T(8,128)(2,1)S(1)}, u32[]{:S(2)}, u32[]{:S(2)}) %collective-permute-start.12) | collective-permute-done | bytes 278560 | tf_op jit(solution)/shard_map/ppermute | solution.py:192
  51.7 1.6 %collective-permute-done.13.refs_3_ = bf16[2,1,136,1024]{3,2,1,0:T(8,128)(2,1)S(1)} collective-permute-done((bf16[2,1,136,1024]{3,2,1,0:T(8,128)(2,1)S(1)}, bf16[2,1,136,1024]{3,2,1,0:T(8,128)(2,1)S(1)}, u32[]{:S(2)}, u32[]{:S(2)}) %collective-permute-start.13) | collective-permute-done | bytes 557088 | tf_op jit(solution)/shard_map/ppermute | solution.py:192
  54.0 1.4 %collective-permute-start.17 = (bf16[2,1,136,1024]{3,2,1,0:T(8,128)(2,1)S(1)}, bf16[2,1,136,1024]{3,2,1,0:T(8,128)(2,1)S(1)}, u32[]{:S(2)}, u32[]{:S(2)}) collective-permute-start(bf16[2,1,136,1024]{3,2,1,0:T(8,128)(2,1)S(1)} %pad_maximum_fusion.3.refs_2_), channel_id=1, source_target_pairs={{0,2},{1,3},{2,0},{3,1},{4,5},{5,4},{6,7},{7,6},{8,10},{9,11},{10,... | collective-permute-start | bytes 1671176 | tf_op jit(solution)/shard_map/ppermute | solution.py:192
  55.6 1.3 %collective-permute-start.20 = (bf16[2,1,128,1024]{3,2,1,0:T(8,128)(2,1)S(1)}, bf16[2,1,128,1024]{3,2,1,0:T(8,128)(2,1)S(1)}, u32[]{:S(2)}, u32[]{:S(2)}) collective-permute-start(bf16[2,1,128,1024]{3,2,1,0:T(8,128)(2,1)S(1)} %add_convert_fusion.3), channel_id=1, source_target_pairs={{0,2},{1,3},{2,0},{3,1},{4,5},{5,4},{6,7},{7,6},{8,10},{9,11},{10,... | collective-permute-start | bytes 1572872 | tf_op jit(solution)/shard_map/ppermute | solution.py:192
  56.8 6.0 %shard_map.85 = (bf16[2,1,128,1024]{3,2,1,0:T(8,128)(2,1)S(1)}, bf16[2,1,128,1024]{3,2,1,0:T(8,128)(2,1)S(1)}, bf16[2,1,128,1024]{3,2,1,0:T(8,128)(2,1)S(1)}, bf16[2,1,128,1024]{3,2,1,0:T(8,128)(2,1)S(1)}) custom-call(s32[4]{0:T(128)S(1)} %xor_bitcast_fusion.refs_0_, s32[1]{0:T(128)} %bitcast.7.refs_1_, ...), custom_call_target="tpu_custom_call" | custom-call | flops 4831838208 | bytes 4194304 | tf_op jit(solution)/shard_map/pallas_call | solution.py:152
  63.6 5.6 %collective-permute-done.20 = bf16[2,1,128,1024]{3,2,1,0:T(8,128)(2,1)S(1)} collective-permute-done((bf16[2,1,128,1024]{3,2,1,0:T(8,128)(2,1)S(1)}, bf16[2,1,128,1024]{3,2,1,0:T(8,128)(2,1)S(1)}, u32[]{:S(2)}, u32[]{:S(2)}) %collective-permute-start.20) | collective-permute-done | bytes 524320 | tf_op jit(solution)/shard_map/ppermute | solution.py:192
  69.7 1.4 %collective-permute-done.23 = bf16[2,1,128,1024]{3,2,1,0:T(8,128)(2,1)S(1)} collective-permute-done((bf16[2,1,128,1024]{3,2,1,0:T(8,128)(2,1)S(1)}, bf16[2,1,128,1024]{3,2,1,0:T(8,128)(2,1)S(1)}, u32[]{:S(2)}, u32[]{:S(2)}) %collective-permute-start.23) | collective-permute-done | bytes 524320 | tf_op jit(solution)/shard_map/ppermute | solution.py:192
  71.3 1.4 %collective-permute-start.24 = (bf16[2,1,128,1024]{3,2,1,0:T(8,128)(2,1)S(1)}, bf16[2,1,128,1024]{3,2,1,0:T(8,128)(2,1)S(1)}, u32[]{:S(2)}, u32[]{:S(2)}) collective-permute-start(bf16[2,1,128,1024]{3,2,1,0:T(8,128)(2,1)S(1)} %add_convert_fusion.2), channel_id=1, source_target_pairs={{0,2},{1,3},{2,0},{3,1},{4,5},{5,4},{6,7},{7,6},{8,10},{9,11},{10,... | collective-permute-start | bytes 1572872 | tf_op jit(solution)/shard_map/ppermute | solution.py:192
  73.9 5.8 %shard_map.86 = (bf16[2,1,128,1024]{3,2,1,0:T(8,128)(2,1)S(1)}, bf16[2,1,128,1024]{3,2,1,0:T(8,128)(2,1)S(1)}, bf16[2,1,128,1024]{3,2,1,0:T(8,128)(2,1)S(1)}, bf16[2,1,128,1024]{3,2,1,0:T(8,128)(2,1)S(1)}) custom-call(s32[4]{0:T(128)S(1)} %xor_bitcast_fusion.refs_0_, s32[1]{0:T(128)} %bitcast.7.refs_1_, ...), custom_call_target="tpu_custom_call" | custom-call | flops 4831838208 | bytes 4194304 | tf_op jit(solution)/shard_map/pallas_call | solution.py:152
  79.7 2.6 %collective-permute-done.22 = bf16[1,1,128,1024]{3,2,1,0:T(8,128)(2,1)S(1)} collective-permute-done((bf16[1,1,128,1024]{3,2,1,0:T(8,128)(2,1)S(1)}, bf16[1,1,128,1024]{3,2,1,0:T(8,128)(2,1)S(1)}, u32[]{:S(2)}, u32[]{:S(2)}) %collective-permute-start.22) | collective-permute-done | bytes 262176 | tf_op jit(solution)/shard_map/ppermute | solution.py:192
  85.4 1.4 %collective-permute-start.30 = (bf16[2,1,128,1024]{3,2,1,0:T(8,128)(2,1)S(1)}, bf16[2,1,128,1024]{3,2,1,0:T(8,128)(2,1)S(1)}, u32[]{:S(2)}, u32[]{:S(2)}) collective-permute-start(bf16[2,1,128,1024]{3,2,1,0:T(8,128)(2,1)S(1)} %add_convert_fusion.1), channel_id=1, source_target_pairs={{0,2},{1,3},{2,0},{3,1},{4,5},{5,4},{6,7},{7,6},{8,10},{9,11},{10,... | collective-permute-start | bytes 1572872 | tf_op jit(solution)/shard_map/ppermute | solution.py:192
  89.2 7.3 %collective-permute-done.28 = bf16[1,1,128,1024]{3,2,1,0:T(8,128)(2,1)S(1)} collective-permute-done((bf16[1,1,128,1024]{3,2,1,0:T(8,128)(2,1)S(1)}, bf16[1,1,128,1024]{3,2,1,0:T(8,128)(2,1)S(1)}, u32[]{:S(2)}, u32[]{:S(2)}) %collective-permute-start.28) | collective-permute-done | bytes 262176 | tf_op jit(solution)/shard_map/ppermute | solution.py:192
  98.2 1.2 %collective-permute-start.32 = (bf16[1,1,128,1024]{3,2,1,0:T(8,128)(2,1)S(1)}, bf16[1,1,128,1024]{3,2,1,0:T(8,128)(2,1)S(1)}, u32[]{:S(2)}, u32[]{:S(2)}) collective-permute-start(bf16[1,1,128,1024]{3,2,1,0:T(8,128)(2,1)S(1)} %slice.75), channel_id=1, source_target_pairs={{0,1},{1,0},{2,3},{3,2},{4,6},{5,7},{6,4},{7,5},{8,9},{9,8},{10,11... | collective-permute-start | bytes 786440 | tf_op jit(solution)/shard_map/ppermute | solution.py:192
  99.4 2.7 %collective-permute-start.35 = (bf16[128,1024]{1,0:T(8,128)(2,1)S(1)}, bf16[128,1024]{1,0:T(8,128)(2,1)S(1)}, u32[]{:S(2)}, u32[]{:S(2)}) collective-permute-start(bf16[128,1024]{1,0:T(8,128)(2,1)S(1)} %fusion.9), channel_id=1, source_target_pairs={{0,24},{1,25},{2,26},{3,27},{4,28},{5,29},{6,30},{7,31},{8,0},{9,1... | collective-permute-start | bytes 786440 | tf_op jit(solution)/shard_map/ppermute | solution.py:192
  102.1 6.1 %collective-permute-done.34 = bf16[2,1,128,1024]{3,2,1,0:T(8,128)(2,1)S(1)} collective-permute-done((bf16[2,1,128,1024]{3,2,1,0:T(8,128)(2,1)S(1)}, bf16[2,1,128,1024]{3,2,1,0:T(8,128)(2,1)S(1)}, u32[]{:S(2)}, u32[]{:S(2)}) %collective-permute-start.34) | collective-permute-done | bytes 524320 | tf_op jit(solution)/shard_map/ppermute | solution.py:192
  110.1 5.0 %collective-permute-done.36 = bf16[1,1,128,1024]{3,2,1,0:T(8,128)(2,1)S(1)} collective-permute-done((bf16[1,1,128,1024]{3,2,1,0:T(8,128)(2,1)S(1)}, bf16[1,1,128,1024]{3,2,1,0:T(8,128)(2,1)S(1)}, u32[]{:S(2)}, u32[]{:S(2)}) %collective-permute-start.36) | collective-permute-done | bytes 262176 | tf_op jit(solution)/shard_map/ppermute | solution.py:192
  115.1 6.8 %collective-permute-done.37 = bf16[128,1024]{1,0:T(8,128)(2,1)S(1)} collective-permute-done((bf16[128,1024]{1,0:T(8,128)(2,1)S(1)}, bf16[128,1024]{1,0:T(8,128)(2,1)S(1)}, u32[]{:S(2)}, u32[]{:S(2)}) %collective-permute-start.37) | collective-permute-done | bytes 262176 | tf_op jit(solution)/shard_map/ppermute | solution.py:192
  (70 shorter events, 16.3 us)
Async XLA Ops:
  1.9 7.7 %collective-permute-start.2 = (bf16[1,1,136,1024]{3,2,1,0:T(8,128)(2,1)}, bf16[1,1,136,1024]{3,2,1,0:T(8,128)(2,1)S(1)}, u32[]{:S(2)}, u32[]{:S(2)}) collective-permute-start(bf16[1,1,136,1024]{3,2,1,0:T(8,128)(2,1)} %bitcast.28), channel_id=1, source_target_pairs={{0,1},{1,0},{2,3},{3,2},{4,6},{5,7},{6,4},{7,5},{8,9},{9,8},{10,11... | collective-permute-start | bytes 835592 | tf_op jit(solution)/shard_map/ppermute | solution.py:192
  4.8 9.6 %collective-permute-start = (bf16[136,1024]{1,0:T(8,128)(2,1)}, bf16[136,1024]{1,0:T(8,128)(2,1)S(1)}, u32[]{:S(2)}, u32[]{:S(2)}) collective-permute-start(bf16[136,1024]{1,0:T(8,128)(2,1)} %shard_map.82), channel_id=1, source_target_pairs={{0,24},{1,25},{2,26},{3,27},{4,28},{5,29},{6,30},{7,31},{8,0},{9,1... | collective-permute-start | bytes 835592 | tf_op jit(solution)/shard_map/ppermute | solution.py:192
  10.6 13.0 %collective-permute-start.4 = (bf16[2,1,136,1024]{3,2,1,0:T(8,128)(2,1)S(1)}, bf16[2,1,136,1024]{3,2,1,0:T(8,128)(2,1)S(1)}, u32[]{:S(2)}, u32[]{:S(2)}) collective-permute-start(bf16[2,1,136,1024]{3,2,1,0:T(8,128)(2,1)S(1)} %pad_maximum_fusion.refs_2_), channel_id=1, source_target_pairs={{0,4},{1,5},{2,6},{3,7},{4,0},{5,1},{6,2},{7,3},{8,12},{9,13},{10,... | collective-permute-start | bytes 1671176 | tf_op jit(solution)/shard_map/ppermute | solution.py:192
  10.6 12.9 %collective-permute-start.3 = (bf16[2,1,136,1024]{3,2,1,0:T(8,128)(2,1)S(1)}, bf16[2,1,136,1024]{3,2,1,0:T(8,128)(2,1)S(1)}, u32[]{:S(2)}, u32[]{:S(2)}) collective-permute-start(bf16[2,1,136,1024]{3,2,1,0:T(8,128)(2,1)S(1)} %pad_maximum_fusion.refs_2_), channel_id=1, source_target_pairs={{0,2},{1,3},{2,0},{3,1},{4,5},{5,4},{6,7},{7,6},{8,10},{9,11},{10,... | collective-permute-start | bytes 1671176 | tf_op jit(solution)/shard_map/ppermute | solution.py:192
  12.8 10.8 %collective-permute-start.5 = (bf16[136,1024]{1,0:T(8,128)(2,1)}, bf16[136,1024]{1,0:T(8,128)(2,1)S(1)}, u32[]{:S(2)}, u32[]{:S(2)}) collective-permute-start(bf16[136,1024]{1,0:T(8,128)(2,1)} %shard_map.82), channel_id=1, source_target_pairs={{0,8},{1,9},{2,10},{3,11},{4,12},{5,13},{6,14},{7,15},{8,16},{9,17... | collective-permute-start | bytes 835592 | tf_op jit(solution)/shard_map/ppermute | solution.py:192
  14.4 9.1 %collective-permute-start.1 = (bf16[1,1,136,1024]{3,2,1,0:T(8,128)(2,1)S(1)}, bf16[1,1,136,1024]{3,2,1,0:T(8,128)(2,1)S(1)}, u32[]{:S(2)}, u32[]{:S(2)}) collective-permute-start(bf16[1,1,136,1024]{3,2,1,0:T(8,128)(2,1)S(1)} %bitcast.34), channel_id=1, source_target_pairs={{0,1},{1,0},{2,3},{3,2},{4,6},{5,7},{6,4},{7,5},{8,9},{9,8},{10,11... | collective-permute-start | bytes 835592 | tf_op jit(solution)/shard_map/ppermute | solution.py:192
  23.5 6.9 %collective-permute-start.10 = (bf16[2,1,136,1024]{3,2,1,0:T(8,128)(2,1)S(1)}, bf16[2,1,136,1024]{3,2,1,0:T(8,128)(2,1)S(1)}, u32[]{:S(2)}, u32[]{:S(2)}) collective-permute-start(bf16[2,1,136,1024]{3,2,1,0:T(8,128)(2,1)S(1)} %collective-permute-done.3.refs_3_), channel_id=1, source_target_pairs={{0,4},{1,5},{2,6},{3,7},{4,0},{5,1},{6,2},{7,3},{8,12},{9,13},{10,... | collective-permute-start | bytes 1671176 | tf_op jit(solution)/shard_map/ppermute | solution.py:192
  23.6 16.4 %collective-permute-start.9 = (bf16[136,1024]{1,0:T(8,128)(2,1)}, bf16[136,1024]{1,0:T(8,128)(2,1)S(1)}, u32[]{:S(2)}, u32[]{:S(2)}) collective-permute-start(bf16[136,1024]{1,0:T(8,128)(2,1)} %shard_map.82), channel_id=1, source_target_pairs={{0,16},{1,17},{2,18},{3,19},{4,20},{5,21},{6,22},{7,23},{8,24},{9,... | collective-permute-start | bytes 835592 | tf_op jit(solution)/shard_map/ppermute | solution.py:192
  26.4 13.7 %collective-permute-start.8 = (bf16[2,1,136,1024]{3,2,1,0:T(8,128)(2,1)S(1)}, bf16[2,1,136,1024]{3,2,1,0:T(8,128)(2,1)S(1)}, u32[]{:S(2)}, u32[]{:S(2)}) collective-permute-start(bf16[2,1,136,1024]{3,2,1,0:T(8,128)(2,1)S(1)} %pad_maximum_fusion.1.refs_2_), channel_id=1, source_target_pairs={{0,4},{1,5},{2,6},{3,7},{4,0},{5,1},{6,2},{7,3},{8,12},{9,13},{10,... | collective-permute-start | bytes 1671176 | tf_op jit(solution)/shard_map/ppermute | solution.py:192
  26.7 13.4 %collective-permute-start.7 = (bf16[2,1,136,1024]{3,2,1,0:T(8,128)(2,1)S(1)}, bf16[2,1,136,1024]{3,2,1,0:T(8,128)(2,1)S(1)}, u32[]{:S(2)}, u32[]{:S(2)}) collective-permute-start(bf16[2,1,136,1024]{3,2,1,0:T(8,128)(2,1)S(1)} %pad_maximum_fusion.1.refs_2_), channel_id=1, source_target_pairs={{0,2},{1,3},{2,0},{3,1},{4,5},{5,4},{6,7},{7,6},{8,10},{9,11},{10,... | collective-permute-start | bytes 1671176 | tf_op jit(solution)/shard_map/ppermute | solution.py:192
  28.9 11.2 %collective-permute-start.6 = (bf16[1,1,136,1024]{3,2,1,0:T(8,128)(2,1)S(1)}, bf16[1,1,136,1024]{3,2,1,0:T(8,128)(2,1)S(1)}, u32[]{:S(2)}, u32[]{:S(2)}) collective-permute-start(bf16[1,1,136,1024]{3,2,1,0:T(8,128)(2,1)S(1)} %bitcast.32), channel_id=1, source_target_pairs={{0,1},{1,0},{2,3},{3,2},{4,6},{5,7},{6,4},{7,5},{8,9},{9,8},{10,11... | collective-permute-start | bytes 835592 | tf_op jit(solution)/shard_map/ppermute | solution.py:192
  40.1 3.5 %collective-permute-start.15 = (bf16[2,1,136,1024]{3,2,1,0:T(8,128)(2,1)S(1)}, bf16[2,1,136,1024]{3,2,1,0:T(8,128)(2,1)S(1)}, u32[]{:S(2)}, u32[]{:S(2)}) collective-permute-start(bf16[2,1,136,1024]{3,2,1,0:T(8,128)(2,1)S(1)} %collective-permute-done.7.refs_3_), channel_id=1, source_target_pairs={{0,4},{1,5},{2,6},{3,7},{4,0},{5,1},{6,2},{7,3},{8,12},{9,13},{10,... | collective-permute-start | bytes 1671176 | tf_op jit(solution)/shard_map/ppermute | solution.py:192
  40.2 11.5 %collective-permute-start.14 = (bf16[2,1,136,1024]{3,2,1,0:T(8,128)(2,1)S(1)}, bf16[2,1,136,1024]{3,2,1,0:T(8,128)(2,1)S(1)}, u32[]{:S(2)}, u32[]{:S(2)}) collective-permute-start(bf16[2,1,136,1024]{3,2,1,0:T(8,128)(2,1)S(1)} %pad_maximum_fusion.2.refs_2_), channel_id=1, source_target_pairs={{0,4},{1,5},{2,6},{3,7},{4,0},{5,1},{6,2},{7,3},{8,12},{9,13},{10,... | collective-permute-start | bytes 1671176 | tf_op jit(solution)/shard_map/ppermute | solution.py:192
  40.8 12.5 %collective-permute-start.13 = (bf16[2,1,136,1024]{3,2,1,0:T(8,128)(2,1)S(1)}, bf16[2,1,136,1024]{3,2,1,0:T(8,128)(2,1)S(1)}, u32[]{:S(2)}, u32[]{:S(2)}) collective-permute-start(bf16[2,1,136,1024]{3,2,1,0:T(8,128)(2,1)S(1)} %pad_maximum_fusion.2.refs_2_), channel_id=1, source_target_pairs={{0,2},{1,3},{2,0},{3,1},{4,5},{5,4},{6,7},{7,6},{8,10},{9,11},{10,... | collective-permute-start | bytes 1671176 | tf_op jit(solution)/shard_map/ppermute | solution.py:192
  42.1 9.6 %collective-permute-start.12 = (bf16[1,1,136,1024]{3,2,1,0:T(8,128)(2,1)S(1)}, bf16[1,1,136,1024]{3,2,1,0:T(8,128)(2,1)S(1)}, u32[]{:S(2)}, u32[]{:S(2)}) collective-permute-start(bf16[1,1,136,1024]{3,2,1,0:T(8,128)(2,1)S(1)} %bitcast.30), channel_id=1, source_target_pairs={{0,1},{1,0},{2,3},{3,2},{4,6},{5,7},{6,4},{7,5},{8,9},{9,8},{10,11... | collective-permute-start | bytes 835592 | tf_op jit(solution)/shard_map/ppermute | solution.py:192
  53.9 8.9 %collective-permute-start.18 = (bf16[2,1,136,1024]{3,2,1,0:T(8,128)(2,1)S(1)}, bf16[2,1,136,1024]{3,2,1,0:T(8,128)(2,1)S(1)}, u32[]{:S(2)}, u32[]{:S(2)}) collective-permute-start(bf16[2,1,136,1024]{3,2,1,0:T(8,128)(2,1)S(1)} %pad_maximum_fusion.3.refs_2_), channel_id=1, source_target_pairs={{0,4},{1,5},{2,6},{3,7},{4,0},{5,1},{6,2},{7,3},{8,12},{9,13},{10,... | collective-permute-start | bytes 1671176 | tf_op jit(solution)/shard_map/ppermute | solution.py:192
  54.0 9.6 %collective-permute-start.17 = (bf16[2,1,136,1024]{3,2,1,0:T(8,128)(2,1)S(1)}, bf16[2,1,136,1024]{3,2,1,0:T(8,128)(2,1)S(1)}, u32[]{:S(2)}, u32[]{:S(2)}) collective-permute-start(bf16[2,1,136,1024]{3,2,1,0:T(8,128)(2,1)S(1)} %pad_maximum_fusion.3.refs_2_), channel_id=1, source_target_pairs={{0,2},{1,3},{2,0},{3,1},{4,5},{5,4},{6,7},{7,6},{8,10},{9,11},{10,... | collective-permute-start | bytes 1671176 | tf_op jit(solution)/shard_map/ppermute | solution.py:192
  55.6 13.6 %collective-permute-start.20 = (bf16[2,1,128,1024]{3,2,1,0:T(8,128)(2,1)S(1)}, bf16[2,1,128,1024]{3,2,1,0:T(8,128)(2,1)S(1)}, u32[]{:S(2)}, u32[]{:S(2)}) collective-permute-start(bf16[2,1,128,1024]{3,2,1,0:T(8,128)(2,1)S(1)} %add_convert_fusion.3), channel_id=1, source_target_pairs={{0,2},{1,3},{2,0},{3,1},{4,5},{5,4},{6,7},{7,6},{8,10},{9,11},{10,... | collective-permute-start | bytes 1572872 | tf_op jit(solution)/shard_map/ppermute | solution.py:192
  69.7 4.2 %collective-permute-start.25 = (bf16[2,1,136,1024]{3,2,1,0:T(8,128)(2,1)S(1)}, bf16[2,1,136,1024]{3,2,1,0:T(8,128)(2,1)S(1)}, u32[]{:S(2)}, u32[]{:S(2)}) collective-permute-start(bf16[2,1,136,1024]{3,2,1,0:T(8,128)(2,1)S(1)} %collective-permute-done.17.refs_3_), channel_id=1, source_target_pairs={{0,4},{1,5},{2,6},{3,7},{4,0},{5,1},{6,2},{7,3},{8,12},{9,13},{10,... | collective-permute-start | bytes 1671176 | tf_op jit(solution)/shard_map/ppermute | solution.py:192
  71.3 12.1 %collective-permute-start.24 = (bf16[2,1,128,1024]{3,2,1,0:T(8,128)(2,1)S(1)}, bf16[2,1,128,1024]{3,2,1,0:T(8,128)(2,1)S(1)}, u32[]{:S(2)}, u32[]{:S(2)}) collective-permute-start(bf16[2,1,128,1024]{3,2,1,0:T(8,128)(2,1)S(1)} %add_convert_fusion.2), channel_id=1, source_target_pairs={{0,2},{1,3},{2,0},{3,1},{4,5},{5,4},{6,7},{7,6},{8,10},{9,11},{10,... | collective-permute-start | bytes 1572872 | tf_op jit(solution)/shard_map/ppermute | solution.py:192
  73.0 9.3 %collective-permute-start.22 = (bf16[1,1,128,1024]{3,2,1,0:T(8,128)(2,1)S(1)}, bf16[1,1,128,1024]{3,2,1,0:T(8,128)(2,1)S(1)}, u32[]{:S(2)}, u32[]{:S(2)}) collective-permute-start(bf16[1,1,128,1024]{3,2,1,0:T(8,128)(2,1)S(1)} %slice.77), channel_id=1, source_target_pairs={{0,1},{1,0},{2,3},{3,2},{4,6},{5,7},{6,4},{7,5},{8,9},{9,8},{10,11... | collective-permute-start | bytes 786440 | tf_op jit(solution)/shard_map/ppermute | solution.py:192
  83.8 24.5 %collective-permute-start.11 = (bf16[2,1,128,1024]{3,2,1,0:T(8,128)(2,1)S(1)}, bf16[2,1,128,1024]{3,2,1,0:T(8,128)(2,1)S(1)}, u32[]{:S(2)}, u32[]{:S(2)}) collective-permute-start(bf16[2,1,128,1024]{3,2,1,0:T(8,128)(2,1)S(1)} %get-tuple-element.71), channel_id=1, source_target_pairs={{0,4},{1,5},{2,6},{3,7},{4,0},{5,1},{6,2},{7,3},{8,12},{9,13},{10,... | collective-permute-start | bytes 1572872 | tf_op jit(solution)/shard_map/ppermute | solution.py:192
  83.9 4.3 %collective-permute-start.33 = (bf16[2,1,128,1024]{3,2,1,0:T(8,128)(2,1)S(1)}, bf16[2,1,128,1024]{3,2,1,0:T(8,128)(2,1)S(1)}, u32[]{:S(2)}, u32[]{:S(2)}) collective-permute-start(bf16[2,1,128,1024]{3,2,1,0:T(8,128)(2,1)S(1)} %get-tuple-element.113), channel_id=1, source_target_pairs={{0,4},{1,5},{2,6},{3,7},{4,0},{5,1},{6,2},{7,3},{8,12},{9,13},{10,... | collective-permute-start | bytes 1572872 | tf_op jit(solution)/shard_map/ppermute | solution.py:192
  84.4 13.4 %collective-permute-start.26 = (bf16[2,1,128,1024]{3,2,1,0:T(8,128)(2,1)S(1)}, bf16[2,1,128,1024]{3,2,1,0:T(8,128)(2,1)S(1)}, u32[]{:S(2)}, u32[]{:S(2)}) collective-permute-start(bf16[2,1,128,1024]{3,2,1,0:T(8,128)(2,1)S(1)} %get-tuple-element.104), channel_id=1, source_target_pairs={{0,4},{1,5},{2,6},{3,7},{4,0},{5,1},{6,2},{7,3},{8,12},{9,13},{10,... | collective-permute-start | bytes 1572872 | tf_op jit(solution)/shard_map/ppermute | solution.py:192
  85.4 12.4 %collective-permute-start.30 = (bf16[2,1,128,1024]{3,2,1,0:T(8,128)(2,1)S(1)}, bf16[2,1,128,1024]{3,2,1,0:T(8,128)(2,1)S(1)}, u32[]{:S(2)}, u32[]{:S(2)}) collective-permute-start(bf16[2,1,128,1024]{3,2,1,0:T(8,128)(2,1)S(1)} %add_convert_fusion.1), channel_id=1, source_target_pairs={{0,2},{1,3},{2,0},{3,1},{4,5},{5,4},{6,7},{7,6},{8,10},{9,11},{10,... | collective-permute-start | bytes 1572872 | tf_op jit(solution)/shard_map/ppermute | solution.py:192
  87.2 9.3 %collective-permute-start.28 = (bf16[1,1,128,1024]{3,2,1,0:T(8,128)(2,1)S(1)}, bf16[1,1,128,1024]{3,2,1,0:T(8,128)(2,1)S(1)}, u32[]{:S(2)}, u32[]{:S(2)}) collective-permute-start(bf16[1,1,128,1024]{3,2,1,0:T(8,128)(2,1)S(1)} %slice.76), channel_id=1, source_target_pairs={{0,1},{1,0},{2,3},{3,2},{4,6},{5,7},{6,4},{7,5},{8,9},{9,8},{10,11... | collective-permute-start | bytes 786440 | tf_op jit(solution)/shard_map/ppermute | solution.py:192
  88.2 9.6 %collective-permute-start.31 = (bf16[128,1024]{1,0:T(8,128)(2,1)S(1)}, bf16[128,1024]{1,0:T(8,128)(2,1)S(1)}, u32[]{:S(2)}, u32[]{:S(2)}) collective-permute-start(bf16[128,1024]{1,0:T(8,128)(2,1)S(1)} %fusion.8), channel_id=1, source_target_pairs={{0,8},{1,9},{2,10},{3,11},{4,12},{5,13},{6,14},{7,15},{8,16},{9,17... | collective-permute-start | bytes 786440 | tf_op jit(solution)/shard_map/ppermute | solution.py:192
  96.5 11.8 %collective-permute-start.34 = (bf16[2,1,128,1024]{3,2,1,0:T(8,128)(2,1)S(1)}, bf16[2,1,128,1024]{3,2,1,0:T(8,128)(2,1)S(1)}, u32[]{:S(2)}, u32[]{:S(2)}) collective-permute-start(bf16[2,1,128,1024]{3,2,1,0:T(8,128)(2,1)S(1)} %add_convert_fusion), channel_id=1, source_target_pairs={{0,2},{1,3},{2,0},{3,1},{4,5},{5,4},{6,7},{7,6},{8,10},{9,11},{10,... | collective-permute-start | bytes 1572872 | tf_op jit(solution)/shard_map/ppermute | solution.py:192
  98.2 10.1 %collective-permute-start.32 = (bf16[1,1,128,1024]{3,2,1,0:T(8,128)(2,1)S(1)}, bf16[1,1,128,1024]{3,2,1,0:T(8,128)(2,1)S(1)}, u32[]{:S(2)}, u32[]{:S(2)}) collective-permute-start(bf16[1,1,128,1024]{3,2,1,0:T(8,128)(2,1)S(1)} %slice.75), channel_id=1, source_target_pairs={{0,1},{1,0},{2,3},{3,2},{4,6},{5,7},{6,4},{7,5},{8,9},{9,8},{10,11... | collective-permute-start | bytes 786440 | tf_op jit(solution)/shard_map/ppermute | solution.py:192
  99.4 8.8 %collective-permute-start.35 = (bf16[128,1024]{1,0:T(8,128)(2,1)S(1)}, bf16[128,1024]{1,0:T(8,128)(2,1)S(1)}, u32[]{:S(2)}, u32[]{:S(2)}) collective-permute-start(bf16[128,1024]{1,0:T(8,128)(2,1)S(1)} %fusion.9), channel_id=1, source_target_pairs={{0,24},{1,25},{2,26},{3,27},{4,28},{5,29},{6,30},{7,31},{8,0},{9,1... | collective-permute-start | bytes 786440 | tf_op jit(solution)/shard_map/ppermute | solution.py:192
  108.6 6.4 %collective-permute-start.36 = (bf16[1,1,128,1024]{3,2,1,0:T(8,128)(2,1)S(1)}, bf16[1,1,128,1024]{3,2,1,0:T(8,128)(2,1)S(1)}, u32[]{:S(2)}, u32[]{:S(2)}) collective-permute-start(bf16[1,1,128,1024]{3,2,1,0:T(8,128)(2,1)S(1)} %slice.74), channel_id=1, source_target_pairs={{0,1},{1,0},{2,3},{3,2},{4,6},{5,7},{6,4},{7,5},{8,9},{9,8},{10,11... | collective-permute-start | bytes 786440 | tf_op jit(solution)/shard_map/ppermute | solution.py:192
  109.6 12.3 %collective-permute-start.37 = (bf16[128,1024]{1,0:T(8,128)(2,1)S(1)}, bf16[128,1024]{1,0:T(8,128)(2,1)S(1)}, u32[]{:S(2)}, u32[]{:S(2)}) collective-permute-start(bf16[128,1024]{1,0:T(8,128)(2,1)S(1)} %fusion.10), channel_id=1, source_target_pairs={{0,16},{1,17},{2,18},{3,19},{4,20},{5,21},{6,22},{7,23},{8,24},{9,... | collective-permute-start | bytes 786440 | tf_op jit(solution)/shard_map/ppermute | solution.py:192
  (6 other events, 16.4 us)

commit v3 on v2

--- a/solution.py
+++ b/solution.py
@@ -17,7 +17,6 @@
 f32 = jnp.float32
 bf16 = jnp.bfloat16
 VMEM = pl.BlockSpec(memory_space=pltpu.VMEM)
-SMEM = pl.BlockSpec(memory_space=pltpu.SMEM)
 
 
 def masks_of(n_tensor):
@@ -61,26 +60,29 @@
 
 
 def expert_kernel(pieces, offsets, block, fetch, *refs):
-    place, first, a0, a1, b0, b1, wg, wu, wd = refs[:9]
-    mine_keep, mine_send, sib_keep, sib_send = refs[9:13]
-    xs, hs = refs[13 + 3 * fetch : 15 + 3 * fetch]
+    a0, a1, b0, b1, wg, wu, wd = refs[:7]
+    mine_keep, mine_send, sib_keep, sib_send = refs[7:11]
+    xs, hs = refs[11 + 3 * fetch : 13 + 3 * fetch]
     half = pieces // 2
     rows = offsets * block
     width = a0.shape[3]
     n_extra = a0.shape[2] - block
     n_exp, hidden = wg.shape[0], wg.shape[1]
     others = [mirror(pieces, j) for j in range(pieces)]
+    group_here, slice_here = lax.axis_index("expert"), lax.axis_index("tensor")
+    masks = masks_of(pieces)
 
     def piece(side, j):
         j = others[j] if side else j
         return ((a0, a1), (b0, b1))[side][j // half], j % half
 
     def columns(j):
-        return pl.ds(pl.multiple_of(place[j] * width, width), width)
+        chunk = slice_here ^ jnp.where(group_here % CORES == 0, spread(masks[0], j), spread(masks[1], j))
+        return pl.ds(pl.multiple_of(chunk * width, width), width)
 
     copies = []
     if fetch:
-        (wg_from, wu_from, wd_from), (wg, wu, wd), sems = (wg, wu, wd), refs[13:16], refs[-1]
+        (wg_from, wu_from, wd_from), (wg, wu, wd), sems = (wg, wu, wd), refs[11:14], refs[-1]
         moves = [(x.at[e], y.at[e]) for e in range(n_exp) for x, y in ((wg_from, wg), (wu_from, wu))]
         moves += [(wd_from.at[:, columns(j)], wd.at[:, columns(j)]) for j in range(pieces)]
         copies = [pltpu.make_async_copy(x, y, sems.at[n]) for n, (x, y) in enumerate(moves)]
@@ -116,7 +118,7 @@
                 tables.append(src[i, o, block:, :].astype(f32))
             scales.append(pick(sum(tables), 0))
             for e in range(n_exp):
-                picked[e].append(pick(tables[0], first[0] + (1 + e)))
+                picked[e].append(pick(tables[0], group_here * n_exp + (1 + e)))
     scale = lax.rsqrt(jnp.concatenate(scales, axis=1) / (pieces * width) + epsilon)
 
     for e in range(n_exp):
@@ -142,7 +144,7 @@
                 (keep if to < half else away)[to % half, o] = out[at : at + block]
 
 
-def run_experts(place, first, a0, a1, b0, b1, weights, block, fetch):
+def run_experts(a0, a1, b0, b1, weights, block, fetch):
     half, offsets, _, width = a0.shape
     pieces = 2 * half
     rows = offsets * block
@@ -152,7 +154,7 @@
     out = pl.pallas_call(
         functools.partial(expert_kernel, pieces, offsets, block, fetch),
         out_shape=[jax.ShapeDtypeStruct((half, offsets, block, width), bf16)] * 4 + held,
-        in_specs=[SMEM] * 2 + [VMEM] * 4 + [pl.BlockSpec(memory_space=pl.ANY) if fetch else VMEM] * 3,
+        in_specs=[VMEM] * 4 + [pl.BlockSpec(memory_space=pl.ANY) if fetch else VMEM] * 3,
         out_specs=[VMEM] * (4 + len(held)),
         scratch_shapes=[
             pltpu.VMEM((2 * rows, pieces * width), bf16),
@@ -165,10 +167,10 @@
             bytes_accessed=8 * rows * pieces * width,
             transcendentals=2 * rows * hidden,
         ),
-    )(place, first, a0, a1, b0, b1, *weights)
+    )(a0, a1, b0, b1, *weights)
     if fetch:
         weights = [pltpu.with_memory_space_constraint(w, pltpu.VMEM) for w in out[4:]]
-    return out[:4], weights
+    return list(out[:4]), weights
 
 
 def body(hidden_in, norm_gain, expert_ids, route_weights, w_gate, w_up, w_down):
@@ -177,8 +179,6 @@
     groups, n_tensor = lax.axis_size("expert"), lax.axis_size("tensor")
     n_z = groups // CORES
     experts_all = exp_local * groups
-    group_here, slice_here = lax.axis_index("expert"), lax.axis_index("tensor")
-    core = group_here % CORES
     masks = masks_of(n_tensor)
     stages = len(masks[0])
 
@@ -209,15 +209,11 @@
         out_specs=VMEM,
     )(hidden_in, norm_gain[None, :], expert_ids.T, route_weights.T)
 
-    chunk = [[spread(masks[c], j) for j in range(n_tensor)] for c in range(CORES)]
-    place = slice_here ^ jnp.array(chunk, jnp.int32)[core]
-    first = (group_here * exp_local).astype(jnp.int32)[None]
-
     weights = [w_gate, w_up, w_down.reshape(-1, w_down.shape[2])]
 
-    near = sorted(range(n_z), key=lambda k: min(k, n_z - k))
     blk, far, blk_sib, out, keep, back = {0: payload[None, None]}, {}, {}, {}, {}, {}
-    tied = range(1, n_z + 2 * stages)
+    passing, still = payload, []
+    tied = range(2, n_z + stages)
 
     def put(store, i, value):
         store[i] = value
@@ -230,16 +226,22 @@
         keep[i] = kept[:half] if s else kept
 
     for r in range(n_z + 2 * stages + 1):
-        moves = []
-        i = r - stages
-        if 0 <= i < n_z:
-            far_sib = core_swap(far[i])
+        short = []
+        moves = [
+            (core_swap(sib_keep), lambda got, i=i: put(keep, i, keep[i] + got.astype(f32))) for i, sib_keep in still
+        ]
+        still = []
+        ready = [r - stages] if 1 <= r - stages < n_z else []
+        if r == stages + 2:
+            ready.append(0)
+        far_sib = [core_swap(far[i]) for i in ready]
         for s in range(stages):
-            if 0 <= r - s < n_z:
-                i = r - s
+            i = r - s
+            if 0 <= i < n_z:
                 got = stage_swap(blk[i], s)
                 if s < stages - 1:
-                    moves.append((got, lambda got, i=i: put(blk, i, jnp.concatenate([blk[i], got], axis=0))))
+                    widen = lambda got, i=i: put(blk, i, jnp.concatenate([blk[i], got], axis=0))
+                    (moves if s else short).append((got, widen))
                 else:
                     moves.append((got, lambda got, i=i: put(far, i, got)))
                     moves.append((core_swap(blk[i]), lambda got, i=i: put(blk_sib, i, got)))
@@ -247,26 +249,41 @@
             i = r - 2 * stages + s
             if 1 <= i <= n_z:
                 i %= n_z
-                moves.append((stage_swap(out[i], s), lambda got, i=i, s=s: summed(i, s, got)))
+                fold = lambda got, i=i, s=s: summed(i, s, got)
+                (moves if s else short).append((stage_swap(out[i], s), fold))
         if r + 1 < n_z:
-            moves.append((shift(payload, -near[r + 1]), lambda got, i=r + 1: put(blk, i, got[None, None])))
+            moves.append((shift(passing, -1), lambda got, i=r + 1: put(blk, i, got[None, None])))
+            passing = moves[-1][0]
         i = r - 2 * stages - 1
         if 1 <= i < n_z:
-            moves.append((shift(keep[i][0, 0].astype(bf16), near[i]), lambda got, i=i: put(back, i, got.astype(f32))))
+            done = keep[i][0, 0]
+            if i > n_z // 2:
+                done = done + back.pop(i - 1)
+            done = shift(done.astype(bf16), -1 if 2 * i >= n_z else i)
+            moves.append((done, lambda got, i=i: put(back, i, got.astype(f32))))
         made = []
-        i = r - stages
-        if 0 <= i < n_z:
-            made, weights = run_experts(place, first, blk[i], far[i], blk_sib[i], far_sib, weights, block, i == 0)
+        for i, sib in zip(ready, far_sib):
+            parts, weights = run_experts(blk[i], far[i], blk_sib[i], sib, weights, block, r == stages + 1)
+            made.append(parts)
+        moves = short + moves
         gots = [got for got, _ in moves]
+        if made:
+            away = [parts[3] for parts in made]
+            gots[: len(short)], away = lax.optimization_barrier((gots[: len(short)], away))
+            made = [parts[:3] + [sib] for parts, sib in zip(made, away)]
+        if r == n_z + stages:
+            gots[: len(short)], out[0] = lax.optimization_barrier((gots[: len(short)], out[0]))
         if r in tied:
-            gots, made = lax.optimization_barrier((gots, made))
+            firm = [parts[:3] for parts in made]
+            gots, firm, far[0] = lax.optimization_barrier((gots, firm, far.get(0)))
+            made = [kept + parts[3:] for kept, parts in zip(firm, made)]
         for got, (_, take) in zip(gots, moves):
             take(got)
-        if made:
-            mine_keep, mine_send, sib_keep, sib_send = made
+        for i, (mine_keep, mine_send, sib_keep, sib_send) in zip(ready, made):
             out[i] = (mine_send.astype(f32) + core_swap(sib_send).astype(f32)).astype(bf16)
-            keep[i] = mine_keep.astype(f32) + core_swap(sib_keep).astype(f32)
-    return sum([back[i] for i in range(1, n_z)], keep[0][0, 0]).astype(bf16)
+            keep[i] = mine_keep.astype(f32)
+            still.append((i, sib_keep))
+    return sum(back.values(), keep[0][0, 0]).astype(bf16)
 
 
 def solution(mesh):

time: 123 us -> 109 us (0.89)
  waiting for transfers between devices: 50.4 us -> 30.1 us
  starting transfers between devices: 38.1 us -> 47.2 us
  Pallas kernels: 29.1 us -> 26.8 us
    ppermute x38, waiting for transfers between devices: 50.4 us -> 30.1 us  [send(): return lax.ppermute(value, AXES, pairs)]
    ppermute x38, starting transfers between devices: 38.1 us -> 47.2 us  [send(): return lax.ppermute(value, AXES, pairs)]
    pallas_call x4, Pallas kernels: 27.2 us -> 24.9 us  [run_experts(): pl.pallas_call(functools.partial(expert_kernel, pieces, offsets, block, f...]
  transfers between devices with their start and end apart: 38 -> 38, of which waited for: 16 -> 12; matrix products, arithmetic and copies ran while one was open for 3% -> 3% of each run, Pallas kernels for 22% -> 23%
where the time goes in v3:
time: 109 us; the launch traced here: 108 us
  starting transfers between devices  47.2 us (43%)
  waiting for transfers between devices  30.1 us (28%)
  Pallas kernels  26.8 us (25%)
  other arithmetic  4.01 us (4%)
    ppermute x38, starting transfers between devices, send(): return lax.ppermute(value, AXES, pairs)  47.2 us
    ppermute x38, waiting for transfers between devices, send(): return lax.ppermute(value, AXES, pairs)  30.1 us
    pallas_call x4, Pallas kernels, run_experts(): pl.pallas_call(functools.partial(expert_kernel, pieces, offsets, block, f...  24.9 us
  transfers between devices with their start and end apart: 38, of which 12 were waited for; matrix products, arithmetic and copies ran while one was open for 3% of the time, Pallas kernels for 23%

profile of v3, /device:TPU:0, one launch (start us, length us, event | category | flops | bytes accessed | tf_op | source)
XLA Modules:
  0.0 108.5 jit_solution(3480669012627535757)
XLA Ops:
  0.0 1.9 %shard_map.73 = bf16[136,1024]{1,0:T(8,128)(2,1)} custom-call(bf16[128,1024]{1,0:T(8,128)(2,1)} %hidden.1, f32[1,1024]{1,0:T(1,128)} %bitcast.35, s32[8,128]{1,0:T(8,128)} %bitcast.36, f32[8,128]{1,0:T(8,128)} %bitcast.37), custom_call_target="tpu_custom_call" | custom-call | tf_op jit(solution)/shard_map/pallas_call | solution.py:205
  1.9 5.0 %collective-permute-start = (bf16[136,1024]{1,0:T(8,128)(2,1)}, bf16[136,1024]{1,0:T(8,128)(2,1)S(1)}, u32[]{:S(2)}, u32[]{:S(2)}) collective-permute-start(bf16[136,1024]{1,0:T(8,128)(2,1)} %shard_map.73), channel_id=1, source_target_pairs={{0,24},{1,25},{2,26},{3,27},{4,28},{5,29},{6,30},{7,31},{8,0},{9,1... | collective-permute-start | bytes 835592 | tf_op jit(solution)/shard_map/ppermute | solution.py:192
  6.9 1.5 %collective-permute-start.7 = (bf16[1,1,136,1024]{3,2,1,0:T(8,128)(2,1)}, bf16[1,1,136,1024]{3,2,1,0:T(8,128)(2,1)S(1)}, u32[]{:S(2)}, u32[]{:S(2)}) collective-permute-start(bf16[1,1,136,1024]{3,2,1,0:T(8,128)(2,1)} %bitcast.27), channel_id=1, source_target_pairs={{0,1},{1,0},{2,3},{3,2},{4,6},{5,7},{6,4},{7,5},{8,9},{9,8},{10,11... | collective-permute-start | bytes 835592 | tf_op jit(solution)/shard_map/ppermute | solution.py:192
  8.4 4.7 %collective-permute-done = bf16[136,1024]{1,0:T(8,128)(2,1)S(1)} collective-permute-done((bf16[136,1024]{1,0:T(8,128)(2,1)}, bf16[136,1024]{1,0:T(8,128)(2,1)S(1)}, u32[]{:S(2)}, u32[]{:S(2)}) %collective-permute-start) | collective-permute-done | bytes 278560 | tf_op jit(solution)/shard_map/ppermute | solution.py:192
  13.2 1.5 %collective-permute-start.3 = (bf16[1,1,136,1024]{3,2,1,0:T(8,128)(2,1)S(1)}, bf16[1,1,136,1024]{3,2,1,0:T(8,128)(2,1)S(1)}, u32[]{:S(2)}, u32[]{:S(2)}) collective-permute-start(bf16[1,1,136,1024]{3,2,1,0:T(8,128)(2,1)S(1)} %bitcast.33), channel_id=1, source_target_pairs={{0,1},{1,0},{2,3},{3,2},{4,6},{5,7},{6,4},{7,5},{8,9},{9,8},{10,11... | collective-permute-start | bytes 835592 | tf_op jit(solution)/shard_map/ppermute | solution.py:192
  14.7 1.0 pad_maximum_fusion.1.refs_0_
  15.7 1.6 %collective-permute-start.8 = (bf16[2,1,136,1024]{3,2,1,0:T(8,128)(2,1)S(1)}, bf16[2,1,136,1024]{3,2,1,0:T(8,128)(2,1)S(1)}, u32[]{:S(2)}, u32[]{:S(2)}) collective-permute-start(bf16[2,1,136,1024]{3,2,1,0:T(8,128)(2,1)S(1)} %pad_maximum_fusion.1.refs_0_), channel_id=1, source_target_pairs={{0,2},{1,3},{2,0},{3,1},{4,5},{5,4},{6,7},{7,6},{8,10},{9,11},{10,... | collective-permute-start | bytes 1671176 | tf_op jit(solution)/shard_map/ppermute | solution.py:192
  17.3 4.2 %collective-permute-start.1 = (bf16[136,1024]{1,0:T(8,128)(2,1)S(1)}, bf16[136,1024]{1,0:T(8,128)(2,1)S(1)}, u32[]{:S(2)}, u32[]{:S(2)}) collective-permute-start(bf16[136,1024]{1,0:T(8,128)(2,1)S(1)} %collective-permute-done), channel_id=1, source_target_pairs={{0,24},{1,25},{2,26},{3,27},{4,28},{5,29},{6,30},{7,31},{8,0},{9,1... | collective-permute-start | bytes 835592 | tf_op jit(solution)/shard_map/ppermute | solution.py:192
  22.4 1.9 %collective-permute-start.4 = (bf16[2,1,136,1024]{3,2,1,0:T(8,128)(2,1)S(1)}, bf16[2,1,136,1024]{3,2,1,0:T(8,128)(2,1)S(1)}, u32[]{:S(2)}, u32[]{:S(2)}) collective-permute-start(bf16[2,1,136,1024]{3,2,1,0:T(8,128)(2,1)S(1)} %pad_maximum_fusion.refs_0_), channel_id=1, source_target_pairs={{0,2},{1,3},{2,0},{3,1},{4,5},{5,4},{6,7},{7,6},{8,10},{9,11},{10,... | collective-permute-start | bytes 1671176 | tf_op jit(solution)/shard_map/ppermute | solution.py:192
  24.3 1.6 %collective-permute-done.1 = bf16[136,1024]{1,0:T(8,128)(2,1)S(1)} collective-permute-done((bf16[136,1024]{1,0:T(8,128)(2,1)S(1)}, bf16[136,1024]{1,0:T(8,128)(2,1)S(1)}, u32[]{:S(2)}, u32[]{:S(2)}) %collective-permute-start.1) | collective-permute-done | bytes 278560 | tf_op jit(solution)/shard_map/ppermute | solution.py:192
  26.4 4.3 %collective-permute-start.6 = (bf16[136,1024]{1,0:T(8,128)(2,1)S(1)}, bf16[136,1024]{1,0:T(8,128)(2,1)S(1)}, u32[]{:S(2)}, u32[]{:S(2)}) collective-permute-start(bf16[136,1024]{1,0:T(8,128)(2,1)S(1)} %collective-permute-done.1), channel_id=1, source_target_pairs={{0,24},{1,25},{2,26},{3,27},{4,28},{5,29},{6,30},{7,31},{8,0},{9,1... | collective-permute-start | bytes 835592 | tf_op jit(solution)/shard_map/ppermute | solution.py:192
  30.7 3.9 %collective-permute-done.2 = bf16[1,1,136,1024]{3,2,1,0:T(8,128)(2,1)S(1)} collective-permute-done((bf16[1,1,136,1024]{3,2,1,0:T(8,128)(2,1)S(1)}, bf16[1,1,136,1024]{3,2,1,0:T(8,128)(2,1)S(1)}, u32[]{:S(2)}, u32[]{:S(2)}) %collective-permute-start.2) | collective-permute-done | bytes 278560 | tf_op jit(solution)/shard_map/ppermute | solution.py:192
  35.1 1.8 %collective-permute-start.11 = (bf16[2,1,136,1024]{3,2,1,0:T(8,128)(2,1)S(1)}, bf16[2,1,136,1024]{3,2,1,0:T(8,128)(2,1)S(1)}, u32[]{:S(2)}, u32[]{:S(2)}) collective-permute-start(bf16[2,1,136,1024]{3,2,1,0:T(8,128)(2,1)S(1)} %pad_maximum_fusion.2.refs_0_), channel_id=1, source_target_pairs={{0,2},{1,3},{2,0},{3,1},{4,5},{5,4},{6,7},{7,6},{8,10},{9,11},{10,... | collective-permute-start | bytes 1671176 | tf_op jit(solution)/shard_map/ppermute | solution.py:192
  36.9 1.5 %collective-permute-start.9 = (bf16[1,1,136,1024]{3,2,1,0:T(8,128)(2,1)S(1)}, bf16[1,1,136,1024]{3,2,1,0:T(8,128)(2,1)S(1)}, u32[]{:S(2)}, u32[]{:S(2)}) collective-permute-start(bf16[1,1,136,1024]{3,2,1,0:T(8,128)(2,1)S(1)} %bitcast.29), channel_id=1, source_target_pairs={{0,1},{1,0},{2,3},{3,2},{4,6},{5,7},{6,4},{7,5},{8,9},{9,8},{10,11... | collective-permute-start | bytes 835592 | tf_op jit(solution)/shard_map/ppermute | solution.py:192
  38.4 9.1 %shard_map.74 = (bf16[2,1,128,1024]{3,2,1,0:T(8,128)(2,1)S(1)}, bf16[2,1,128,1024]{3,2,1,0:T(8,128)(2,1)S(1)}, bf16[2,1,128,1024]{3,2,1,0:T(8,128)(2,1)S(1)}, bf...) custom-call(bf16[2,1,136,1024]{3,2,1,0:T(8,128)(2,1)S(1)} %pad_maxim, ...), custom_call_target="tpu_custom_call" | custom-call | flops 4831838208 | bytes 4194304 | tf_op jit(solution)/shard_map/pallas_call | solution.py:154
  48.3 1.3 %collective-permute-start.14 = (bf16[2,1,136,1024]{3,2,1,0:T(8,128)(2,1)S(1)}, bf16[2,1,136,1024]{3,2,1,0:T(8,128)(2,1)S(1)}, u32[]{:S(2)}, u32[]{:S(2)}) collective-permute-start(bf16[2,1,136,1024]{3,2,1,0:T(8,128)(2,1)S(1)} %pad_maximum_fusion.3.refs_0_), channel_id=1, source_target_pairs={{0,2},{1,3},{2,0},{3,1},{4,5},{5,4},{6,7},{7,6},{8,10},{9,11},{10,... | collective-permute-start | bytes 1671176 | tf_op jit(solution)/shard_map/ppermute | solution.py:192
  51.9 5.2 %shard_map.76 = (bf16[2,1,128,1024]{3,2,1,0:T(8,128)(2,1)S(1)}, bf16[2,1,128,1024]{3,2,1,0:T(8,128)(2,1)S(1)}, bf16[2,1,128,1024]{3,2,1,0:T(8,128)(2,1)S(1)}, bf16[2,1,128,1024]{3,2,1,0:T(8,128)(2,1)S(1)}) custom-call(bf16[2,1,136,1024]{3,2,1,0:T(8,128)(2,1)S(1)} %pad_maximum_fusion.1.refs_0_, bf16[2,1,136,1024]{3,2,1,0:T(8,128)(2,1)S(1)} %collective-permute-done.8.refs_1_, ...), custom_call_target="tpu_custom_call" | custom-call | flops 4831838208 | bytes 4194304 | tf_op jit(solution)/shard_map/pallas_call | solution.py:154
  57.2 5.4 %shard_map.75 = (bf16[2,1,128,1024]{3,2,1,0:T(8,128)(2,1)S(1)}, bf16[2,1,128,1024]{3,2,1,0:T(8,128)(2,1)S(1)}, bf16[2,1,128,1024]{3,2,1,0:T(8,128)(2,1)S(1)}, bf16[2,1,128,1024]{3,2,1,0:T(8,128)(2,1)S(1)}) custom-call(bf16[2,1,136,1024]{3,2,1,0:T(8,128)(2,1)S(1)} %pad_maximum_fusion.2.refs_0_, bf16[2,1,136,1024]{3,2,1,0:T(8,128)(2,1)S(1)} %collective-permute-done.11.refs_1_, ...), custom_call_target="tpu_custom_call" | custom-call | flops 4831838208 | bytes 4194304 | tf_op jit(solution)/shard_map/pallas_call | solution.py:154
  63.8 1.2 %collective-permute-start.21 = (bf16[1,1,128,1024]{3,2,1,0:T(8,128)(2,1)S(1)}, bf16[1,1,128,1024]{3,2,1,0:T(8,128)(2,1)S(1)}, u32[]{:S(2)}, u32[]{:S(2)}) collective-permute-start(bf16[1,1,128,1024]{3,2,1,0:T(8,128)(2,1)S(1)} %slice.77), channel_id=1, source_target_pairs={{0,1},{1,0},{2,3},{3,2},{4,6},{5,7},{6,4},{7,5},{8,9},{9,8},{10,11... | collective-permute-start | bytes 786440 | tf_op jit(solution)/shard_map/ppermute | solution.py:192
  65.7 1.5 %collective-permute-start.26 = (bf16[2,1,128,1024]{3,2,1,0:T(8,128)(2,1)S(1)}, bf16[2,1,128,1024]{3,2,1,0:T(8,128)(2,1)S(1)}, u32[]{:S(2)}, u32[]{:S(2)}) collective-permute-start(bf16[2,1,128,1024]{3,2,1,0:T(8,128)(2,1)S(1)} %add_convert_fusion.2), channel_id=1, source_target_pairs={{0,2},{1,3},{2,0},{3,1},{4,5},{5,4},{6,7},{7,6},{8,10},{9,11},{10,... | collective-permute-start | bytes 1572872 | tf_op jit(solution)/shard_map/ppermute | solution.py:192
  67.2 5.2 %shard_map.77 = (bf16[2,1,128,1024]{3,2,1,0:T(8,128)(2,1)S(1)}, bf16[2,1,128,1024]{3,2,1,0:T(8,128)(2,1)S(1)}, bf16[2,1,128,1024]{3,2,1,0:T(8,128)(2,1)S(1)}, bf16[2,1,128,1024]{3,2,1,0:T(8,128)(2,1)S(1)}) custom-call(bf16[2,1,136,1024]{3,2,1,0:T(8,128)(2,1)S(1)} %pad_maximum_fusion.3.refs_0_, bf16[2,1,136,1024]{3,2,1,0:T(8,128)(2,1)S(1)} %collective-permute-done.14.refs_1_, ...), custom_call_target="tpu_custom_call" | custom-call | flops 4831838208 | bytes 4194304 | tf_op jit(solution)/shard_map/pallas_call | solution.py:154
  73.0 2.4 %collective-permute-done.26 = bf16[2,1,128,1024]{3,2,1,0:T(8,128)(2,1)S(1)} collective-permute-done((bf16[2,1,128,1024]{3,2,1,0:T(8,128)(2,1)S(1)}, bf16[2,1,128,1024]{3,2,1,0:T(8,128)(2,1)S(1)}, u32[]{:S(2)}, u32[]{:S(2)}) %collective-permute-start.26) | collective-permute-done | bytes 524320 | tf_op jit(solution)/shard_map/ppermute | solution.py:192
  76.0 1.2 %collective-permute-start.27 = (bf16[1,1,128,1024]{3,2,1,0:T(8,128)(2,1)S(1)}, bf16[1,1,128,1024]{3,2,1,0:T(8,128)(2,1)S(1)}, u32[]{:S(2)}, u32[]{:S(2)}) collective-permute-start(bf16[1,1,128,1024]{3,2,1,0:T(8,128)(2,1)S(1)} %slice.76), channel_id=1, source_target_pairs={{0,1},{1,0},{2,3},{3,2},{4,6},{5,7},{6,4},{7,5},{8,9},{9,8},{10,11... | collective-permute-start | bytes 786440 | tf_op jit(solution)/shard_map/ppermute | solution.py:192
  77.4 1.5 %collective-permute-start.34 = (bf16[2,1,128,1024]{3,2,1,0:T(8,128)(2,1)S(1)}, bf16[2,1,128,1024]{3,2,1,0:T(8,128)(2,1)S(1)}, u32[]{:S(2)}, u32[]{:S(2)}) collective-permute-start(bf16[2,1,128,1024]{3,2,1,0:T(8,128)(2,1)S(1)} %add_convert_fusion), channel_id=1, source_target_pairs={{0,2},{1,3},{2,0},{3,1},{4,5},{5,4},{6,7},{7,6},{8,10},{9,11},{10,... | collective-permute-start | bytes 1572872 | tf_op jit(solution)/shard_map/ppermute | solution.py:192
  79.5 5.3 %collective-permute-done.27 = bf16[1,1,128,1024]{3,2,1,0:T(8,128)(2,1)S(1)} collective-permute-done((bf16[1,1,128,1024]{3,2,1,0:T(8,128)(2,1)S(1)}, bf16[1,1,128,1024]{3,2,1,0:T(8,128)(2,1)S(1)}, u32[]{:S(2)}, u32[]{:S(2)}) %collective-permute-start.27) | collective-permute-done | bytes 262176 | tf_op jit(solution)/shard_map/ppermute | solution.py:192
  84.8 1.7 %collective-permute-start.29 = (bf16[2,1,128,1024]{3,2,1,0:T(8,128)(2,1)S(1)}, bf16[2,1,128,1024]{3,2,1,0:T(8,128)(2,1)S(1)}, u32[]{:S(2)}, u32[]{:S(2)}) collective-permute-start(bf16[2,1,128,1024]{3,2,1,0:T(8,128)(2,1)S(1)} %add_convert_fusion.1), channel_id=1, source_target_pairs={{0,2},{1,3},{2,0},{3,1},{4,5},{5,4},{6,7},{7,6},{8,10},{9,11},{10,... | collective-permute-start | bytes 1572872 | tf_op jit(solution)/shard_map/ppermute | solution.py:192
  86.5 4.3 %collective-permute-start.36 = (bf16[128,1024]{1,0:T(8,128)(2,1)S(1)}, bf16[128,1024]{1,0:T(8,128)(2,1)S(1)}, u32[]{:S(2)}, u32[]{:S(2)}) collective-permute-start(bf16[128,1024]{1,0:T(8,128)(2,1)S(1)} %fusion.10), channel_id=1, source_target_pairs={{0,24},{1,25},{2,26},{3,27},{4,28},{5,29},{6,30},{7,31},{8,0},{9,1... | collective-permute-start | bytes 786440 | tf_op jit(solution)/shard_map/ppermute | solution.py:192
  91.2 1.4 %collective-permute-start.35 = (bf16[1,1,128,1024]{3,2,1,0:T(8,128)(2,1)S(1)}, bf16[1,1,128,1024]{3,2,1,0:T(8,128)(2,1)S(1)}, u32[]{:S(2)}, u32[]{:S(2)}) collective-permute-start(bf16[1,1,128,1024]{3,2,1,0:T(8,128)(2,1)S(1)} %slice.74), channel_id=1, source_target_pairs={{0,1},{1,0},{2,3},{3,2},{4,6},{5,7},{6,4},{7,5},{8,9},{9,8},{10,11... | collective-permute-start | bytes 786440 | tf_op jit(solution)/shard_map/ppermute | solution.py:192
  92.6 4.2 %collective-permute-done.29 = bf16[2,1,128,1024]{3,2,1,0:T(8,128)(2,1)S(1)} collective-permute-done((bf16[2,1,128,1024]{3,2,1,0:T(8,128)(2,1)S(1)}, bf16[2,1,128,1024]{3,2,1,0:T(8,128)(2,1)S(1)}, u32[]{:S(2)}, u32[]{:S(2)}) %collective-permute-start.29) | collective-permute-done | bytes 524320 | tf_op jit(solution)/shard_map/ppermute | solution.py:192
  97.1 1.3 %collective-permute-start.30 = (bf16[1,1,128,1024]{3,2,1,0:T(8,128)(2,1)S(1)}, bf16[1,1,128,1024]{3,2,1,0:T(8,128)(2,1)S(1)}, u32[]{:S(2)}, u32[]{:S(2)}) collective-permute-start(bf16[1,1,128,1024]{3,2,1,0:T(8,128)(2,1)S(1)} %slice.75), channel_id=1, source_target_pairs={{0,1},{1,0},{2,3},{3,2},{4,6},{5,7},{6,4},{7,5},{8,9},{9,8},{10,11... | collective-permute-start | bytes 786440 | tf_op jit(solution)/shard_map/ppermute | solution.py:192
  98.5 4.1 %collective-permute-start.37 = (bf16[128,1024]{1,0:T(8,128)(2,1)S(1)}, bf16[128,1024]{1,0:T(8,128)(2,1)S(1)}, u32[]{:S(2)}, u32[]{:S(2)}) collective-permute-start(bf16[128,1024]{1,0:T(8,128)(2,1)S(1)} %fusion.3), channel_id=1, source_target_pairs={{0,24},{1,25},{2,26},{3,27},{4,28},{5,29},{6,30},{7,31},{8,0},{9,1... | collective-permute-start | bytes 786440 | tf_op jit(solution)/shard_map/ppermute | solution.py:192
  103.5 4.1 %collective-permute-done.37 = bf16[128,1024]{1,0:T(8,128)(2,1)S(1)} collective-permute-done((bf16[128,1024]{1,0:T(8,128)(2,1)S(1)}, bf16[128,1024]{1,0:T(8,128)(2,1)S(1)}, u32[]{:S(2)}, u32[]{:S(2)}) %collective-permute-start.37) | collective-permute-done | bytes 262176 | tf_op jit(solution)/shard_map/ppermute | solution.py:192
  (69 shorter events, 11.4 us)
Async XLA Ops:
  1.9 11.3 %collective-permute-start = (bf16[136,1024]{1,0:T(8,128)(2,1)}, bf16[136,1024]{1,0:T(8,128)(2,1)S(1)}, u32[]{:S(2)}, u32[]{:S(2)}) collective-permute-start(bf16[136,1024]{1,0:T(8,128)(2,1)} %shard_map.73), channel_id=1, source_target_pairs={{0,24},{1,25},{2,26},{3,27},{4,28},{5,29},{6,30},{7,31},{8,0},{9,1... | collective-permute-start | bytes 835592 | tf_op jit(solution)/shard_map/ppermute | solution.py:192
  6.9 7.7 %collective-permute-start.7 = (bf16[1,1,136,1024]{3,2,1,0:T(8,128)(2,1)}, bf16[1,1,136,1024]{3,2,1,0:T(8,128)(2,1)S(1)}, u32[]{:S(2)}, u32[]{:S(2)}) collective-permute-start(bf16[1,1,136,1024]{3,2,1,0:T(8,128)(2,1)} %bitcast.27), channel_id=1, source_target_pairs={{0,1},{1,0},{2,3},{3,2},{4,6},{5,7},{6,4},{7,5},{8,9},{9,8},{10,11... | collective-permute-start | bytes 835592 | tf_op jit(solution)/shard_map/ppermute | solution.py:192
  13.2 9.2 %collective-permute-start.3 = (bf16[1,1,136,1024]{3,2,1,0:T(8,128)(2,1)S(1)}, bf16[1,1,136,1024]{3,2,1,0:T(8,128)(2,1)S(1)}, u32[]{:S(2)}, u32[]{:S(2)}) collective-permute-start(bf16[1,1,136,1024]{3,2,1,0:T(8,128)(2,1)S(1)} %bitcast.33), channel_id=1, source_target_pairs={{0,1},{1,0},{2,3},{3,2},{4,6},{5,7},{6,4},{7,5},{8,9},{9,8},{10,11... | collective-permute-start | bytes 835592 | tf_op jit(solution)/shard_map/ppermute | solution.py:192
  15.7 15.1 %collective-permute-start.8 = (bf16[2,1,136,1024]{3,2,1,0:T(8,128)(2,1)S(1)}, bf16[2,1,136,1024]{3,2,1,0:T(8,128)(2,1)S(1)}, u32[]{:S(2)}, u32[]{:S(2)}) collective-permute-start(bf16[2,1,136,1024]{3,2,1,0:T(8,128)(2,1)S(1)} %pad_maximum_fusion.1.refs_0_), channel_id=1, source_target_pairs={{0,2},{1,3},{2,0},{3,1},{4,5},{5,4},{6,7},{7,6},{8,10},{9,11},{10,... | collective-permute-start | bytes 1671176 | tf_op jit(solution)/shard_map/ppermute | solution.py:192
  17.3 8.7 %collective-permute-start.1 = (bf16[136,1024]{1,0:T(8,128)(2,1)S(1)}, bf16[136,1024]{1,0:T(8,128)(2,1)S(1)}, u32[]{:S(2)}, u32[]{:S(2)}) collective-permute-start(bf16[136,1024]{1,0:T(8,128)(2,1)S(1)} %collective-permute-done), channel_id=1, source_target_pairs={{0,24},{1,25},{2,26},{3,27},{4,28},{5,29},{6,30},{7,31},{8,0},{9,1... | collective-permute-start | bytes 835592 | tf_op jit(solution)/shard_map/ppermute | solution.py:192
  22.4 12.6 %collective-permute-start.4 = (bf16[2,1,136,1024]{3,2,1,0:T(8,128)(2,1)S(1)}, bf16[2,1,136,1024]{3,2,1,0:T(8,128)(2,1)S(1)}, u32[]{:S(2)}, u32[]{:S(2)}) collective-permute-start(bf16[2,1,136,1024]{3,2,1,0:T(8,128)(2,1)S(1)} %pad_maximum_fusion.refs_0_), channel_id=1, source_target_pairs={{0,2},{1,3},{2,0},{3,1},{4,5},{5,4},{6,7},{7,6},{8,10},{9,11},{10,... | collective-permute-start | bytes 1671176 | tf_op jit(solution)/shard_map/ppermute | solution.py:192
  24.3 10.8 %collective-permute-start.5 = (bf16[2,1,136,1024]{3,2,1,0:T(8,128)(2,1)S(1)}, bf16[2,1,136,1024]{3,2,1,0:T(8,128)(2,1)S(1)}, u32[]{:S(2)}, u32[]{:S(2)}) collective-permute-start(bf16[2,1,136,1024]{3,2,1,0:T(8,128)(2,1)S(1)} %pad_maximum_fusion.refs_0_), channel_id=1, source_target_pairs={{0,4},{1,5},{2,6},{3,7},{4,0},{5,1},{6,2},{7,3},{8,12},{9,13},{10,... | collective-permute-start | bytes 1671176 | tf_op jit(solution)/shard_map/ppermute | solution.py:192
  25.9 8.7 %collective-permute-start.2 = (bf16[1,1,136,1024]{3,2,1,0:T(8,128)(2,1)S(1)}, bf16[1,1,136,1024]{3,2,1,0:T(8,128)(2,1)S(1)}, u32[]{:S(2)}, u32[]{:S(2)}) collective-permute-start(bf16[1,1,136,1024]{3,2,1,0:T(8,128)(2,1)S(1)} %bitcast.31), channel_id=1, source_target_pairs={{0,1},{1,0},{2,3},{3,2},{4,6},{5,7},{6,4},{7,5},{8,9},{9,8},{10,11... | collective-permute-start | bytes 835592 | tf_op jit(solution)/shard_map/ppermute | solution.py:192
  26.4 8.6 %collective-permute-start.6 = (bf16[136,1024]{1,0:T(8,128)(2,1)S(1)}, bf16[136,1024]{1,0:T(8,128)(2,1)S(1)}, u32[]{:S(2)}, u32[]{:S(2)}) collective-permute-start(bf16[136,1024]{1,0:T(8,128)(2,1)S(1)} %collective-permute-done.1), channel_id=1, source_target_pairs={{0,24},{1,25},{2,26},{3,27},{4,28},{5,29},{6,30},{7,31},{8,0},{9,1... | collective-permute-start | bytes 835592 | tf_op jit(solution)/shard_map/ppermute | solution.py:192
  35.1 13.0 %collective-permute-start.11 = (bf16[2,1,136,1024]{3,2,1,0:T(8,128)(2,1)S(1)}, bf16[2,1,136,1024]{3,2,1,0:T(8,128)(2,1)S(1)}, u32[]{:S(2)}, u32[]{:S(2)}) collective-permute-start(bf16[2,1,136,1024]{3,2,1,0:T(8,128)(2,1)S(1)} %pad_maximum_fusion.2.refs_0_), channel_id=1, source_target_pairs={{0,2},{1,3},{2,0},{3,1},{4,5},{5,4},{6,7},{7,6},{8,10},{9,11},{10,... | collective-permute-start | bytes 1671176 | tf_op jit(solution)/shard_map/ppermute | solution.py:192
  36.9 11.2 %collective-permute-start.12 = (bf16[2,1,136,1024]{3,2,1,0:T(8,128)(2,1)S(1)}, bf16[2,1,136,1024]{3,2,1,0:T(8,128)(2,1)S(1)}, u32[]{:S(2)}, u32[]{:S(2)}) collective-permute-start(bf16[2,1,136,1024]{3,2,1,0:T(8,128)(2,1)S(1)} %pad_maximum_fusion.2.refs_0_), channel_id=1, source_target_pairs={{0,4},{1,5},{2,6},{3,7},{4,0},{5,1},{6,2},{7,3},{8,12},{9,13},{10,... | collective-permute-start | bytes 1671176 | tf_op jit(solution)/shard_map/ppermute | solution.py:192
  36.9 10.6 %collective-permute-start.9 = (bf16[1,1,136,1024]{3,2,1,0:T(8,128)(2,1)S(1)}, bf16[1,1,136,1024]{3,2,1,0:T(8,128)(2,1)S(1)}, u32[]{:S(2)}, u32[]{:S(2)}) collective-permute-start(bf16[1,1,136,1024]{3,2,1,0:T(8,128)(2,1)S(1)} %bitcast.29), channel_id=1, source_target_pairs={{0,1},{1,0},{2,3},{3,2},{4,6},{5,7},{6,4},{7,5},{8,9},{9,8},{10,11... | collective-permute-start | bytes 835592 | tf_op jit(solution)/shard_map/ppermute | solution.py:192
  48.3 14.4 %collective-permute-start.14 = (bf16[2,1,136,1024]{3,2,1,0:T(8,128)(2,1)S(1)}, bf16[2,1,136,1024]{3,2,1,0:T(8,128)(2,1)S(1)}, u32[]{:S(2)}, u32[]{:S(2)}) collective-permute-start(bf16[2,1,136,1024]{3,2,1,0:T(8,128)(2,1)S(1)} %pad_maximum_fusion.3.refs_0_), channel_id=1, source_target_pairs={{0,2},{1,3},{2,0},{3,1},{4,5},{5,4},{6,7},{7,6},{8,10},{9,11},{10,... | collective-permute-start | bytes 1671176 | tf_op jit(solution)/shard_map/ppermute | solution.py:192
  49.6 13.1 %collective-permute-start.15 = (bf16[2,1,136,1024]{3,2,1,0:T(8,128)(2,1)S(1)}, bf16[2,1,136,1024]{3,2,1,0:T(8,128)(2,1)S(1)}, u32[]{:S(2)}, u32[]{:S(2)}) collective-permute-start(bf16[2,1,136,1024]{3,2,1,0:T(8,128)(2,1)S(1)} %pad_maximum_fusion.3.refs_0_), channel_id=1, source_target_pairs={{0,4},{1,5},{2,6},{3,7},{4,0},{5,1},{6,2},{7,3},{8,12},{9,13},{10,... | collective-permute-start | bytes 1671176 | tf_op jit(solution)/shard_map/ppermute | solution.py:192
  49.6 7.6 %collective-permute-start.18 = (bf16[2,1,136,1024]{3,2,1,0:T(8,128)(2,1)S(1)}, bf16[2,1,136,1024]{3,2,1,0:T(8,128)(2,1)S(1)}, u32[]{:S(2)}, u32[]{:S(2)}) collective-permute-start(bf16[2,1,136,1024]{3,2,1,0:T(8,128)(2,1)S(1)} %collective-permute-done.11.refs_1_), channel_id=1, source_target_pairs={{0,4},{1,5},{2,6},{3,7},{4,0},{5,1},{6,2},{7,3},{8,12},{9,13},{10,... | collective-permute-start | bytes 1671176 | tf_op jit(solution)/shard_map/ppermute | solution.py:192
  50.3 12.3 %collective-permute-start.13 = (bf16[2,1,128,1024]{3,2,1,0:T(8,128)(2,1)S(1)}, bf16[2,1,128,1024]{3,2,1,0:T(8,128)(2,1)S(1)}, u32[]{:S(2)}, u32[]{:S(2)}) collective-permute-start(bf16[2,1,128,1024]{3,2,1,0:T(8,128)(2,1)S(1)} %get-tuple-element.71), channel_id=1, source_target_pairs={{0,4},{1,5},{2,6},{3,7},{4,0},{5,1},{6,2},{7,3},{8,12},{9,13},{10,... | collective-permute-start | bytes 1572872 | tf_op jit(solution)/shard_map/ppermute | solution.py:192
  51.1 12.4 %collective-permute-start.17 = (bf16[2,1,128,1024]{3,2,1,0:T(8,128)(2,1)S(1)}, bf16[2,1,128,1024]{3,2,1,0:T(8,128)(2,1)S(1)}, u32[]{:S(2)}, u32[]{:S(2)}) collective-permute-start(bf16[2,1,128,1024]{3,2,1,0:T(8,128)(2,1)S(1)} %add_convert_fusion.3), channel_id=1, source_target_pairs={{0,2},{1,3},{2,0},{3,1},{4,5},{5,4},{6,7},{7,6},{8,10},{9,11},{10,... | collective-permute-start | bytes 1572872 | tf_op jit(solution)/shard_map/ppermute | solution.py:192
  63.8 8.6 %collective-permute-start.21 = (bf16[1,1,128,1024]{3,2,1,0:T(8,128)(2,1)S(1)}, bf16[1,1,128,1024]{3,2,1,0:T(8,128)(2,1)S(1)}, u32[]{:S(2)}, u32[]{:S(2)}) collective-permute-start(bf16[1,1,128,1024]{3,2,1,0:T(8,128)(2,1)S(1)} %slice.77), channel_id=1, source_target_pairs={{0,1},{1,0},{2,3},{3,2},{4,6},{5,7},{6,4},{7,5},{8,9},{9,8},{10,11... | collective-permute-start | bytes 786440 | tf_op jit(solution)/shard_map/ppermute | solution.py:192
  65.0 8.0 %collective-permute-start.23 = (bf16[2,1,128,1024]{3,2,1,0:T(8,128)(2,1)S(1)}, bf16[2,1,128,1024]{3,2,1,0:T(8,128)(2,1)S(1)}, u32[]{:S(2)}, u32[]{:S(2)}) collective-permute-start(bf16[2,1,128,1024]{3,2,1,0:T(8,128)(2,1)S(1)} %get-tuple-element.95), channel_id=1, source_target_pairs={{0,4},{1,5},{2,6},{3,7},{4,0},{5,1},{6,2},{7,3},{8,12},{9,13},{10,... | collective-permute-start | bytes 1572872 | tf_op jit(solution)/shard_map/ppermute | solution.py:192
  65.3 7.7 %collective-permute-start.24 = (bf16[2,1,128,1024]{3,2,1,0:T(8,128)(2,1)S(1)}, bf16[2,1,128,1024]{3,2,1,0:T(8,128)(2,1)S(1)}, u32[]{:S(2)}, u32[]{:S(2)}) collective-permute-start(bf16[2,1,128,1024]{3,2,1,0:T(8,128)(2,1)S(1)} %get-tuple-element.96), channel_id=1, source_target_pairs={{0,4},{1,5},{2,6},{3,7},{4,0},{5,1},{6,2},{7,3},{8,12},{9,13},{10,... | collective-permute-start | bytes 1572872 | tf_op jit(solution)/shard_map/ppermute | solution.py:192
  65.7 9.6 %collective-permute-start.26 = (bf16[2,1,128,1024]{3,2,1,0:T(8,128)(2,1)S(1)}, bf16[2,1,128,1024]{3,2,1,0:T(8,128)(2,1)S(1)}, u32[]{:S(2)}, u32[]{:S(2)}) collective-permute-start(bf16[2,1,128,1024]{3,2,1,0:T(8,128)(2,1)S(1)} %add_convert_fusion.2), channel_id=1, source_target_pairs={{0,2},{1,3},{2,0},{3,1},{4,5},{5,4},{6,7},{7,6},{8,10},{9,11},{10,... | collective-permute-start | bytes 1572872 | tf_op jit(solution)/shard_map/ppermute | solution.py:192
  72.4 4.8 %collective-permute-start.33 = (bf16[2,1,128,1024]{3,2,1,0:T(8,128)(2,1)S(1)}, bf16[2,1,128,1024]{3,2,1,0:T(8,128)(2,1)S(1)}, u32[]{:S(2)}, u32[]{:S(2)}) collective-permute-start(bf16[2,1,128,1024]{3,2,1,0:T(8,128)(2,1)S(1)} %get-tuple-element.115), channel_id=1, source_target_pairs={{0,4},{1,5},{2,6},{3,7},{4,0},{5,1},{6,2},{7,3},{8,12},{9,13},{10,... | collective-permute-start | bytes 1572872 | tf_op jit(solution)/shard_map/ppermute | solution.py:192
  72.5 6.4 %collective-permute-start.28 = (bf16[2,1,128,1024]{3,2,1,0:T(8,128)(2,1)S(1)}, bf16[2,1,128,1024]{3,2,1,0:T(8,128)(2,1)S(1)}, u32[]{:S(2)}, u32[]{:S(2)}) collective-permute-start(bf16[2,1,128,1024]{3,2,1,0:T(8,128)(2,1)S(1)} %get-tuple-element.109), channel_id=1, source_target_pairs={{0,4},{1,5},{2,6},{3,7},{4,0},{5,1},{6,2},{7,3},{8,12},{9,13},{10,... | collective-permute-start | bytes 1572872 | tf_op jit(solution)/shard_map/ppermute | solution.py:192
  75.4 15.5 %collective-permute-start.32 = (bf16[2,1,128,1024]{3,2,1,0:T(8,128)(2,1)S(1)}, bf16[2,1,128,1024]{3,2,1,0:T(8,128)(2,1)S(1)}, u32[]{:S(2)}, u32[]{:S(2)}) collective-permute-start(bf16[2,1,128,1024]{3,2,1,0:T(8,128)(2,1)S(1)} %get-tuple-element.113), channel_id=1, source_target_pairs={{0,4},{1,5},{2,6},{3,7},{4,0},{5,1},{6,2},{7,3},{8,12},{9,13},{10,... | collective-permute-start | bytes 1572872 | tf_op jit(solution)/shard_map/ppermute | solution.py:192
  76.0 8.8 %collective-permute-start.27 = (bf16[1,1,128,1024]{3,2,1,0:T(8,128)(2,1)S(1)}, bf16[1,1,128,1024]{3,2,1,0:T(8,128)(2,1)S(1)}, u32[]{:S(2)}, u32[]{:S(2)}) collective-permute-start(bf16[1,1,128,1024]{3,2,1,0:T(8,128)(2,1)S(1)} %slice.76), channel_id=1, source_target_pairs={{0,1},{1,0},{2,3},{3,2},{4,6},{5,7},{6,4},{7,5},{8,9},{9,8},{10,11... | collective-permute-start | bytes 786440 | tf_op jit(solution)/shard_map/ppermute | solution.py:192
  77.4 13.4 %collective-permute-start.34 = (bf16[2,1,128,1024]{3,2,1,0:T(8,128)(2,1)S(1)}, bf16[2,1,128,1024]{3,2,1,0:T(8,128)(2,1)S(1)}, u32[]{:S(2)}, u32[]{:S(2)}) collective-permute-start(bf16[2,1,128,1024]{3,2,1,0:T(8,128)(2,1)S(1)} %add_convert_fusion), channel_id=1, source_target_pairs={{0,2},{1,3},{2,0},{3,1},{4,5},{5,4},{6,7},{7,6},{8,10},{9,11},{10,... | collective-permute-start | bytes 1572872 | tf_op jit(solution)/shard_map/ppermute | solution.py:192
  79.1 23.4 %collective-permute-start.31 = (bf16[128,1024]{1,0:T(8,128)(2,1)S(1)}, bf16[128,1024]{1,0:T(8,128)(2,1)S(1)}, u32[]{:S(2)}, u32[]{:S(2)}) collective-permute-start(bf16[128,1024]{1,0:T(8,128)(2,1)S(1)} %fusion.9), channel_id=1, source_target_pairs={{0,8},{1,9},{2,10},{3,11},{4,12},{5,13},{6,14},{7,15},{8,16},{9,17... | collective-permute-start | bytes 786440 | tf_op jit(solution)/shard_map/ppermute | solution.py:192
  84.8 12.0 %collective-permute-start.29 = (bf16[2,1,128,1024]{3,2,1,0:T(8,128)(2,1)S(1)}, bf16[2,1,128,1024]{3,2,1,0:T(8,128)(2,1)S(1)}, u32[]{:S(2)}, u32[]{:S(2)}) collective-permute-start(bf16[2,1,128,1024]{3,2,1,0:T(8,128)(2,1)S(1)} %add_convert_fusion.1), channel_id=1, source_target_pairs={{0,2},{1,3},{2,0},{3,1},{4,5},{5,4},{6,7},{7,6},{8,10},{9,11},{10,... | collective-permute-start | bytes 1572872 | tf_op jit(solution)/shard_map/ppermute | solution.py:192
  86.5 11.9 %collective-permute-start.36 = (bf16[128,1024]{1,0:T(8,128)(2,1)S(1)}, bf16[128,1024]{1,0:T(8,128)(2,1)S(1)}, u32[]{:S(2)}, u32[]{:S(2)}) collective-permute-start(bf16[128,1024]{1,0:T(8,128)(2,1)S(1)} %fusion.10), channel_id=1, source_target_pairs={{0,24},{1,25},{2,26},{3,27},{4,28},{5,29},{6,30},{7,31},{8,0},{9,1... | collective-permute-start | bytes 786440 | tf_op jit(solution)/shard_map/ppermute | solution.py:192
  91.2 7.2 %collective-permute-start.35 = (bf16[1,1,128,1024]{3,2,1,0:T(8,128)(2,1)S(1)}, bf16[1,1,128,1024]{3,2,1,0:T(8,128)(2,1)S(1)}, u32[]{:S(2)}, u32[]{:S(2)}) collective-permute-start(bf16[1,1,128,1024]{3,2,1,0:T(8,128)(2,1)S(1)} %slice.74), channel_id=1, source_target_pairs={{0,1},{1,0},{2,3},{3,2},{4,6},{5,7},{6,4},{7,5},{8,9},{9,8},{10,11... | collective-permute-start | bytes 786440 | tf_op jit(solution)/shard_map/ppermute | solution.py:192
  97.1 6.4 %collective-permute-start.30 = (bf16[1,1,128,1024]{3,2,1,0:T(8,128)(2,1)S(1)}, bf16[1,1,128,1024]{3,2,1,0:T(8,128)(2,1)S(1)}, u32[]{:S(2)}, u32[]{:S(2)}) collective-permute-start(bf16[1,1,128,1024]{3,2,1,0:T(8,128)(2,1)S(1)} %slice.75), channel_id=1, source_target_pairs={{0,1},{1,0},{2,3},{3,2},{4,6},{5,7},{6,4},{7,5},{8,9},{9,8},{10,11... | collective-permute-start | bytes 786440 | tf_op jit(solution)/shard_map/ppermute | solution.py:192
  98.5 9.2 %collective-permute-start.37 = (bf16[128,1024]{1,0:T(8,128)(2,1)S(1)}, bf16[128,1024]{1,0:T(8,128)(2,1)S(1)}, u32[]{:S(2)}, u32[]{:S(2)}) collective-permute-start(bf16[128,1024]{1,0:T(8,128)(2,1)S(1)} %fusion.3), channel_id=1, source_target_pairs={{0,24},{1,25},{2,26},{3,27},{4,28},{5,29},{6,30},{7,31},{8,0},{9,1... | collective-permute-start | bytes 786440 | tf_op jit(solution)/shard_map/ppermute | solution.py:192
  (6 other events, 17.8 us)

commit v4 on v3

--- a/solution.py
+++ b/solution.py
@@ -257,9 +257,7 @@
         i = r - 2 * stages - 1
         if 1 <= i < n_z:
             done = keep[i][0, 0]
-            if i > n_z // 2:
-                done = done + back.pop(i - 1)
-            done = shift(done.astype(bf16), -1 if 2 * i >= n_z else i)
+            done = shift(done.astype(bf16), i)
             moves.append((done, lambda got, i=i: put(back, i, got.astype(f32))))
         made = []
         for i, sib in zip(ready, far_sib):

time: 109 us -> 108 us (level)
  starting transfers between devices: 47.2 us -> 43.1 us
  waiting for transfers between devices: 30.1 us -> 33.8 us
    ppermute x38, starting transfers between devices: 47.2 us -> 43.1 us  [send(): return lax.ppermute(value, AXES, pairs)]
    ppermute x38, waiting for transfers between devices: 30.1 us -> 33.8 us  [send(): return lax.ppermute(value, AXES, pairs)]
  transfers between devices with their start and end apart: 38 -> 38, of which waited for: 12 -> 13; matrix products, arithmetic and copies ran while one was open for 3% -> 3% of each run, Pallas kernels for 23% -> 23%
where the time goes in v4:
time: 108 us
  starting transfers between devices  43.1 us (40%)
  waiting for transfers between devices  33.8 us (31%)
  Pallas kernels  26.8 us (25%)
  other arithmetic  4.02 us (4%)
    ppermute x38, starting transfers between devices, send(): return lax.ppermute(value, AXES, pairs)  43.1 us
    ppermute x38, waiting for transfers between devices, send(): return lax.ppermute(value, AXES, pairs)  33.8 us
    pallas_call x4, Pallas kernels, run_experts(): pl.pallas_call(functools.partial(expert_kernel, pieces, offsets, block, f...  24.9 us
  transfers between devices with their start and end apart: 38, of which 13 were waited for; matrix products, arithmetic and copies ran while one was open for 3% of the time, Pallas kernels for 23%

profile of v4, /device:TPU:0, one launch (start us, length us, event | category | flops | bytes accessed | tf_op | source)
XLA Modules:
  0.0 108.1 jit_solution(4516006320435530051)
XLA Ops:
  0.0 1.9 %shard_map.73 = bf16[136,1024]{1,0:T(8,128)(2,1)} custom-call(bf16[128,1024]{1,0:T(8,128)(2,1)} %hidden.1, f32[1,1024]{1,0:T(1,128)} %bitcast.33, s32[8,128]{1,0:T(8,128)} %bitcast.34, f32[8,128]{1,0:T(8,128)} %bitcast.35), custom_call_target="tpu_custom_call" | custom-call | tf_op jit(solution)/shard_map/pallas_call | solution.py:205
  1.9 5.0 %collective-permute-start = (bf16[136,1024]{1,0:T(8,128)(2,1)}, bf16[136,1024]{1,0:T(8,128)(2,1)S(1)}, u32[]{:S(2)}, u32[]{:S(2)}) collective-permute-start(bf16[136,1024]{1,0:T(8,128)(2,1)} %shard_map.73), channel_id=1, source_target_pairs={{0,24},{1,25},{2,26},{3,27},{4,28},{5,29},{6,30},{7,31},{8,0},{9,1... | collective-permute-start | bytes 835592 | tf_op jit(solution)/shard_map/ppermute | solution.py:192
  6.9 1.5 %collective-permute-start.7 = (bf16[1,1,136,1024]{3,2,1,0:T(8,128)(2,1)}, bf16[1,1,136,1024]{3,2,1,0:T(8,128)(2,1)S(1)}, u32[]{:S(2)}, u32[]{:S(2)}) collective-permute-start(bf16[1,1,136,1024]{3,2,1,0:T(8,128)(2,1)} %bitcast.25), channel_id=1, source_target_pairs={{0,1},{1,0},{2,3},{3,2},{4,6},{5,7},{6,4},{7,5},{8,9},{9,8},{10,11... | collective-permute-start | bytes 835592 | tf_op jit(solution)/shard_map/ppermute | solution.py:192
  8.4 4.7 %collective-permute-done = bf16[136,1024]{1,0:T(8,128)(2,1)S(1)} collective-permute-done((bf16[136,1024]{1,0:T(8,128)(2,1)}, bf16[136,1024]{1,0:T(8,128)(2,1)S(1)}, u32[]{:S(2)}, u32[]{:S(2)}) %collective-permute-start) | collective-permute-done | bytes 278560 | tf_op jit(solution)/shard_map/ppermute | solution.py:192
  13.2 1.5 %collective-permute-start.3 = (bf16[1,1,136,1024]{3,2,1,0:T(8,128)(2,1)S(1)}, bf16[1,1,136,1024]{3,2,1,0:T(8,128)(2,1)S(1)}, u32[]{:S(2)}, u32[]{:S(2)}) collective-permute-start(bf16[1,1,136,1024]{3,2,1,0:T(8,128)(2,1)S(1)} %bitcast.31), channel_id=1, source_target_pairs={{0,1},{1,0},{2,3},{3,2},{4,6},{5,7},{6,4},{7,5},{8,9},{9,8},{10,11... | collective-permute-start | bytes 835592 | tf_op jit(solution)/shard_map/ppermute | solution.py:192
  14.7 1.0 pad_maximum_fusion.1.refs_0_
  15.7 1.6 %collective-permute-start.8 = (bf16[2,1,136,1024]{3,2,1,0:T(8,128)(2,1)S(1)}, bf16[2,1,136,1024]{3,2,1,0:T(8,128)(2,1)S(1)}, u32[]{:S(2)}, u32[]{:S(2)}) collective-permute-start(bf16[2,1,136,1024]{3,2,1,0:T(8,128)(2,1)S(1)} %pad_maximum_fusion.1.refs_0_), channel_id=1, source_target_pairs={{0,2},{1,3},{2,0},{3,1},{4,5},{5,4},{6,7},{7,6},{8,10},{9,11},{10,... | collective-permute-start | bytes 1671176 | tf_op jit(solution)/shard_map/ppermute | solution.py:192
  17.3 4.2 %collective-permute-start.1 = (bf16[136,1024]{1,0:T(8,128)(2,1)S(1)}, bf16[136,1024]{1,0:T(8,128)(2,1)S(1)}, u32[]{:S(2)}, u32[]{:S(2)}) collective-permute-start(bf16[136,1024]{1,0:T(8,128)(2,1)S(1)} %collective-permute-done), channel_id=1, source_target_pairs={{0,24},{1,25},{2,26},{3,27},{4,28},{5,29},{6,30},{7,31},{8,0},{9,1... | collective-permute-start | bytes 835592 | tf_op jit(solution)/shard_map/ppermute | solution.py:192
  22.4 1.9 %collective-permute-start.4 = (bf16[2,1,136,1024]{3,2,1,0:T(8,128)(2,1)S(1)}, bf16[2,1,136,1024]{3,2,1,0:T(8,128)(2,1)S(1)}, u32[]{:S(2)}, u32[]{:S(2)}) collective-permute-start(bf16[2,1,136,1024]{3,2,1,0:T(8,128)(2,1)S(1)} %pad_maximum_fusion.refs_0_), channel_id=1, source_target_pairs={{0,2},{1,3},{2,0},{3,1},{4,5},{5,4},{6,7},{7,6},{8,10},{9,11},{10,... | collective-permute-start | bytes 1671176 | tf_op jit(solution)/shard_map/ppermute | solution.py:192
  24.3 1.6 %collective-permute-done.1 = bf16[136,1024]{1,0:T(8,128)(2,1)S(1)} collective-permute-done((bf16[136,1024]{1,0:T(8,128)(2,1)S(1)}, bf16[136,1024]{1,0:T(8,128)(2,1)S(1)}, u32[]{:S(2)}, u32[]{:S(2)}) %collective-permute-start.1) | collective-permute-done | bytes 278560 | tf_op jit(solution)/shard_map/ppermute | solution.py:192
  26.4 4.3 %collective-permute-start.6 = (bf16[136,1024]{1,0:T(8,128)(2,1)S(1)}, bf16[136,1024]{1,0:T(8,128)(2,1)S(1)}, u32[]{:S(2)}, u32[]{:S(2)}) collective-permute-start(bf16[136,1024]{1,0:T(8,128)(2,1)S(1)} %collective-permute-done.1), channel_id=1, source_target_pairs={{0,24},{1,25},{2,26},{3,27},{4,28},{5,29},{6,30},{7,31},{8,0},{9,1... | collective-permute-start | bytes 835592 | tf_op jit(solution)/shard_map/ppermute | solution.py:192
  30.7 3.9 %collective-permute-done.2 = bf16[1,1,136,1024]{3,2,1,0:T(8,128)(2,1)S(1)} collective-permute-done((bf16[1,1,136,1024]{3,2,1,0:T(8,128)(2,1)S(1)}, bf16[1,1,136,1024]{3,2,1,0:T(8,128)(2,1)S(1)}, u32[]{:S(2)}, u32[]{:S(2)}) %collective-permute-start.2) | collective-permute-done | bytes 278560 | tf_op jit(solution)/shard_map/ppermute | solution.py:192
  35.1 1.8 %collective-permute-start.11 = (bf16[2,1,136,1024]{3,2,1,0:T(8,128)(2,1)S(1)}, bf16[2,1,136,1024]{3,2,1,0:T(8,128)(2,1)S(1)}, u32[]{:S(2)}, u32[]{:S(2)}) collective-permute-start(bf16[2,1,136,1024]{3,2,1,0:T(8,128)(2,1)S(1)} %pad_maximum_fusion.2.refs_0_), channel_id=1, source_target_pairs={{0,2},{1,3},{2,0},{3,1},{4,5},{5,4},{6,7},{7,6},{8,10},{9,11},{10,... | collective-permute-start | bytes 1671176 | tf_op jit(solution)/shard_map/ppermute | solution.py:192
  36.9 1.5 %collective-permute-start.9 = (bf16[1,1,136,1024]{3,2,1,0:T(8,128)(2,1)S(1)}, bf16[1,1,136,1024]{3,2,1,0:T(8,128)(2,1)S(1)}, u32[]{:S(2)}, u32[]{:S(2)}) collective-permute-start(bf16[1,1,136,1024]{3,2,1,0:T(8,128)(2,1)S(1)} %bitcast.27), channel_id=1, source_target_pairs={{0,1},{1,0},{2,3},{3,2},{4,6},{5,7},{6,4},{7,5},{8,9},{9,8},{10,11... | collective-permute-start | bytes 835592 | tf_op jit(solution)/shard_map/ppermute | solution.py:192
  38.4 9.1 %shard_map.74 = (bf16[2,1,128,1024]{3,2,1,0:T(8,128)(2,1)S(1)}, bf16[2,1,128,1024]{3,2,1,0:T(8,128)(2,1)S(1)}, bf16[2,1,128,1024]{3,2,1,0:T(8,128)(2,1)S(1)}, bf...) custom-call(bf16[2,1,136,1024]{3,2,1,0:T(8,128)(2,1)S(1)} %pad_maxim, ...), custom_call_target="tpu_custom_call" | custom-call | flops 4831838208 | bytes 4194304 | tf_op jit(solution)/shard_map/pallas_call | solution.py:154
  48.3 1.3 %collective-permute-start.14 = (bf16[2,1,136,1024]{3,2,1,0:T(8,128)(2,1)S(1)}, bf16[2,1,136,1024]{3,2,1,0:T(8,128)(2,1)S(1)}, u32[]{:S(2)}, u32[]{:S(2)}) collective-permute-start(bf16[2,1,136,1024]{3,2,1,0:T(8,128)(2,1)S(1)} %pad_maximum_fusion.3.refs_0_), channel_id=1, source_target_pairs={{0,2},{1,3},{2,0},{3,1},{4,5},{5,4},{6,7},{7,6},{8,10},{9,11},{10,... | collective-permute-start | bytes 1671176 | tf_op jit(solution)/shard_map/ppermute | solution.py:192
  51.9 5.2 %shard_map.76 = (bf16[2,1,128,1024]{3,2,1,0:T(8,128)(2,1)S(1)}, bf16[2,1,128,1024]{3,2,1,0:T(8,128)(2,1)S(1)}, bf16[2,1,128,1024]{3,2,1,0:T(8,128)(2,1)S(1)}, bf16[2,1,128,1024]{3,2,1,0:T(8,128)(2,1)S(1)}) custom-call(bf16[2,1,136,1024]{3,2,1,0:T(8,128)(2,1)S(1)} %pad_maximum_fusion.1.refs_0_, bf16[2,1,136,1024]{3,2,1,0:T(8,128)(2,1)S(1)} %collective-permute-done.8.refs_1_, ...), custom_call_target="tpu_custom_call" | custom-call | flops 4831838208 | bytes 4194304 | tf_op jit(solution)/shard_map/pallas_call | solution.py:154
  57.2 5.4 %shard_map.75 = (bf16[2,1,128,1024]{3,2,1,0:T(8,128)(2,1)S(1)}, bf16[2,1,128,1024]{3,2,1,0:T(8,128)(2,1)S(1)}, bf16[2,1,128,1024]{3,2,1,0:T(8,128)(2,1)S(1)}, bf16[2,1,128,1024]{3,2,1,0:T(8,128)(2,1)S(1)}) custom-call(bf16[2,1,136,1024]{3,2,1,0:T(8,128)(2,1)S(1)} %pad_maximum_fusion.2.refs_0_, bf16[2,1,136,1024]{3,2,1,0:T(8,128)(2,1)S(1)} %collective-permute-done.11.refs_1_, ...), custom_call_target="tpu_custom_call" | custom-call | flops 4831838208 | bytes 4194304 | tf_op jit(solution)/shard_map/pallas_call | solution.py:154
  63.8 1.2 %collective-permute-start.21 = (bf16[1,1,128,1024]{3,2,1,0:T(8,128)(2,1)S(1)}, bf16[1,1,128,1024]{3,2,1,0:T(8,128)(2,1)S(1)}, u32[]{:S(2)}, u32[]{:S(2)}) collective-permute-start(bf16[1,1,128,1024]{3,2,1,0:T(8,128)(2,1)S(1)} %slice.77), channel_id=1, source_target_pairs={{0,1},{1,0},{2,3},{3,2},{4,6},{5,7},{6,4},{7,5},{8,9},{9,8},{10,11... | collective-permute-start | bytes 786440 | tf_op jit(solution)/shard_map/ppermute | solution.py:192
  65.7 1.5 %collective-permute-start.26 = (bf16[2,1,128,1024]{3,2,1,0:T(8,128)(2,1)S(1)}, bf16[2,1,128,1024]{3,2,1,0:T(8,128)(2,1)S(1)}, u32[]{:S(2)}, u32[]{:S(2)}) collective-permute-start(bf16[2,1,128,1024]{3,2,1,0:T(8,128)(2,1)S(1)} %add_convert_fusion.2), channel_id=1, source_target_pairs={{0,2},{1,3},{2,0},{3,1},{4,5},{5,4},{6,7},{7,6},{8,10},{9,11},{10,... | collective-permute-start | bytes 1572872 | tf_op jit(solution)/shard_map/ppermute | solution.py:192
  67.2 5.2 %shard_map.77 = (bf16[2,1,128,1024]{3,2,1,0:T(8,128)(2,1)S(1)}, bf16[2,1,128,1024]{3,2,1,0:T(8,128)(2,1)S(1)}, bf16[2,1,128,1024]{3,2,1,0:T(8,128)(2,1)S(1)}, bf16[2,1,128,1024]{3,2,1,0:T(8,128)(2,1)S(1)}) custom-call(bf16[2,1,136,1024]{3,2,1,0:T(8,128)(2,1)S(1)} %pad_maximum_fusion.3.refs_0_, bf16[2,1,136,1024]{3,2,1,0:T(8,128)(2,1)S(1)} %collective-permute-done.14.refs_1_, ...), custom_call_target="tpu_custom_call" | custom-call | flops 4831838208 | bytes 4194304 | tf_op jit(solution)/shard_map/pallas_call | solution.py:154
  73.0 2.4 %collective-permute-done.26 = bf16[2,1,128,1024]{3,2,1,0:T(8,128)(2,1)S(1)} collective-permute-done((bf16[2,1,128,1024]{3,2,1,0:T(8,128)(2,1)S(1)}, bf16[2,1,128,1024]{3,2,1,0:T(8,128)(2,1)S(1)}, u32[]{:S(2)}, u32[]{:S(2)}) %collective-permute-start.26) | collective-permute-done | bytes 524320 | tf_op jit(solution)/shard_map/ppermute | solution.py:192
  75.7 1.1 collective-permute-start.27
  77.2 1.4 %collective-permute-start.35 = (bf16[2,1,128,1024]{3,2,1,0:T(8,128)(2,1)S(1)}, bf16[2,1,128,1024]{3,2,1,0:T(8,128)(2,1)S(1)}, u32[]{:S(2)}, u32[]{:S(2)}) collective-permute-start(bf16[2,1,128,1024]{3,2,1,0:T(8,128)(2,1)S(1)} %add_convert_fusion), channel_id=1, source_target_pairs={{0,2},{1,3},{2,0},{3,1},{4,5},{5,4},{6,7},{7,6},{8,10},{9,11},{10,... | collective-permute-start | bytes 1572872 | tf_op jit(solution)/shard_map/ppermute | solution.py:192
  79.2 4.9 %collective-permute-done.27 = bf16[1,1,128,1024]{3,2,1,0:T(8,128)(2,1)S(1)} collective-permute-done((bf16[1,1,128,1024]{3,2,1,0:T(8,128)(2,1)S(1)}, bf16[1,1,128,1024]{3,2,1,0:T(8,128)(2,1)S(1)}, u32[]{:S(2)}, u32[]{:S(2)}) %collective-permute-start.27) | collective-permute-done | bytes 262176 | tf_op jit(solution)/shard_map/ppermute | solution.py:192
  85.1 1.4 %collective-permute-start.32 = (bf16[128,1024]{1,0:T(8,128)(2,1)S(1)}, bf16[128,1024]{1,0:T(8,128)(2,1)S(1)}, u32[]{:S(2)}, u32[]{:S(2)}) collective-permute-start(bf16[128,1024]{1,0:T(8,128)(2,1)S(1)} %fusion.9), channel_id=1, source_target_pairs={{0,16},{1,17},{2,18},{3,19},{4,20},{5,21},{6,22},{7,23},{8,24},{9,... | collective-permute-start | bytes 786440 | tf_op jit(solution)/shard_map/ppermute | solution.py:192
  87.4 1.5 %collective-permute-start.36 = (bf16[1,1,128,1024]{3,2,1,0:T(8,128)(2,1)S(1)}, bf16[1,1,128,1024]{3,2,1,0:T(8,128)(2,1)S(1)}, u32[]{:S(2)}, u32[]{:S(2)}) collective-permute-start(bf16[1,1,128,1024]{3,2,1,0:T(8,128)(2,1)S(1)} %slice.74), channel_id=1, source_target_pairs={{0,1},{1,0},{2,3},{3,2},{4,6},{5,7},{6,4},{7,5},{8,9},{9,8},{10,11... | collective-permute-start | bytes 786440 | tf_op jit(solution)/shard_map/ppermute | solution.py:192
  88.9 6.9 %collective-permute-done.29 = bf16[2,1,128,1024]{3,2,1,0:T(8,128)(2,1)S(1)} collective-permute-done((bf16[2,1,128,1024]{3,2,1,0:T(8,128)(2,1)S(1)}, bf16[2,1,128,1024]{3,2,1,0:T(8,128)(2,1)S(1)}, u32[]{:S(2)}, u32[]{:S(2)}) %collective-permute-start.29) | collective-permute-done | bytes 524320 | tf_op jit(solution)/shard_map/ppermute | solution.py:192
  96.1 0.9 collective-permute-start.30
  97.1 4.3 %collective-permute-start.37 = (bf16[128,1024]{1,0:T(8,128)(2,1)S(1)}, bf16[128,1024]{1,0:T(8,128)(2,1)S(1)}, u32[]{:S(2)}, u32[]{:S(2)}) collective-permute-start(bf16[128,1024]{1,0:T(8,128)(2,1)S(1)} %fusion.10), channel_id=1, source_target_pairs={{0,24},{1,25},{2,26},{3,27},{4,28},{5,29},{6,30},{7,31},{8,0},{9,1... | collective-permute-start | bytes 786440 | tf_op jit(solution)/shard_map/ppermute | solution.py:192
  101.4 1.1 collective-permute-done.30
  102.5 4.7 %collective-permute-done.37 = bf16[128,1024]{1,0:T(8,128)(2,1)S(1)} collective-permute-done((bf16[128,1024]{1,0:T(8,128)(2,1)S(1)}, bf16[128,1024]{1,0:T(8,128)(2,1)S(1)}, u32[]{:S(2)}, u32[]{:S(2)}) %collective-permute-start.37) | collective-permute-done | bytes 262176 | tf_op jit(solution)/shard_map/ppermute | solution.py:192
  (69 shorter events, 11.9 us)
Async XLA Ops:
  1.9 11.3 %collective-permute-start = (bf16[136,1024]{1,0:T(8,128)(2,1)}, bf16[136,1024]{1,0:T(8,128)(2,1)S(1)}, u32[]{:S(2)}, u32[]{:S(2)}) collective-permute-start(bf16[136,1024]{1,0:T(8,128)(2,1)} %shard_map.73), channel_id=1, source_target_pairs={{0,24},{1,25},{2,26},{3,27},{4,28},{5,29},{6,30},{7,31},{8,0},{9,1... | collective-permute-start | bytes 835592 | tf_op jit(solution)/shard_map/ppermute | solution.py:192
  6.9 7.7 %collective-permute-start.7 = (bf16[1,1,136,1024]{3,2,1,0:T(8,128)(2,1)}, bf16[1,1,136,1024]{3,2,1,0:T(8,128)(2,1)S(1)}, u32[]{:S(2)}, u32[]{:S(2)}) collective-permute-start(bf16[1,1,136,1024]{3,2,1,0:T(8,128)(2,1)} %bitcast.25), channel_id=1, source_target_pairs={{0,1},{1,0},{2,3},{3,2},{4,6},{5,7},{6,4},{7,5},{8,9},{9,8},{10,11... | collective-permute-start | bytes 835592 | tf_op jit(solution)/shard_map/ppermute | solution.py:192
  13.2 9.2 %collective-permute-start.3 = (bf16[1,1,136,1024]{3,2,1,0:T(8,128)(2,1)S(1)}, bf16[1,1,136,1024]{3,2,1,0:T(8,128)(2,1)S(1)}, u32[]{:S(2)}, u32[]{:S(2)}) collective-permute-start(bf16[1,1,136,1024]{3,2,1,0:T(8,128)(2,1)S(1)} %bitcast.31), channel_id=1, source_target_pairs={{0,1},{1,0},{2,3},{3,2},{4,6},{5,7},{6,4},{7,5},{8,9},{9,8},{10,11... | collective-permute-start | bytes 835592 | tf_op jit(solution)/shard_map/ppermute | solution.py:192
  15.7 15.1 %collective-permute-start.8 = (bf16[2,1,136,1024]{3,2,1,0:T(8,128)(2,1)S(1)}, bf16[2,1,136,1024]{3,2,1,0:T(8,128)(2,1)S(1)}, u32[]{:S(2)}, u32[]{:S(2)}) collective-permute-start(bf16[2,1,136,1024]{3,2,1,0:T(8,128)(2,1)S(1)} %pad_maximum_fusion.1.refs_0_), channel_id=1, source_target_pairs={{0,2},{1,3},{2,0},{3,1},{4,5},{5,4},{6,7},{7,6},{8,10},{9,11},{10,... | collective-permute-start | bytes 1671176 | tf_op jit(solution)/shard_map/ppermute | solution.py:192
  17.3 8.7 %collective-permute-start.1 = (bf16[136,1024]{1,0:T(8,128)(2,1)S(1)}, bf16[136,1024]{1,0:T(8,128)(2,1)S(1)}, u32[]{:S(2)}, u32[]{:S(2)}) collective-permute-start(bf16[136,1024]{1,0:T(8,128)(2,1)S(1)} %collective-permute-done), channel_id=1, source_target_pairs={{0,24},{1,25},{2,26},{3,27},{4,28},{5,29},{6,30},{7,31},{8,0},{9,1... | collective-permute-start | bytes 835592 | tf_op jit(solution)/shard_map/ppermute | solution.py:192
  22.4 12.6 %collective-permute-start.4 = (bf16[2,1,136,1024]{3,2,1,0:T(8,128)(2,1)S(1)}, bf16[2,1,136,1024]{3,2,1,0:T(8,128)(2,1)S(1)}, u32[]{:S(2)}, u32[]{:S(2)}) collective-permute-start(bf16[2,1,136,1024]{3,2,1,0:T(8,128)(2,1)S(1)} %pad_maximum_fusion.refs_0_), channel_id=1, source_target_pairs={{0,2},{1,3},{2,0},{3,1},{4,5},{5,4},{6,7},{7,6},{8,10},{9,11},{10,... | collective-permute-start | bytes 1671176 | tf_op jit(solution)/shard_map/ppermute | solution.py:192
  24.3 10.8 %collective-permute-start.5 = (bf16[2,1,136,1024]{3,2,1,0:T(8,128)(2,1)S(1)}, bf16[2,1,136,1024]{3,2,1,0:T(8,128)(2,1)S(1)}, u32[]{:S(2)}, u32[]{:S(2)}) collective-permute-start(bf16[2,1,136,1024]{3,2,1,0:T(8,128)(2,1)S(1)} %pad_maximum_fusion.refs_0_), channel_id=1, source_target_pairs={{0,4},{1,5},{2,6},{3,7},{4,0},{5,1},{6,2},{7,3},{8,12},{9,13},{10,... | collective-permute-start | bytes 1671176 | tf_op jit(solution)/shard_map/ppermute | solution.py:192
  25.9 8.7 %collective-permute-start.2 = (bf16[1,1,136,1024]{3,2,1,0:T(8,128)(2,1)S(1)}, bf16[1,1,136,1024]{3,2,1,0:T(8,128)(2,1)S(1)}, u32[]{:S(2)}, u32[]{:S(2)}) collective-permute-start(bf16[1,1,136,1024]{3,2,1,0:T(8,128)(2,1)S(1)} %bitcast.29), channel_id=1, source_target_pairs={{0,1},{1,0},{2,3},{3,2},{4,6},{5,7},{6,4},{7,5},{8,9},{9,8},{10,11... | collective-permute-start | bytes 835592 | tf_op jit(solution)/shard_map/ppermute | solution.py:192
  26.4 8.6 %collective-permute-start.6 = (bf16[136,1024]{1,0:T(8,128)(2,1)S(1)}, bf16[136,1024]{1,0:T(8,128)(2,1)S(1)}, u32[]{:S(2)}, u32[]{:S(2)}) collective-permute-start(bf16[136,1024]{1,0:T(8,128)(2,1)S(1)} %collective-permute-done.1), channel_id=1, source_target_pairs={{0,24},{1,25},{2,26},{3,27},{4,28},{5,29},{6,30},{7,31},{8,0},{9,1... | collective-permute-start | bytes 835592 | tf_op jit(solution)/shard_map/ppermute | solution.py:192
  35.1 13.0 %collective-permute-start.11 = (bf16[2,1,136,1024]{3,2,1,0:T(8,128)(2,1)S(1)}, bf16[2,1,136,1024]{3,2,1,0:T(8,128)(2,1)S(1)}, u32[]{:S(2)}, u32[]{:S(2)}) collective-permute-start(bf16[2,1,136,1024]{3,2,1,0:T(8,128)(2,1)S(1)} %pad_maximum_fusion.2.refs_0_), channel_id=1, source_target_pairs={{0,2},{1,3},{2,0},{3,1},{4,5},{5,4},{6,7},{7,6},{8,10},{9,11},{10,... | collective-permute-start | bytes 1671176 | tf_op jit(solution)/shard_map/ppermute | solution.py:192
  36.9 11.2 %collective-permute-start.12 = (bf16[2,1,136,1024]{3,2,1,0:T(8,128)(2,1)S(1)}, bf16[2,1,136,1024]{3,2,1,0:T(8,128)(2,1)S(1)}, u32[]{:S(2)}, u32[]{:S(2)}) collective-permute-start(bf16[2,1,136,1024]{3,2,1,0:T(8,128)(2,1)S(1)} %pad_maximum_fusion.2.refs_0_), channel_id=1, source_target_pairs={{0,4},{1,5},{2,6},{3,7},{4,0},{5,1},{6,2},{7,3},{8,12},{9,13},{10,... | collective-permute-start | bytes 1671176 | tf_op jit(solution)/shard_map/ppermute | solution.py:192
  36.9 10.6 %collective-permute-start.9 = (bf16[1,1,136,1024]{3,2,1,0:T(8,128)(2,1)S(1)}, bf16[1,1,136,1024]{3,2,1,0:T(8,128)(2,1)S(1)}, u32[]{:S(2)}, u32[]{:S(2)}) collective-permute-start(bf16[1,1,136,1024]{3,2,1,0:T(8,128)(2,1)S(1)} %bitcast.27), channel_id=1, source_target_pairs={{0,1},{1,0},{2,3},{3,2},{4,6},{5,7},{6,4},{7,5},{8,9},{9,8},{10,11... | collective-permute-start | bytes 835592 | tf_op jit(solution)/shard_map/ppermute | solution.py:192
  48.3 14.4 %collective-permute-start.14 = (bf16[2,1,136,1024]{3,2,1,0:T(8,128)(2,1)S(1)}, bf16[2,1,136,1024]{3,2,1,0:T(8,128)(2,1)S(1)}, u32[]{:S(2)}, u32[]{:S(2)}) collective-permute-start(bf16[2,1,136,1024]{3,2,1,0:T(8,128)(2,1)S(1)} %pad_maximum_fusion.3.refs_0_), channel_id=1, source_target_pairs={{0,2},{1,3},{2,0},{3,1},{4,5},{5,4},{6,7},{7,6},{8,10},{9,11},{10,... | collective-permute-start | bytes 1671176 | tf_op jit(solution)/shard_map/ppermute | solution.py:192
  49.6 13.1 %collective-permute-start.15 = (bf16[2,1,136,1024]{3,2,1,0:T(8,128)(2,1)S(1)}, bf16[2,1,136,1024]{3,2,1,0:T(8,128)(2,1)S(1)}, u32[]{:S(2)}, u32[]{:S(2)}) collective-permute-start(bf16[2,1,136,1024]{3,2,1,0:T(8,128)(2,1)S(1)} %pad_maximum_fusion.3.refs_0_), channel_id=1, source_target_pairs={{0,4},{1,5},{2,6},{3,7},{4,0},{5,1},{6,2},{7,3},{8,12},{9,13},{10,... | collective-permute-start | bytes 1671176 | tf_op jit(solution)/shard_map/ppermute | solution.py:192
  49.6 7.6 %collective-permute-start.18 = (bf16[2,1,136,1024]{3,2,1,0:T(8,128)(2,1)S(1)}, bf16[2,1,136,1024]{3,2,1,0:T(8,128)(2,1)S(1)}, u32[]{:S(2)}, u32[]{:S(2)}) collective-permute-start(bf16[2,1,136,1024]{3,2,1,0:T(8,128)(2,1)S(1)} %collective-permute-done.11.refs_1_), channel_id=1, source_target_pairs={{0,4},{1,5},{2,6},{3,7},{4,0},{5,1},{6,2},{7,3},{8,12},{9,13},{10,... | collective-permute-start | bytes 1671176 | tf_op jit(solution)/shard_map/ppermute | solution.py:192
  50.3 12.3 %collective-permute-start.13 = (bf16[2,1,128,1024]{3,2,1,0:T(8,128)(2,1)S(1)}, bf16[2,1,128,1024]{3,2,1,0:T(8,128)(2,1)S(1)}, u32[]{:S(2)}, u32[]{:S(2)}) collective-permute-start(bf16[2,1,128,1024]{3,2,1,0:T(8,128)(2,1)S(1)} %get-tuple-element.71), channel_id=1, source_target_pairs={{0,4},{1,5},{2,6},{3,7},{4,0},{5,1},{6,2},{7,3},{8,12},{9,13},{10,... | collective-permute-start | bytes 1572872 | tf_op jit(solution)/shard_map/ppermute | solution.py:192
  51.1 12.4 %collective-permute-start.17 = (bf16[2,1,128,1024]{3,2,1,0:T(8,128)(2,1)S(1)}, bf16[2,1,128,1024]{3,2,1,0:T(8,128)(2,1)S(1)}, u32[]{:S(2)}, u32[]{:S(2)}) collective-permute-start(bf16[2,1,128,1024]{3,2,1,0:T(8,128)(2,1)S(1)} %add_convert_fusion.3), channel_id=1, source_target_pairs={{0,2},{1,3},{2,0},{3,1},{4,5},{5,4},{6,7},{7,6},{8,10},{9,11},{10,... | collective-permute-start | bytes 1572872 | tf_op jit(solution)/shard_map/ppermute | solution.py:192
  63.8 8.6 %collective-permute-start.21 = (bf16[1,1,128,1024]{3,2,1,0:T(8,128)(2,1)S(1)}, bf16[1,1,128,1024]{3,2,1,0:T(8,128)(2,1)S(1)}, u32[]{:S(2)}, u32[]{:S(2)}) collective-permute-start(bf16[1,1,128,1024]{3,2,1,0:T(8,128)(2,1)S(1)} %slice.77), channel_id=1, source_target_pairs={{0,1},{1,0},{2,3},{3,2},{4,6},{5,7},{6,4},{7,5},{8,9},{9,8},{10,11... | collective-permute-start | bytes 786440 | tf_op jit(solution)/shard_map/ppermute | solution.py:192
  65.0 8.0 %collective-permute-start.23 = (bf16[2,1,128,1024]{3,2,1,0:T(8,128)(2,1)S(1)}, bf16[2,1,128,1024]{3,2,1,0:T(8,128)(2,1)S(1)}, u32[]{:S(2)}, u32[]{:S(2)}) collective-permute-start(bf16[2,1,128,1024]{3,2,1,0:T(8,128)(2,1)S(1)} %get-tuple-element.95), channel_id=1, source_target_pairs={{0,4},{1,5},{2,6},{3,7},{4,0},{5,1},{6,2},{7,3},{8,12},{9,13},{10,... | collective-permute-start | bytes 1572872 | tf_op jit(solution)/shard_map/ppermute | solution.py:192
  65.3 7.7 %collective-permute-start.24 = (bf16[2,1,128,1024]{3,2,1,0:T(8,128)(2,1)S(1)}, bf16[2,1,128,1024]{3,2,1,0:T(8,128)(2,1)S(1)}, u32[]{:S(2)}, u32[]{:S(2)}) collective-permute-start(bf16[2,1,128,1024]{3,2,1,0:T(8,128)(2,1)S(1)} %get-tuple-element.96), channel_id=1, source_target_pairs={{0,4},{1,5},{2,6},{3,7},{4,0},{5,1},{6,2},{7,3},{8,12},{9,13},{10,... | collective-permute-start | bytes 1572872 | tf_op jit(solution)/shard_map/ppermute | solution.py:192
  65.7 9.6 %collective-permute-start.26 = (bf16[2,1,128,1024]{3,2,1,0:T(8,128)(2,1)S(1)}, bf16[2,1,128,1024]{3,2,1,0:T(8,128)(2,1)S(1)}, u32[]{:S(2)}, u32[]{:S(2)}) collective-permute-start(bf16[2,1,128,1024]{3,2,1,0:T(8,128)(2,1)S(1)} %add_convert_fusion.2), channel_id=1, source_target_pairs={{0,2},{1,3},{2,0},{3,1},{4,5},{5,4},{6,7},{7,6},{8,10},{9,11},{10,... | collective-permute-start | bytes 1572872 | tf_op jit(solution)/shard_map/ppermute | solution.py:192
  72.4 4.6 %collective-permute-start.34 = (bf16[2,1,128,1024]{3,2,1,0:T(8,128)(2,1)S(1)}, bf16[2,1,128,1024]{3,2,1,0:T(8,128)(2,1)S(1)}, u32[]{:S(2)}, u32[]{:S(2)}) collective-permute-start(bf16[2,1,128,1024]{3,2,1,0:T(8,128)(2,1)S(1)} %get-tuple-element.116), channel_id=1, source_target_pairs={{0,4},{1,5},{2,6},{3,7},{4,0},{5,1},{6,2},{7,3},{8,12},{9,13},{10,... | collective-permute-start | bytes 1572872 | tf_op jit(solution)/shard_map/ppermute | solution.py:192
  72.5 6.1 %collective-permute-start.28 = (bf16[2,1,128,1024]{3,2,1,0:T(8,128)(2,1)S(1)}, bf16[2,1,128,1024]{3,2,1,0:T(8,128)(2,1)S(1)}, u32[]{:S(2)}, u32[]{:S(2)}) collective-permute-start(bf16[2,1,128,1024]{3,2,1,0:T(8,128)(2,1)S(1)} %get-tuple-element.109), channel_id=1, source_target_pairs={{0,4},{1,5},{2,6},{3,7},{4,0},{5,1},{6,2},{7,3},{8,12},{9,13},{10,... | collective-permute-start | bytes 1572872 | tf_op jit(solution)/shard_map/ppermute | solution.py:192
  75.7 8.5 %collective-permute-start.27 = (bf16[1,1,128,1024]{3,2,1,0:T(8,128)(2,1)S(1)}, bf16[1,1,128,1024]{3,2,1,0:T(8,128)(2,1)S(1)}, u32[]{:S(2)}, u32[]{:S(2)}) collective-permute-start(bf16[1,1,128,1024]{3,2,1,0:T(8,128)(2,1)S(1)} %slice.76), channel_id=1, source_target_pairs={{0,1},{1,0},{2,3},{3,2},{4,6},{5,7},{6,4},{7,5},{8,9},{9,8},{10,11... | collective-permute-start | bytes 786440 | tf_op jit(solution)/shard_map/ppermute | solution.py:192
  76.8 9.7 %collective-permute-start.33 = (bf16[2,1,128,1024]{3,2,1,0:T(8,128)(2,1)S(1)}, bf16[2,1,128,1024]{3,2,1,0:T(8,128)(2,1)S(1)}, u32[]{:S(2)}, u32[]{:S(2)}) collective-permute-start(bf16[2,1,128,1024]{3,2,1,0:T(8,128)(2,1)S(1)} %get-tuple-element.114), channel_id=1, source_target_pairs={{0,4},{1,5},{2,6},{3,7},{4,0},{5,1},{6,2},{7,3},{8,12},{9,13},{10,... | collective-permute-start | bytes 1572872 | tf_op jit(solution)/shard_map/ppermute | solution.py:192
  77.2 9.8 %collective-permute-start.35 = (bf16[2,1,128,1024]{3,2,1,0:T(8,128)(2,1)S(1)}, bf16[2,1,128,1024]{3,2,1,0:T(8,128)(2,1)S(1)}, u32[]{:S(2)}, u32[]{:S(2)}) collective-permute-start(bf16[2,1,128,1024]{3,2,1,0:T(8,128)(2,1)S(1)} %add_convert_fusion), channel_id=1, source_target_pairs={{0,2},{1,3},{2,0},{3,1},{4,5},{5,4},{6,7},{7,6},{8,10},{9,11},{10,... | collective-permute-start | bytes 1572872 | tf_op jit(solution)/shard_map/ppermute | solution.py:192
  78.9 22.6 %collective-permute-start.31 = (bf16[128,1024]{1,0:T(8,128)(2,1)S(1)}, bf16[128,1024]{1,0:T(8,128)(2,1)S(1)}, u32[]{:S(2)}, u32[]{:S(2)}) collective-permute-start(bf16[128,1024]{1,0:T(8,128)(2,1)S(1)} %fusion.8), channel_id=1, source_target_pairs={{0,8},{1,9},{2,10},{3,11},{4,12},{5,13},{6,14},{7,15},{8,16},{9,17... | collective-permute-start | bytes 786440 | tf_op jit(solution)/shard_map/ppermute | solution.py:192
  84.1 11.6 %collective-permute-start.29 = (bf16[2,1,128,1024]{3,2,1,0:T(8,128)(2,1)S(1)}, bf16[2,1,128,1024]{3,2,1,0:T(8,128)(2,1)S(1)}, u32[]{:S(2)}, u32[]{:S(2)}) collective-permute-start(bf16[2,1,128,1024]{3,2,1,0:T(8,128)(2,1)S(1)} %add_convert_fusion.1), channel_id=1, source_target_pairs={{0,2},{1,3},{2,0},{3,1},{4,5},{5,4},{6,7},{7,6},{8,10},{9,11},{10,... | collective-permute-start | bytes 1572872 | tf_op jit(solution)/shard_map/ppermute | solution.py:192
  85.1 16.3 %collective-permute-start.32 = (bf16[128,1024]{1,0:T(8,128)(2,1)S(1)}, bf16[128,1024]{1,0:T(8,128)(2,1)S(1)}, u32[]{:S(2)}, u32[]{:S(2)}) collective-permute-start(bf16[128,1024]{1,0:T(8,128)(2,1)S(1)} %fusion.9), channel_id=1, source_target_pairs={{0,16},{1,17},{2,18},{3,19},{4,20},{5,21},{6,22},{7,23},{8,24},{9,... | collective-permute-start | bytes 786440 | tf_op jit(solution)/shard_map/ppermute | solution.py:192
  87.4 9.7 %collective-permute-start.36 = (bf16[1,1,128,1024]{3,2,1,0:T(8,128)(2,1)S(1)}, bf16[1,1,128,1024]{3,2,1,0:T(8,128)(2,1)S(1)}, u32[]{:S(2)}, u32[]{:S(2)}) collective-permute-start(bf16[1,1,128,1024]{3,2,1,0:T(8,128)(2,1)S(1)} %slice.74), channel_id=1, source_target_pairs={{0,1},{1,0},{2,3},{3,2},{4,6},{5,7},{6,4},{7,5},{8,9},{9,8},{10,11... | collective-permute-start | bytes 786440 | tf_op jit(solution)/shard_map/ppermute | solution.py:192
  96.1 6.4 %collective-permute-start.30 = (bf16[1,1,128,1024]{3,2,1,0:T(8,128)(2,1)S(1)}, bf16[1,1,128,1024]{3,2,1,0:T(8,128)(2,1)S(1)}, u32[]{:S(2)}, u32[]{:S(2)}) collective-permute-start(bf16[1,1,128,1024]{3,2,1,0:T(8,128)(2,1)S(1)} %slice.75), channel_id=1, source_target_pairs={{0,1},{1,0},{2,3},{3,2},{4,6},{5,7},{6,4},{7,5},{8,9},{9,8},{10,11... | collective-permute-start | bytes 786440 | tf_op jit(solution)/shard_map/ppermute | solution.py:192
  97.1 10.2 %collective-permute-start.37 = (bf16[128,1024]{1,0:T(8,128)(2,1)S(1)}, bf16[128,1024]{1,0:T(8,128)(2,1)S(1)}, u32[]{:S(2)}, u32[]{:S(2)}) collective-permute-start(bf16[128,1024]{1,0:T(8,128)(2,1)S(1)} %fusion.10), channel_id=1, source_target_pairs={{0,24},{1,25},{2,26},{3,27},{4,28},{5,29},{6,30},{7,31},{8,0},{9,1... | collective-permute-start | bytes 786440 | tf_op jit(solution)/shard_map/ppermute | solution.py:192
  (6 other events, 17.8 us)
